TPU v7x, 256 devices: a whole 4x4x8 slice. The times are simulated.
256 devices in a mesh: comp: 8 (over z_hi, y), brick: 32 (over x, z_lo, core).
Axes of the slice: x: 4, y: 4, z: 8 (z_hi: 2, z_lo: 4; z = z_hi * 4 + z_lo), core: 2. Of those that a mesh axis runs over, the one named last changes fastest.
Arguments:
- initial: float32 [8, 16, 16, 16, 4096], P('comp', None, None, None, 'brick'), may hold values from -6 to 6
- levels: int32 [8, 4], P('comp'), may hold values from 1 to 6
- weights: int32 [8], P('comp'), may hold values from -1 to 1, as said below
- velocity: float32 [4], replicated, may hold values from 0.2 to 2
- diffusivity: float32 [4], replicated, may hold values from 0.01 to 0.1
Outputs:
- combined: float32 [16, 16, 16, 4096], P(None, None, None, 'brick')
Inputs may be any that keep to these rules, and one draw needn't show every extreme that they name: `weights`: each coefficient is -1 or +1, both signs occur.
All inputs are finite; a program needn't handle non-finite values.
Results may differ from a plain program's by a relative error of at most 0.0001.
Values sent between devices are 32-bit elements; how exact they have to be, the bound alone decides.
No kernel may reach another device: no remote copies, remote signals or barrier semaphores. Data moves between devices by JAX's collectives and lax.ppermute only.
A program may use at most 192 MiB of HBM per device.

v0:
```python
import jax
import jax.numpy as jnp
from jax import lax
from jax.sharding import PartitionSpec as P

cfl_limit = 0.9


def extended_2(x, sides, width):
    for axis, dim in sides:
        peers, length = (lax.axis_size(axis), x.shape[dim])
        up = [(i, (i + 1) % peers) for i in range(peers)]
        down = [(j, i) for i, j in up]
        last = lax.slice_in_dim(x, length - width, length, axis=dim)
        leading = lax.slice_in_dim(x, 0, width, axis=dim)
        before = lax.ppermute(last, axis, up)
        after = lax.ppermute(leading, axis, down)
        x = jnp.concatenate([before, x, after], axis=dim)
    return x


def step_factors(level, velocity, diffusivity):
    inverse = jnp.exp2(level.astype(jnp.float32))
    total = jnp.sum(velocity * inverse + 2.0 * diffusivity * inverse * inverse)
    delta = cfl_limit / total
    return (delta * velocity * inverse, delta * diffusivity * inverse * inverse)


def substep_wide(extended, advect, diffuse):
    center = extended[..., 1:-1]
    result = center
    for axis_num in range(3):
        lower = jnp.roll(center, 1, axis=axis_num)
        upper = jnp.roll(center, -1, axis=axis_num)
        result = (
            result
            - advect[axis_num] * (center - lower)
            + diffuse[axis_num] * (upper - 2.0 * center + lower)
        )
    lower = extended[..., :-2]
    upper = extended[..., 2:]
    return result - advect[3] * (center - lower) + diffuse[3] * (upper - 2.0 * center + lower)


def surplus_lines(lines, tail, depth):
    row_count = lines.shape[0]
    line_len = lines.shape[1]
    result = lines
    for level_num in range(depth):
        stride = 1 << level_num
        blocks = lines.reshape(row_count, line_len // (2 * stride), 2 * stride)
        left = blocks[:, :, 0]
        right = jnp.concatenate([left[:, 1:], tail], axis=1)
        middle = blocks[:, :, stride] - 0.5 * (left + right)
        result = (
            result.reshape(row_count, line_len // (2 * stride), 2 * stride)
            .at[:, :, stride]
            .set(middle)
            .reshape(row_count, line_len)
        )
    return result


def local(initial, levels, weights, velocity, diffusivity):
    advect, diffuse = step_factors(levels[0], velocity, diffusivity)
    field = initial[0]
    for turn in range(2):
        extended = extended_2(field, (("brick", 3),), 1)
        field = substep_wide(extended, advect, diffuse)
    depth_rows = field.shape[0] * field.shape[1] * field.shape[2]
    brick_len = field.shape[3]
    rows = field.reshape(depth_rows, brick_len)
    lines = lax.all_to_all(rows, "brick", split_axis=0, concat_axis=1, tiled=True)
    line_len = lines.shape[1]
    lines = surplus_lines(lines, lines[:, 0:1], line_len.bit_length() - 1)
    surplus = lax.all_to_all(lines, "brick", split_axis=1, concat_axis=0, tiled=True)
    term = weights[0].astype(jnp.float32) * surplus.reshape(field.shape)
    return lax.psum(term, "comp")


def solution(mesh):
    return jax.shard_map(
        local,
        mesh=mesh,
        in_specs=(P("comp", None, None, None, "brick"), P("comp", None), P("comp"), P(), P()),
        out_specs=P(None, None, None, "brick"),
        check_vma=False,
    )
```

profile of v0, /device:TPU:4, one launch (start us, length us, event | category | flops | bytes accessed | tf_op | source)
XLA Modules:
  0.0 463.1 jit_solution(5939373133372263598)
XLA Ops:
  6.5 5.0 %fusion.65 = (f32[16,16,16,1]{3,2,1,0:T(8,128)}, f32[16,16,16,1]{3,2,1,0:T(8,128)}) fusion(f32[16,16,16,128]{3,2,1,0:T(8,128)} %bitcast.129), kind=kLoop, calls=%fused_computation.127 | loop fusion | bytes 65536 | tf_op jit(solution)/shard_map/slice | solution.py:14
  11.5 3.3 copy.233
  14.9 3.1 copy.235
  18.0 4.5 collective-permute-start.1
  22.5 2.4 fusion.64
  24.9 2.3 fusion.62
  27.4 2.4 slice_bitcast_fusion.1
  31.9 2.9 copy.234
  34.8 2.9 copy.236
  37.7 14.6 %fusion.10 = f32[16,16,16,128]{3,2,1,0:T(8,128)S(1)} fusion(f32[16,16,16,1]{3,2,1,0:T(8,128)} %copy.236, f32[16,16,16,128]{3,2,1,0:T(8,128)} %bitcast.130, f32[16,16,16,1]{3,2,1,0:T(8,128)} %copy.234, f32[1,16,16,128]{3,2,1,0:T(8,128)S(1)} %get-tuple-element.169, f32[15,16,16,128]{3,2,1,0:T(8,128)} %get-tuple-element.171, ...), kind=kLoop, calls=%fused_computation.13 | loop fusion | flops 19398656 | bytes 16810016 | tf_op jit(solution)/shard_map/add | solution.py:42
  52.3 2.7 fusion.60
  55.0 2.4 fusion.59
  57.4 2.3 fusion.55
  59.7 2.2 fusion.57
  62.2 3.1 copy.237
  65.4 3.1 copy.239
  68.5 4.7 %collective-permute-start.3 = (f32[16,16,16,1]{2,1,3,0:T(8,128)S(1)}, f32[16,16,16,1]{2,1,3,0:T(8,128)S(1)}, u32[]{:S(2)}, u32[]{:S(2)}) collective-permute-start(f32[16,16,16,1]{2,1,3,0:T(8,128)S(1)} %copy.239), channel_id=1, source_target_pairs={{1,0},{2,1},{3,2},{4,3},{5,4},{6,5},{7,6},{8,7},{9,8},{10,9},{11,1... | collective-permute-start | bytes 49160 | tf_op jit(solution)/shard_map/ppermute | solution.py:17
  73.2 2.9 copy.238
  76.1 2.9 copy.240
  79.0 13.5 %fusion.3 = f32[16,16,16,128]{3,2,1,0:T(8,128)} fusion(f32[16,16,16,1]{3,2,1,0:T(8,128)} %copy.240, f32[16,16,16,128]{3,2,1,0:T(8,128)S(1)} %fusion.10, f32[16,16,16,1]{3,2,1,0:T(8,128)} %copy.238, f32[1,16,16,128]{3,2,1,0:T(8,128)S(1)} %get-tuple-element.155, f32[15,16,16,128]{3,2,1,0:T(8,128)} %get-tuple-element.157, ...), kind=kLoop, calls=%fused_computation.4 | loop fusion | flops 19398656 | bytes 16810016 | tf_op jit(solution)/shard_map/add | solution.py:42
  92.5 1.9 copy.241
  94.4 59.3 %all_to_all.32 = f32[32,128,128]{1,2,0:T(8,128)} all-to-all(f32[32,128,128]{1,2,0:T(8,128)S(1)} %copy.241), channel_id=1, replica_groups=mesh['comp'=8,'brick'=32] {'brick'}, dimensions={0} | all-to-all | bytes 4194304 | tf_op jit(solution)/shard_map/all_to_all | solution.py:73
  154.6 2.8 copy.287
  157.4 2.0 slice.609
  159.5 6.5 %copy.246 = f32[128,2047,1]{0,2,1:T(1,128)S(1)} copy(f32[128,2047,1]{0,1,2:T(8,128)S(1)} %slice_bitcast_fusion.2) | data formatting | bytes 2096128 | tf_op jit(solution)/shard_map/concatenate | solution.py:53
  166.0 2.0 slice.613
  169.3 5.3 %slice_subtract_fusion = f32[128,2048,1]{0,2,1:T(1,128)S(1)} fusion(f32[128,2048,2]{0,2,1:T(2,128)} %bitcast.18, f32[128,1,1]{0,2,1:T(1,128)S(1)} %get-tuple-element.151, f32[128,2047,1]{0,2,1:T(1,128)S(1)} %copy.246), kind=kLoop, calls=%fused_computation.57 | loop fusion | flops 1048576 | bytes 4194304 | tf_op jit(solution)/shard_map/sub | solution.py:54
  174.6 3.4 slice_subtract_fusion.1
  178.0 1.7 slice.616
  180.1 2.8 slice_subtract_fusion.2
  184.3 1.7 slice_subtract_fusion.3
  187.2 1.3 slice_subtract_fusion.4
  195.1 26.0 %scatter.40 = f32[128,2048,2]{0,2,1:T(2,128)} dynamic-update-slice(f32[128,2048,2]{0,2,1:T(2,128)} %bitcast.18, f32[128,2048,1]{0,2,1:T(1,128)S(1)} %slice_subtract_fusion, s32[]{:T(128)} %constant.347.clone.1, s32[]{:T(128)} %constant.347.clone.1, s32[]{:T(128)} %constant.348.clone.1) | dynamic-update-slice | bytes 2097156 | tf_op jit(solution)/shard_map/scatter | solution.py:58
  221.1 14.4 %scatter.41 = f32[128,1024,4]{0,2,1:T(4,128)} dynamic-update-slice(f32[128,1024,4]{0,2,1:T(4,128)} %bitcast.24, f32[128,1024,1]{0,2,1:T(1,128)S(1)} %slice_subtract_fusion.1, s32[]{:T(128)} %constant.347.clone.1, s32[]{:T(128)} %constant.347.clone.1, s32[]{:T(128)} %constant.349.clone.1) | dynamic-update-slice | bytes 1048580 | tf_op jit(solution)/shard_map/scatter | solution.py:58
  235.5 8.0 %scatter.44 = f32[128,512,8]{0,2,1:T(8,128)} dynamic-update-slice(f32[128,512,8]{0,2,1:T(8,128)} %bitcast.29, f32[128,512,1]{0,2,1:T(1,128)S(1)} %slice_subtract_fusion.2, s32[]{:T(128)} %constant.347.clone.1, s32[]{:T(128)} %constant.347.clone.1, s32[]{:T(128)} %constant.350.clone.1) | dynamic-update-slice | bytes 524292 | tf_op jit(solution)/shard_map/scatter | solution.py:58
  243.5 4.6 %scatter.45 = f32[128,256,16]{0,2,1:T(8,128)} dynamic-update-slice(f32[128,256,16]{0,2,1:T(8,128)} %bitcast.34, f32[128,256,1]{0,2,1:T(1,128)S(1)} %slice_subtract_fusion.3, s32[]{:T(128)} %constant.347.clone.1, s32[]{:T(128)} %constant.347.clone.1, s32[]{:T(128)} %constant.351.clone.1) | dynamic-update-slice | bytes 262148 | tf_op jit(solution)/shard_map/scatter | solution.py:58
  248.2 2.9 scatter.46
  251.1 1.8 scatter.49
  252.9 1.6 scatter.50
  254.6 1.5 scatter.51
  256.0 1.4 scatter.54
  257.4 1.3 scatter.55
  261.4 6.5 %all-to-all-start.1 = ((f32[128,32,128]{0,2,1:T(8,128)}), f32[128,32,128]{0,2,1:T(8,128)S(1)}, u32[]{:S(2)}, u32[]{:S(2)}) async-start(f32[128,32,128]{0,2,1:T(8,128)} %bitcast.78), calls=%async_computation.1 | async-start | bytes 4194304 | tf_op jit(solution)/shard_map/all_to_all | solution.py:76
  268.6 47.2 %all-to-all-done.1 = f32[128,32,128]{0,2,1:T(8,128)S(1)} async-done(((f32[128,32,128]{0,2,1:T(8,128)}), f32[128,32,128]{0,2,1:T(8,128)S(1)}, u32[]{:S(2)}, u32[]{:S(2)}) %all-to-all-start.1) | async-done | bytes 2097184 | tf_op jit(solution)/shard_map/all_to_all | solution.py:76
  315.8 1.5 multiply_bitcast_fusion
  317.2 2.9 copy.272
  320.1 133.1 %all-reduce.2.cloned.1.call-done = f32[16,16,16,128]{3,2,1,0:T(8,128)} async-done(((f32[16,16,16,128]{3,2,1,0:T(8,128)}), f32[16,16,16,128]{3,2,1,0:T(8,128)}) %all-reduce.2.cloned.1.call-update) | async-done | bytes 2097168 | tf_op jit(solution)/shard_map/psum | solution.py:78
  453.2 3.1 copy.302
  (60 shorter events, 16.3 us)
Async XLA Ops:
  11.5 11.0 %copy-start = (f32[1,16,16,16,128]{4,3,2,1,0:T(8,128)S(1)}, f32[1,16,16,16,128]{4,3,2,1,0:T(8,128)}, u32[]{:S(2)}) copy-start(f32[1,16,16,16,128]{4,3,2,1,0:T(8,128)} %param.29) | copy-start | bytes 6291460
  14.8 17.1 %collective-permute-start = (f32[16,16,16,1]{2,1,3,0:T(8,128)S(1)}, f32[16,16,16,1]{2,1,3,0:T(8,128)S(1)}, u32[]{:S(2)}, u32[]{:S(2)}) collective-permute-start(f32[16,16,16,1]{2,1,3,0:T(8,128)S(1)} %copy.233), channel_id=1, source_target_pairs={{0,1},{1,2},{2,3},{3,4},{4,5},{5,6},{6,7},{7,8},{8,9},{9,10},{10,1... | collective-permute-start | bytes 49160 | tf_op jit(solution)/shard_map/ppermute | solution.py:16
  18.0 16.8 %collective-permute-start.1 = (f32[16,16,16,1]{2,1,3,0:T(8,128)S(1)}, f32[16,16,16,1]{2,1,3,0:T(8,128)S(1)}, u32[]{:S(2)}, u32[]{:S(2)}) collective-permute-start(f32[16,16,16,1]{2,1,3,0:T(8,128)S(1)} %copy.235), channel_id=1, source_target_pairs={{1,0},{2,1},{3,2},{4,3},{5,4},{6,5},{7,6},{8,7},{9,8},{10,9},{11,1... | collective-permute-start | bytes 49160 | tf_op jit(solution)/shard_map/ppermute | solution.py:17
  27.4 2.5 copy-start.1
  27.4 2.5 copy-start.2
  27.4 2.5 copy-start.3
  65.3 7.9 %collective-permute-start.2 = (f32[16,16,16,1]{2,1,3,0:T(8,128)S(1)}, f32[16,16,16,1]{2,1,3,0:T(8,128)S(1)}, u32[]{:S(2)}, u32[]{:S(2)}) collective-permute-start(f32[16,16,16,1]{2,1,3,0:T(8,128)S(1)} %copy.237), channel_id=1, source_target_pairs={{0,1},{1,2},{2,3},{3,4},{4,5},{5,6},{6,7},{7,8},{8,9},{9,10},{10,1... | collective-permute-start | bytes 49160 | tf_op jit(solution)/shard_map/ppermute | solution.py:16
  68.5 7.6 %collective-permute-start.3 = (f32[16,16,16,1]{2,1,3,0:T(8,128)S(1)}, f32[16,16,16,1]{2,1,3,0:T(8,128)S(1)}, u32[]{:S(2)}, u32[]{:S(2)}) collective-permute-start(f32[16,16,16,1]{2,1,3,0:T(8,128)S(1)} %copy.239), channel_id=1, source_target_pairs={{1,0},{2,1},{3,2},{4,3},{5,4},{6,5},{7,6},{8,7},{9,8},{10,9},{11,1... | collective-permute-start | bytes 49160 | tf_op jit(solution)/shard_map/ppermute | solution.py:17
  261.4 54.4 %all-to-all-start.1 = ((f32[128,32,128]{0,2,1:T(8,128)}), f32[128,32,128]{0,2,1:T(8,128)S(1)}, u32[]{:S(2)}, u32[]{:S(2)}) async-start(f32[128,32,128]{0,2,1:T(8,128)} %bitcast.78), calls=%async_computation.1 | async-start | bytes 4194304 | tf_op jit(solution)/shard_map/all_to_all | solution.py:76
  267.9 185.3 %all-reduce.2.cloned.1.call-start = ((), (), s32[]{:S(2)}) async-start(), calls=%async_computation.2 | async-start | bytes 4194304 | tf_op jit(solution)/shard_map/psum | solution.py:78
Sparse Core Ops, SparseCore 0:
  320.2 132.8 all-reduce.1
where the time goes:
time: 470 us; the launch traced here: 463 us
  waiting for transfers between devices  180 us (38%)
  local copies, waits for them, and re-layouts  144 us (31%)
  blocking collectives  59.3 us (13%)
  other arithmetic  48.8 us (10%)
  starting transfers between devices  15.9 us (3%)
  between operations  15.1 us (3%)
    psum x1, waiting for transfers between devices, local(): return lax.psum(term, 'comp')  133 us
    scatter x12, local copies, waits for them, and re-layouts, surplus_lines(): result = result.reshape(row_count, line_len // (2 * stride), 2 * stride)....  66.2 us
    all_to_all x1, blocking collectives, local(): lax.all_to_all(rows, 'brick', split_axis=0, concat_axis=1, tiled=True)  59.3 us
    all_to_all x1, waiting for transfers between devices, local(): lax.all_to_all(lines, 'brick', split_axis=1, concat_axis=0, tiled=True)  47.2 us
    add x2, other arithmetic, substep_wide(): result - advect[3] * (center - lower)  28.1 us
    sub x12, other arithmetic, surplus_lines(): middle = blocks[:, :, stride] - 0.5 * (left + right)  18.7 us
    slice x12, local copies, waits for them, and re-layouts, substep_wide(): lower = jnp.roll(center, 1, axis=axis_num)  14.4 us
    slice x4, local copies, waits for them, and re-layouts, extended_2(): last = lax.slice_in_dim(x, length - width, length, axis=dim)  14.1 us
  transfers between devices with their start and end apart: 6, of which 2 were waited for; matrix products, arithmetic and copies ran while one was open for 4% of the time, Pallas kernels for 0%

commit v1 on v0

v1 whole, which is shorter than its diff:
```python
import functools
import jax
import jax.numpy as jnp
import numpy as np
from jax import lax
from jax.experimental import pallas as pl
from jax.experimental.pallas import tpu as pltpu
from jax.sharding import Mesh, PartitionSpec as P

cfl_limit = 0.9
BRICK = ("x", "zl", "core")
HI = lax.Precision.HIGHEST
VM = pl.BlockSpec(memory_space=pltpu.VMEM)
SM = pl.BlockSpec(memory_space=pltpu.SMEM)
F32 = jnp.float32


def compiler_params():
    return pltpu.CompilerParams(vmem_limit_bytes=40 * 1024 * 1024)


def factors(lev, vel, dif):
    inv = [jnp.left_shift(1, lev[0, d]).astype(F32) for d in range(4)]
    total = sum(vel[d] * inv[d] + 2.0 * dif[d] * inv[d] * inv[d] for d in range(4))
    delta = cfl_limit / jnp.full((1, 128), total, F32)
    adv = [delta * (vel[d] * inv[d]) for d in range(4)]
    dfs = [delta * (dif[d] * inv[d] * inv[d]) for d in range(4)]
    center = 1.0 - sum(adv[d] + 2.0 * dfs[d] for d in range(4))
    return center, [adv[d] + dfs[d] for d in range(4)], dfs


def lane_id(shape):
    return lax.broadcasted_iota(jnp.int32, shape, len(shape) - 1)


def lane_factors(lo, hi):
    lane = lane_id((1, 128))
    return jnp.where(lane == 0, 0.0, lo), jnp.where(lane == 127, 0.0, hi)


def step_row(ref, p, i, fac):
    center, lo, hi, lo3, hi3 = fac
    before, after = lax.rem(p + 15, 16), lax.rem(p + 1, 16)
    u = ref[p, i]
    out = center * u + lo[0] * ref[before, i] + hi[0] * ref[after, i]
    out = out + lo[1] * ref[p, (i + 15) % 16] + hi[1] * ref[p, (i + 1) % 16]
    out = out + lo[2] * pltpu.roll(u, 1, 0) + hi[2] * pltpu.roll(u, 15, 0)
    return out + lo3 * pltpu.roll(u, 1, 1) + hi3 * pltpu.roll(u, 127, 1)


def ends_kernel(x_ref, lo_ref, hi_ref):
    row = lax.broadcasted_iota(jnp.int32, (8, 128), 0)
    lane = lane_id((8, 128))
    want = jnp.where(row < 2, row, row + 124)
    pick = jnp.where((lane == want) & (row < 4), 1.0, 0.0).astype(F32)
    for c in range(32):
        block = x_ref[c // 2, 8 * (c % 2) : 8 * (c % 2) + 8].reshape(128, 128)
        got = lax.dot_general(pick, block, (((1,), (1,)), ((), ())), precision=HI, preferred_element_type=F32)
        at = (slice(c // 2, c // 2 + 1), slice(128 * (c % 2), 128 * (c % 2) + 128))
        lo_ref[0, at[0], at[1]] = got[0:1]
        lo_ref[1, at[0], at[1]] = got[1:2]
        hi_ref[0, at[0], at[1]] = got[2:3]
        hi_ref[1, at[0], at[1]] = got[3:4]


def first_kernel(lev, vel, dif, x_ref, u_ref):
    center, lo, hi = factors(lev, vel, dif)
    fac = (center, lo, hi) + lane_factors(lo[3], hi[3])

    def plane(p, _):
        for i in range(16):
            u_ref[p, i] = step_row(x_ref, p, i, fac)
        return 0

    lax.fori_loop(0, 16, plane, 0)


def layer_step(u, below, above, center, lo, hi):
    def wide(v):
        return jnp.concatenate([v, v], axis=1)

    lane = lane_id((16, 256)) & 15
    out = wide(center) * u + wide(lo[0]) * pltpu.roll(u, 1, 0) + wide(hi[0]) * pltpu.roll(u, 15, 0)
    out = out + wide(lo[1]) * pltpu.roll(u, 16, 1) + wide(hi[1]) * pltpu.roll(u, 240, 1)
    down = jnp.where(lane == 0, pltpu.roll(u, 241, 1), pltpu.roll(u, 1, 1))
    up = jnp.where(lane == 15, pltpu.roll(u, 15, 1), pltpu.roll(u, 255, 1))
    out = out + wide(lo[2]) * down + wide(hi[2]) * up
    return out + wide(lo[3]) * below + wide(hi[3]) * above


def spread(pair, ends):
    return lax.dot_general(pair, ends, (((0,), (0,)), ((), ())), precision=HI, preferred_element_type=F32)


def quarters(y):
    a1 = jnp.where((y == 1) | (y == 2), 1, 0)
    return a1, lax.shift_right_logical(y, 1)


def second_kernel(lev, vel, dif, wgt, pos, u_ref, lo_ref, hi_ref, left_ref, right_ref, *rest):
    outs, (first_ref, full_ref, halo_ref) = rest[:8], rest[8:]
    center, lo, hi = factors(lev, vel, dif)
    fac = (center, lo, hi) + lane_factors(lo[3], hi[3])
    below = layer_step(left_ref[1], left_ref[0], lo_ref[0], center, lo, hi)
    above = layer_step(right_ref[0], hi_ref[1], right_ref[1], center, lo, hi)
    halo_ref[...] = jnp.zeros_like(halo_ref)
    lows, highs = (left_ref[1], below), (right_ref[0], above)
    for s in range(2):
        for c in range(32):
            at = (slice(c // 2, c // 2 + 1), slice(128 * (c % 2), 128 * (c % 2) + 128))
            halo_ref[s, c, 0:1, :] = lows[s][at]
            halo_ref[s, c, 1:2, :] = highs[s][at]
    row = lax.broadcasted_iota(jnp.int32, (8, 128), 0)
    lane = lane_id((8, 128))
    ends = jnp.where((row == 0) & (lane == 0), lo[3], 0.0) + jnp.where((row == 1) & (lane == 127), hi[3], 0.0)

    def mend(c, _):
        p, h = lax.div(c, 2), lax.rem(c, 2)
        at = pl.ds(h * 8, 8)
        full_ref[p, at] = u_ref[p, at] + spread(halo_ref[0, c], ends).reshape(8, 16, 128)
        return 0

    lax.fori_loop(0, 32, mend, 0)
    weight = wgt[0].astype(F32)
    pick = jnp.where((row == 0) & (lane == 0), 1.0, 0.0).astype(F32)
    a1, a2 = quarters(pos[0])

    def plane(p, out_ref, slot):
        got = []
        for h in range(2):
            edge = spread(halo_ref[1, 2 * p + h], ends)
            rows = []
            for i in range(8):
                v = weight * (step_row(full_ref, p, 8 * h + i, fac) + edge[16 * i : 16 * i + 16])
                out_ref[slot, 128 * h + 16 * i : 128 * h + 16 * i + 16, :] = v
                rows.append(v)
            block = jnp.concatenate(rows, axis=0)
            got.append(lax.dot_general(pick, block, (((1,), (1,)), ((), ())), precision=HI, preferred_element_type=F32)[0:1])
        first_ref[pl.ds(p, 1), :] = jnp.concatenate(got, axis=1)

    for n, out_ref in enumerate(outs):
        chunk, which, keep = n // 4, (n // 2) % 2, n % 2
        big, small = (a2, a1) if which else (a1, a2)

        def body(r, _, out_ref=out_ref, chunk=chunk, which=which, keep=keep, big=big, small=small):
            half = big if keep else 1 - big
            bit = jnp.where(r == 1, small, 1 - small)
            plane(8 * chunk + 4 * which + 2 * half + bit, out_ref, r)
            return 0

        lax.fori_loop(0, 2, body, 0)


def surplus_kernel(a_ref, b_ref, mat_ref, o_ref):
    for n in range(a_ref.shape[0]):
        o_ref[n] = jnp.dot(a_ref[n] + b_ref[n], mat_ref[...], precision=HI, preferred_element_type=F32)


def last_kernel(rounds, pos, table, *refs):
    got, rest = refs[:rounds], refs[rounds:]
    pieces, (out_ref, fix_ref) = rest[:-2], rest[-2:]
    b = pos[1]
    near = sum(table[0, b, r] * got[r][...] for r in range(rounds))
    first = sum(table[1, b, r] * got[r][...] for r in range(rounds))
    fix_ref[...] = jnp.zeros_like(fix_ref)
    for c in range(32):
        at = (slice(c // 2, c // 2 + 1), slice(128 * (c % 2), 128 * (c % 2) + 128))
        fix_ref[c, 0:1, :] = near[at]
        fix_ref[c, 1:2, :] = first[at]
    row = lax.broadcasted_iota(jnp.int32, (8, 128), 0)
    lane = lane_id((8, 128))
    gap = 128 - lane
    tail = (lane > 0) & ((gap & (gap - 1)) == 0)
    ends = jnp.where((row == 0) & tail, -0.5, 0.0) + jnp.where((row == 1) & (lane == 0), 1.0, 0.0)
    a1, a2 = quarters(pos[0])
    for chunk in range(2):
        own, one, three, far_a, far_b = pieces[5 * chunk : 5 * chunk + 5]
        for which in range(2):
            far = far_b if which else far_a
            for src, f1, f2 in ((own.at[which], 0, 0), (one.at[which], 1, 0), (three.at[which], 0, 1), (far.at[0], 1, 1)):
                x1, x2 = a1 ^ f1, a2 ^ f2
                q = 2 * x2 + x1 if which else 2 * x1 + x2
                p = 8 * chunk + 4 * which + q
                for h in range(2):
                    part = src[128 * h : 128 * h + 128, :] + spread(fix_ref[2 * p + h], ends)
                    out_ref[p, 8 * h : 8 * h + 8] = part.reshape(8, 16, 128)


def level_rounds(n):
    edges = set()
    for b in range(n):
        edges.add(((b + 1) % n, b))
        if b:
            s = b & -b
            edges.add((b - s, b))
            edges.add(((b + s) % n, b))
    out = {}
    for src, dst in edges:
        out.setdefault(src, []).append(dst)
    rounds = []
    for src in sorted(out, key=lambda k: (-len(out[k]), k)):
        for dst in sorted(out[src]):
            for r in rounds:
                if all(s != src and d != dst for s, d in r):
                    r.append((src, dst))
                    break
            else:
                rounds.append([(src, dst)])
    table = np.zeros((2, n, len(rounds)), np.float32)
    for k, r in enumerate(rounds):
        for src, dst in r:
            if src == (dst + 1) % n:
                table[0, dst, k] = 1.0
            if dst:
                s = dst & -dst
                table[1, dst, k] -= 0.5 * ((src == dst - s) + (src == (dst + s) % n))
    return rounds, table


def surplus_matrix():
    m = np.eye(128, dtype=np.float32)
    for j in range(1, 128):
        s = j & -j
        m[j - s, j] -= 0.5
        if j + s < 128:
            m[j + s, j] -= 0.5
    return m


def local(initial, levels, weights, velocity, diffusivity):
    near = [(i, i ^ 1) for i in range(4)]
    mirror = [(i, 3 - i) for i in range(4)]
    pair = [(0, 1), (1, 0)]
    n = lax.axis_size(BRICK)
    up = [(i, (i + 1) % n) for i in range(n)]
    down = [(i, (i - 1) % n) for i in range(n)]
    x = initial[0]
    pos = jnp.stack([lax.axis_index("y"), lax.axis_index(BRICK)]).astype(jnp.int32)
    layers = jax.ShapeDtypeStruct((2, 16, 256), F32)
    params = compiler_params()

    lo, hi = pl.pallas_call(ends_kernel, out_shape=(layers, layers), in_specs=[VM], out_specs=(VM, VM), compiler_params=params)(x)
    left = lax.ppermute(hi, BRICK, up)
    right = lax.ppermute(lo, BRICK, down)
    u = pl.pallas_call(
        first_kernel,
        out_shape=jax.ShapeDtypeStruct(x.shape, F32),
        in_specs=[SM] * 3 + [VM],
        out_specs=VM,
        compiler_params=params,
        cost_estimate=pl.CostEstimate(flops=10000000, bytes_accessed=4 << 20, transcendentals=0),
    )(levels, velocity, diffusivity, x)
    half = jax.ShapeDtypeStruct((2, 256, 128), F32)
    outs = pl.pallas_call(
        second_kernel,
        out_shape=(half,) * 8 + (jax.ShapeDtypeStruct((16, 256), F32),),
        in_specs=[SM] * 5 + [VM] * 5,
        out_specs=(VM,) * 9,
        scratch_shapes=[pltpu.VMEM((16, 16, 16, 128), F32), pltpu.VMEM((2, 32, 8, 128), F32)],
        compiler_params=params,
    )(levels, velocity, diffusivity, weights, pos, u, lo, hi, left, right)
    first = outs[8]

    steps = []
    for c in range(2):
        send_a, keep_a, send_b, keep_b = outs[4 * c : 4 * c + 4]
        steps.append((keep_a, keep_b, lax.ppermute(send_a, "y", near), lax.ppermute(send_b, "y", mirror)))
    pieces = []
    for keep_a, keep_b, got_a, got_b in steps:
        more_a = lax.ppermute(keep_a[0] + got_a[0], "y", mirror)
        more_b = lax.ppermute(keep_b[0] + got_b[0], "y", near)
        mine = jnp.stack([keep_a[1] + got_a[1] + more_a, keep_b[1] + got_b[1] + more_b])
        other = lax.ppermute(mine, "zh", pair)
        own = pl.pallas_call(
            surplus_kernel, out_shape=half, in_specs=[VM] * 3, out_specs=VM, compiler_params=params
        )(mine, other, jnp.asarray(surplus_matrix()))
        one = lax.ppermute(own, "y", near)
        three = lax.ppermute(own, "y", mirror)
        far_a = lax.ppermute(three[0:1], "y", near)
        far_b = lax.ppermute(one[1:2], "y", mirror)
        pieces += [own, one, three, far_a, far_b]

    first = first + lax.ppermute(first, "y", near)
    first = first + lax.ppermute(first, "y", mirror)
    first = first + lax.ppermute(first, "zh", pair)
    rounds, table = level_rounds(n)
    got = [lax.ppermute(first, BRICK, r) for r in rounds]
    return pl.pallas_call(
        functools.partial(last_kernel, len(rounds)),
        out_shape=jax.ShapeDtypeStruct((16, 16, 16, 128), F32),
        in_specs=[SM] * 2 + [VM] * (len(rounds) + len(pieces)),
        out_specs=VM,
        scratch_shapes=[pltpu.VMEM((32, 8, 128), F32)],
        compiler_params=params,
    )(pos, jnp.asarray(table), *got, *pieces)


def solution(mesh):
    wide = Mesh(mesh.devices.reshape(2, 4, 4, 4, 2), ("zh", "y", "x", "zl", "core"))
    comp = ("zh", "y")
    return jax.shard_map(
        local,
        mesh=wide,
        in_specs=(P(comp, None, None, None, BRICK), P(comp, None), P(comp), P(), P()),
        out_specs=P(None, None, None, BRICK),
        check_vma=False,
    )
```

time: 470 us -> 143 us (0.30)
  the two profiles are of different devices: /device:TPU:4 before, /device:TPU:64 now
where the time goes in v1:
time: 143 us
  waiting for transfers between devices  63 us (44%)
  starting transfers between devices  45.4 us (32%)
  Pallas kernels  31.6 us (22%)
  local copies, waits for them, and re-layouts  1.69 us (1%)
    ppermute x9, waiting for transfers between devices, local(): got = [lax.ppermute(first, BRICK, r) for r in rounds]  28.4 us
    pallas_call x1, Pallas kernels, local(): pl.pallas_call(second_kernel, out_shape=(half,) * 8 + (jax.ShapeDtypeStru...  20.5 us
    ppermute x2, waiting for transfers between devices, local(): other = lax.ppermute(mine, 'zh', pair)  10.9 us
    ppermute x9, starting transfers between devices, local(): got = [lax.ppermute(first, BRICK, r) for r in rounds]  10.3 us
    ppermute x2, starting transfers between devices, local(): other = lax.ppermute(mine, 'zh', pair)  8.53 us
    ppermute x1, waiting for transfers between devices, local(): first = first + lax.ppermute(first, 'y', near)  6.35 us
    ppermute x2, starting transfers between devices, local(): more_a = lax.ppermute(keep_a[0] + got_a[0], 'y', mirror)  6.19 us
    ppermute x2, waiting for transfers between devices, local(): lax.ppermute(send_a, 'y', near)  5.85 us
  transfers between devices with their start and end apart: 32, of which 12 were waited for; matrix products, arithmetic and copies ran while one was open for 0% of the time, Pallas kernels for 2%

profile of v1, /device:TPU:64, one launch (start us, length us, event | category | flops | bytes accessed | tf_op | source)
XLA Modules:
  0.0 143.0 jit_solution(2308932662960693070)
XLA Ops:
  0.0 1.6 %copy-done = f32[1,16,16,16,128]{4,3,2,1,0:T(8,128)S(1)} copy-done((f32[1,16,16,16,128]{4,3,2,1,0:T(8,128)S(1)}, f32[1,16,16,16,128]{4,3,2,1,0:T(8,128)}, u32[]{:S(2)}) %copy-start) | copy-done | bytes 2097176
  1.6 3.3 %shard_map.83 = (f32[2,16,256]{2,1,0:T(8,128)S(1)}, f32[2,16,256]{2,1,0:T(8,128)S(1)}) custom-call(f32[16,16,16,128]{3,2,1,0:T(8,128)S(1)} %bitcast.43), custom_call_target="tpu_custom_call" | custom-call | tf_op jit(solution)/shard_map/pallas_call | solution.py:242
  5.0 0.5 collective-permute-start
  6.3 2.8 %shard_map.82.u_ref = f32[16,16,16,128]{3,2,1,0:T(8,128)S(1)} custom-call(s32[1,4]{1,0:T(1,128)S(1)} %copy-done.4, f32[4]{0:T(128)S(1)} %copy-done.5, f32[4]{0:T(128)S(1)} %copy-done.6, f32[16,16,16,128]{3,2,1,0:T(8,128)S(1)} %bitcast.44), custom_call_target="tpu_custom_call" | custom-call | flops 10000000 | bytes 4194304 | tf_op jit(solution)/shard_map/pallas_call | solution.py:245
  9.1 20.5 %shard_map.84 = (f32[2,256,128]{2,1,0:T(8,128)S(1)}, f32[2,256,128]{2,1,0:T(8,128)S(1)}, f32[2,256,128]{2,1,0:T(8,128)S(1)}, f32[2,256,128]{2,1,0:T(8,128)S(1)},...) custom-call(s32[1,4]{1,0:T(1,128)S(1)} %copy-done.4, ...), custom_call_target="tpu_custom_call" | custom-call | tf_op jit(solution)/shard_map/pallas_call | solution.py:254
  29.6 1.6 %collective-permute-start.14 = (f32[2,256,128]{2,1,0:T(8,128)S(1)}, f32[2,256,128]{2,1,0:T(8,128)S(1)}, u32[]{:S(2)}, u32[]{:S(2)}) collective-permute-start(f32[2,256,128]{2,1,0:T(8,128)S(1)} %get-tuple-element.20), channel_id=1, source_target_pairs={{0,32},{32,0},{64,96},{96,64},{1,33},{33,1},{65,97},{97,65},{2,34}... | collective-permute-start | bytes 786440 | tf_op jit(solution)/shard_map/ppermute | solution.py:267
  31.2 2.2 %collective-permute-start.16 = (f32[2,256,128]{2,1,0:T(8,128)S(1)}, f32[2,256,128]{2,1,0:T(8,128)S(1)}, u32[]{:S(2)}, u32[]{:S(2)}) collective-permute-start(f32[2,256,128]{2,1,0:T(8,128)S(1)} %get-tuple-element.22), channel_id=1, source_target_pairs={{0,96},{32,64},{64,32},{96,0},{1,97},{33,65},{65,33},{97,1},{2,98}... | collective-permute-start | bytes 786440 | tf_op jit(solution)/shard_map/ppermute | solution.py:267
  33.4 0.7 collective-permute-start.23
  34.0 0.6 collective-permute-start.25
  34.7 3.6 %collective-permute-done.14 = f32[2,256,128]{2,1,0:T(8,128)S(1)} collective-permute-done((f32[2,256,128]{2,1,0:T(8,128)S(1)}, f32[2,256,128]{2,1,0:T(8,128)S(1)}, u32[]{:S(2)}, u32[]{:S(2)}) %collective-permute-start.14) | collective-permute-done | bytes 262176 | tf_op jit(solution)/shard_map/ppermute | solution.py:267
  38.3 3.1 %collective-permute-start.15 = (f32[256,128]{1,0:T(8,128)S(1)}, f32[256,128]{1,0:T(8,128)S(1)}, u32[]{:S(2)}, u32[]{:S(2)}) collective-permute-start(f32[256,128]{1,0:T(8,128)S(1)} %fusion.12), channel_id=1, source_target_pairs={{0,96},{32,64},{64,32},{96,0},{1,97},{33,65},{65,33},{97,1},{2,98}... | collective-permute-start | bytes 393224 | tf_op jit(solution)/shard_map/ppermute | solution.py:270
  41.4 0.2 collective-permute-start.17
  41.6 2.3 %collective-permute-done.23 = f32[2,256,128]{2,1,0:T(8,128)S(1)} collective-permute-done((f32[2,256,128]{2,1,0:T(8,128)S(1)}, f32[2,256,128]{2,1,0:T(8,128)S(1)}, u32[]{:S(2)}, u32[]{:S(2)}) %collective-permute-start.23) | collective-permute-done | bytes 262176 | tf_op jit(solution)/shard_map/ppermute | solution.py:267
  43.9 3.1 %collective-permute-start.24 = (f32[256,128]{1,0:T(8,128)S(1)}, f32[256,128]{1,0:T(8,128)S(1)}, u32[]{:S(2)}, u32[]{:S(2)}) collective-permute-start(f32[256,128]{1,0:T(8,128)S(1)} %fusion.4), channel_id=1, source_target_pairs={{0,96},{32,64},{64,32},{96,0},{1,97},{33,65},{65,33},{97,1},{2,98}... | collective-permute-start | bytes 393224 | tf_op jit(solution)/shard_map/ppermute | solution.py:270
  47.0 0.2 collective-permute-start.26
  47.2 2.4 %collective-permute-done.15 = f32[256,128]{1,0:T(8,128)S(1)} collective-permute-done((f32[256,128]{1,0:T(8,128)S(1)}, f32[256,128]{1,0:T(8,128)S(1)}, u32[]{:S(2)}, u32[]{:S(2)}) %collective-permute-start.15) | collective-permute-done | bytes 131104 | tf_op jit(solution)/shard_map/ppermute | solution.py:270
  49.8 6.0 %collective-permute-start.18 = (f32[2,256,128]{2,1,0:T(8,128)S(1)}, f32[2,256,128]{2,1,0:T(8,128)S(1)}, u32[]{:S(2)}, u32[]{:S(2)}) collective-permute-start(f32[2,256,128]{2,1,0:T(8,128)S(1)} %pad_maximum_fusion.a_ref), channel_id=1, source_target_pairs={{0,128},{128,0},{1,129},{129,1},{2,130},{130,2},{3,131},{131,3},{4... | collective-permute-start | bytes 786440 | tf_op jit(solution)/shard_map/ppermute | solution.py:273
  55.9 2.5 %collective-permute-start.27 = (f32[2,256,128]{2,1,0:T(8,128)S(1)}, f32[2,256,128]{2,1,0:T(8,128)S(1)}, u32[]{:S(2)}, u32[]{:S(2)}) collective-permute-start(f32[2,256,128]{2,1,0:T(8,128)S(1)} %pad_maximum_fusion.1.a_ref), channel_id=1, source_target_pairs={{0,128},{128,0},{1,129},{129,1},{2,130},{130,2},{3,131},{131,3},{4... | collective-permute-start | bytes 786440 | tf_op jit(solution)/shard_map/ppermute | solution.py:273
  58.4 7.6 %collective-permute-done.18.b_ref = f32[2,256,128]{2,1,0:T(8,128)S(1)} collective-permute-done((f32[2,256,128]{2,1,0:T(8,128)S(1)}, f32[2,256,128]{2,1,0:T(8,128)S(1)}, u32[]{:S(2)}, u32[]{:S(2)}) %collective-permute-start.18) | collective-permute-done | bytes 262176 | tf_op jit(solution)/shard_map/ppermute | solution.py:273
  66.0 0.4 shard_map.85.refs_9_
  66.4 1.8 %collective-permute-start.20 = (f32[2,256,128]{2,1,0:T(8,128)S(1)}, f32[2,256,128]{2,1,0:T(8,128)S(1)}, u32[]{:S(2)}, u32[]{:S(2)}) collective-permute-start(f32[2,256,128]{2,1,0:T(8,128)S(1)} %shard_map.85.refs_9_), channel_id=1, source_target_pairs={{0,96},{32,64},{64,32},{96,0},{1,97},{33,65},{65,33},{97,1},{2,98}... | collective-permute-start | bytes 786440 | tf_op jit(solution)/shard_map/ppermute | solution.py:278
  68.2 3.3 %collective-permute-done.27.b_ref = f32[2,256,128]{2,1,0:T(8,128)S(1)} collective-permute-done((f32[2,256,128]{2,1,0:T(8,128)S(1)}, f32[2,256,128]{2,1,0:T(8,128)S(1)}, u32[]{:S(2)}, u32[]{:S(2)}) %collective-permute-start.27) | collective-permute-done | bytes 262176 | tf_op jit(solution)/shard_map/ppermute | solution.py:273
  71.5 0.4 shard_map.86.refs_14_
  71.9 1.9 %collective-permute-start.29 = (f32[2,256,128]{2,1,0:T(8,128)S(1)}, f32[2,256,128]{2,1,0:T(8,128)S(1)}, u32[]{:S(2)}, u32[]{:S(2)}) collective-permute-start(f32[2,256,128]{2,1,0:T(8,128)S(1)} %shard_map.86.refs_14_), channel_id=1, source_target_pairs={{0,96},{32,64},{64,32},{96,0},{1,97},{33,65},{65,33},{97,1},{2,98}... | collective-permute-start | bytes 786440 | tf_op jit(solution)/shard_map/ppermute | solution.py:278
  73.8 0.9 collective-permute-start.28
  74.7 1.1 collective-permute-start.2
  75.8 6.4 %collective-permute-done.2 = f32[16,256]{1,0:T(8,128)S(1)} collective-permute-done((f32[16,256]{1,0:T(8,128)S(1)}, f32[16,256]{1,0:T(8,128)S(1)}, u32[]{:S(2)}, u32[]{:S(2)}) %collective-permute-start.2) | collective-permute-done | bytes 16416 | tf_op jit(solution)/shard_map/ppermute | solution.py:283
  82.2 1.2 collective-permute-start.3
  83.4 3.7 %collective-permute-done.3 = f32[16,256]{1,0:T(8,128)S(1)} collective-permute-done((f32[16,256]{1,0:T(8,128)S(1)}, f32[16,256]{1,0:T(8,128)S(1)}, u32[]{:S(2)}, u32[]{:S(2)}) %collective-permute-start.3) | collective-permute-done | bytes 16416 | tf_op jit(solution)/shard_map/ppermute | solution.py:284
  87.1 2.3 %collective-permute-start.4 = (f32[16,256]{1,0:T(8,128)S(1)}, f32[16,256]{1,0:T(8,128)S(1)}, u32[]{:S(2)}, u32[]{:S(2)}) collective-permute-start(f32[16,256]{1,0:T(8,128)S(1)} %add.78), channel_id=1, source_target_pairs={{0,128},{128,0},{1,129},{129,1},{2,130},{130,2},{3,131},{131,3},{4... | collective-permute-start | bytes 49160 | tf_op jit(solution)/shard_map/ppermute | solution.py:285
  89.5 5.3 %collective-permute-done.4 = f32[16,256]{1,0:T(8,128)S(1)} collective-permute-done((f32[16,256]{1,0:T(8,128)S(1)}, f32[16,256]{1,0:T(8,128)S(1)}, u32[]{:S(2)}, u32[]{:S(2)}) %collective-permute-start.4) | collective-permute-done | bytes 16416 | tf_op jit(solution)/shard_map/ppermute | solution.py:285
  94.8 0.7 collective-permute-start.13
  95.5 0.7 collective-permute-start.12
  96.3 1.3 collective-permute-start.22
  97.6 1.5 %collective-permute-start.30 = (f32[1,256,128]{2,1,0:T(8,128)S(1)}, f32[1,256,128]{2,1,0:T(8,128)S(1)}, u32[]{:S(2)}, u32[]{:S(2)}) collective-permute-start(f32[1,256,128]{2,1,0:T(8,128)S(1)} %slice.90), channel_id=1, source_target_pairs={{0,32},{32,0},{64,96},{96,64},{1,33},{33,1},{65,97},{97,65},{2,34}... | collective-permute-start | bytes 393224 | tf_op jit(solution)/shard_map/ppermute | solution.py:279
  99.1 2.1 %collective-permute-start.31 = (f32[1,256,128]{2,1,0:T(8,128)S(1)}, f32[1,256,128]{2,1,0:T(8,128)S(1)}, u32[]{:S(2)}, u32[]{:S(2)}) collective-permute-start(f32[1,256,128]{2,1,0:T(8,128)S(1)} %slice.91), channel_id=1, source_target_pairs={{0,96},{32,64},{64,32},{96,0},{1,97},{33,65},{65,33},{97,1},{2,98}... | collective-permute-start | bytes 393224 | tf_op jit(solution)/shard_map/ppermute | solution.py:280
  101.2 0.7 collective-permute-start.11
  101.9 0.7 collective-permute-start.10
  102.6 0.7 collective-permute-start.9
  103.3 1.3 collective-permute-start.8
  104.6 1.4 collective-permute-done.8.refs_3_
  106.0 1.9 %collective-permute-start.7 = (f32[16,256]{1,0:T(8,128)S(1)}, f32[16,256]{1,0:T(8,128)S(1)}, u32[]{:S(2)}, u32[]{:S(2)}) collective-permute-start(f32[16,256]{1,0:T(8,128)S(1)} %add.79), channel_id=1, source_target_pairs={{0,4},{16,14},{8,7},{24,23},{4,5},{12,13},{20,21},{28,29},{10,11},... | collective-permute-start | bytes 49160 | tf_op jit(solution)/shard_map/ppermute | solution.py:287
  107.9 20.0 %collective-permute-done.7.refs_2_ = f32[16,256]{1,0:T(8,128)S(1)} collective-permute-done((f32[16,256]{1,0:T(8,128)S(1)}, f32[16,256]{1,0:T(8,128)S(1)}, u32[]{:S(2)}, u32[]{:S(2)}) %collective-permute-start.7) | collective-permute-done | bytes 16416 | tf_op jit(solution)/shard_map/ppermute | solution.py:287
  127.9 1.9 %collective-permute-start.6 = (f32[16,256]{1,0:T(8,128)S(1)}, f32[16,256]{1,0:T(8,128)S(1)}, u32[]{:S(2)}, u32[]{:S(2)}) collective-permute-start(f32[16,256]{1,0:T(8,128)S(1)} %add.79), channel_id=1, source_target_pairs={{0,2},{16,12},{8,6},{24,22},{4,3},{12,11},{20,19},{28,27},{2,1},{6... | collective-permute-start | bytes 49160 | tf_op jit(solution)/shard_map/ppermute | solution.py:287
  129.8 1.4 collective-permute-done.6.refs_1_
  131.2 1.9 %collective-permute-start.5 = (f32[16,256]{1,0:T(8,128)S(1)}, f32[16,256]{1,0:T(8,128)S(1)}, u32[]{:S(2)}, u32[]{:S(2)}) collective-permute-start(f32[16,256]{1,0:T(8,128)S(1)} %add.79), channel_id=1, source_target_pairs={{0,1},{16,8},{8,4},{24,20},{4,2},{12,10},{20,18},{28,26},{2,3},{6,... | collective-permute-start | bytes 49160 | tf_op jit(solution)/shard_map/ppermute | solution.py:287
  133.2 5.5 %collective-permute-done.5.refs_0_ = f32[16,256]{1,0:T(8,128)S(1)} collective-permute-done((f32[16,256]{1,0:T(8,128)S(1)}, f32[16,256]{1,0:T(8,128)S(1)}, u32[]{:S(2)}, u32[]{:S(2)}) %collective-permute-start.5) | collective-permute-done | bytes 16416 | tf_op jit(solution)/shard_map/ppermute | solution.py:287
  138.7 4.3 %shard_map.87 = f32[16,16,16,128]{3,2,1,0:T(8,128)} custom-call(s32[2]{0:T(128)S(1)} %pad_add_fusion.pos, f32[2,32,9]{2,1,0:T(8,128)S(1)} %copy-done.3, f32[16,256]{1,0:T(8,128)S(1)} %collective-permute-done.5.refs_0_, f32[16,256]{1,0:T(8,128)S(1)} %collective-permute-done.6.refs_1_, f32[16,256]{1,0:T(8,128)S(1)} %collective-permute-done.7.refs_2_, ...), custom_call_target="tpu_custom_call" | custom-call | tf_op jit(solution)/shard_map/pallas_call | solution.py:288
  (54 shorter events, 0.6 us)
Async XLA Ops:
  0.0 6.2 %copy-start.6 = (f32[4]{0:T(128)S(1)}, f32[4]{0:T(128)}, u32[]{:S(2)}) copy-start(f32[4]{0:T(128)} %dif.3) | copy-start | bytes 52
  0.0 6.2 %copy-start.5 = (f32[4]{0:T(128)S(1)}, f32[4]{0:T(128)}, u32[]{:S(2)}) copy-start(f32[4]{0:T(128)} %vel.3) | copy-start | bytes 52
  0.0 6.3 %copy-start.4 = (s32[1,4]{1,0:T(1,128)S(1)}, s32[1,4]{1,0:T(1,128)}, u32[]{:S(2)}) copy-start(s32[1,4]{1,0:T(1,128)} %lev.3) | copy-start | bytes 52
  0.0 1.6 %copy-start = (f32[1,16,16,16,128]{4,3,2,1,0:T(8,128)S(1)}, f32[1,16,16,16,128]{4,3,2,1,0:T(8,128)}, u32[]{:S(2)}) copy-start(f32[1,16,16,16,128]{4,3,2,1,0:T(8,128)} %param.8) | copy-start | bytes 6291460
  1.6 4.6 %copy-start.1 = (f32[1,16,16,16,128]{4,3,2,1,0:T(8,128)S(1)}, f32[1,16,16,16,128]{4,3,2,1,0:T(8,128)}, u32[]{:S(2)}) copy-start(f32[1,16,16,16,128]{4,3,2,1,0:T(8,128)} %param.8) | copy-start | bytes 6291460
  5.0 4.1 %collective-permute-start.1 = (f32[2,16,256]{2,1,0:T(8,128)S(1)}, f32[2,16,256]{2,1,0:T(8,128)S(1)}, u32[]{:S(2)}, u32[]{:S(2)}) collective-permute-start(f32[2,16,256]{2,1,0:T(8,128)S(1)} %get-tuple-element.16.lo_ref), channel_id=1, source_target_pairs={{0,31},{1,0},{2,1},{3,2},{4,3},{5,4},{6,5},{7,6},{8,7},{9,8},{10,9... | collective-permute-start | bytes 98312 | tf_op jit(solution)/shard_map/ppermute | solution.py:244
  5.0 4.1 %collective-permute-start = (f32[2,16,256]{2,1,0:T(8,128)S(1)}, f32[2,16,256]{2,1,0:T(8,128)S(1)}, u32[]{:S(2)}, u32[]{:S(2)}) collective-permute-start(f32[2,16,256]{2,1,0:T(8,128)S(1)} %get-tuple-element.17.hi_ref), channel_id=1, source_target_pairs={{0,1},{1,2},{2,3},{3,4},{4,5},{5,6},{6,7},{7,8},{8,9},{9,10},{10,1... | collective-permute-start | bytes 98312 | tf_op jit(solution)/shard_map/ppermute | solution.py:243
  29.6 8.7 %collective-permute-start.14 = (f32[2,256,128]{2,1,0:T(8,128)S(1)}, f32[2,256,128]{2,1,0:T(8,128)S(1)}, u32[]{:S(2)}, u32[]{:S(2)}) collective-permute-start(f32[2,256,128]{2,1,0:T(8,128)S(1)} %get-tuple-element.20), channel_id=1, source_target_pairs={{0,32},{32,0},{64,96},{96,64},{1,33},{33,1},{65,97},{97,65},{2,34}... | collective-permute-start | bytes 786440 | tf_op jit(solution)/shard_map/ppermute | solution.py:267
  31.2 10.2 %collective-permute-start.16 = (f32[2,256,128]{2,1,0:T(8,128)S(1)}, f32[2,256,128]{2,1,0:T(8,128)S(1)}, u32[]{:S(2)}, u32[]{:S(2)}) collective-permute-start(f32[2,256,128]{2,1,0:T(8,128)S(1)} %get-tuple-element.22), channel_id=1, source_target_pairs={{0,96},{32,64},{64,32},{96,0},{1,97},{33,65},{65,33},{97,1},{2,98}... | collective-permute-start | bytes 786440 | tf_op jit(solution)/shard_map/ppermute | solution.py:267
  33.4 10.5 %collective-permute-start.23 = (f32[2,256,128]{2,1,0:T(8,128)S(1)}, f32[2,256,128]{2,1,0:T(8,128)S(1)}, u32[]{:S(2)}, u32[]{:S(2)}) collective-permute-start(f32[2,256,128]{2,1,0:T(8,128)S(1)} %get-tuple-element.24), channel_id=1, source_target_pairs={{0,32},{32,0},{64,96},{96,64},{1,33},{33,1},{65,97},{97,65},{2,34}... | collective-permute-start | bytes 786440 | tf_op jit(solution)/shard_map/ppermute | solution.py:267
  34.0 12.9 %collective-permute-start.25 = (f32[2,256,128]{2,1,0:T(8,128)S(1)}, f32[2,256,128]{2,1,0:T(8,128)S(1)}, u32[]{:S(2)}, u32[]{:S(2)}) collective-permute-start(f32[2,256,128]{2,1,0:T(8,128)S(1)} %get-tuple-element.26), channel_id=1, source_target_pairs={{0,96},{32,64},{64,32},{96,0},{1,97},{33,65},{65,33},{97,1},{2,98}... | collective-permute-start | bytes 786440 | tf_op jit(solution)/shard_map/ppermute | solution.py:267
  38.3 11.4 %collective-permute-start.15 = (f32[256,128]{1,0:T(8,128)S(1)}, f32[256,128]{1,0:T(8,128)S(1)}, u32[]{:S(2)}, u32[]{:S(2)}) collective-permute-start(f32[256,128]{1,0:T(8,128)S(1)} %fusion.12), channel_id=1, source_target_pairs={{0,96},{32,64},{64,32},{96,0},{1,97},{33,65},{65,33},{97,1},{2,98}... | collective-permute-start | bytes 393224 | tf_op jit(solution)/shard_map/ppermute | solution.py:270
  41.4 24.7 %copy-start.2 = (f32[128,128]{1,0:T(8,128)S(1)}, f32[128,128]{1,0:T(8,128)}, u32[]{:S(2)}) copy-start(f32[128,128]{1,0:T(8,128)} %constant.23.clone.mat_ref) | copy-start | bytes 196612
  41.4 8.3 %collective-permute-start.17 = (f32[256,128]{1,0:T(8,128)S(1)}, f32[256,128]{1,0:T(8,128)S(1)}, u32[]{:S(2)}, u32[]{:S(2)}) collective-permute-start(f32[256,128]{1,0:T(8,128)S(1)} %fusion.8), channel_id=1, source_target_pairs={{0,32},{32,0},{64,96},{96,64},{1,33},{33,1},{65,97},{97,65},{2,34}... | collective-permute-start | bytes 393224 | tf_op jit(solution)/shard_map/ppermute | solution.py:271
  43.9 11.9 %collective-permute-start.24 = (f32[256,128]{1,0:T(8,128)S(1)}, f32[256,128]{1,0:T(8,128)S(1)}, u32[]{:S(2)}, u32[]{:S(2)}) collective-permute-start(f32[256,128]{1,0:T(8,128)S(1)} %fusion.4), channel_id=1, source_target_pairs={{0,96},{32,64},{64,32},{96,0},{1,97},{33,65},{65,33},{97,1},{2,98}... | collective-permute-start | bytes 393224 | tf_op jit(solution)/shard_map/ppermute | solution.py:270
  47.0 8.8 %collective-permute-start.26 = (f32[256,128]{1,0:T(8,128)S(1)}, f32[256,128]{1,0:T(8,128)S(1)}, u32[]{:S(2)}, u32[]{:S(2)}) collective-permute-start(f32[256,128]{1,0:T(8,128)S(1)} %fusion), channel_id=1, source_target_pairs={{0,32},{32,0},{64,96},{96,64},{1,33},{33,1},{65,97},{97,65},{2,34}... | collective-permute-start | bytes 393224 | tf_op jit(solution)/shard_map/ppermute | solution.py:271
  49.8 16.2 %collective-permute-start.18 = (f32[2,256,128]{2,1,0:T(8,128)S(1)}, f32[2,256,128]{2,1,0:T(8,128)S(1)}, u32[]{:S(2)}, u32[]{:S(2)}) collective-permute-start(f32[2,256,128]{2,1,0:T(8,128)S(1)} %pad_maximum_fusion.a_ref), channel_id=1, source_target_pairs={{0,128},{128,0},{1,129},{129,1},{2,130},{130,2},{3,131},{131,3},{4... | collective-permute-start | bytes 786440 | tf_op jit(solution)/shard_map/ppermute | solution.py:273
  55.8 82.9 %copy-start.3 = (f32[2,32,9]{2,1,0:T(8,128)S(1)}, f32[2,32,9]{2,1,0:T(8,128)}, u32[]{:S(2)}) copy-start(f32[2,32,9]{2,1,0:T(8,128)} %constant.24.clone.table) | copy-start | bytes 6916
  55.9 15.6 %collective-permute-start.27 = (f32[2,256,128]{2,1,0:T(8,128)S(1)}, f32[2,256,128]{2,1,0:T(8,128)S(1)}, u32[]{:S(2)}, u32[]{:S(2)}) collective-permute-start(f32[2,256,128]{2,1,0:T(8,128)S(1)} %pad_maximum_fusion.1.a_ref), channel_id=1, source_target_pairs={{0,128},{128,0},{1,129},{129,1},{2,130},{130,2},{3,131},{131,3},{4... | collective-permute-start | bytes 786440 | tf_op jit(solution)/shard_map/ppermute | solution.py:273
  66.4 29.1 %collective-permute-start.20 = (f32[2,256,128]{2,1,0:T(8,128)S(1)}, f32[2,256,128]{2,1,0:T(8,128)S(1)}, u32[]{:S(2)}, u32[]{:S(2)}) collective-permute-start(f32[2,256,128]{2,1,0:T(8,128)S(1)} %shard_map.85.refs_9_), channel_id=1, source_target_pairs={{0,96},{32,64},{64,32},{96,0},{1,97},{33,65},{65,33},{97,1},{2,98}... | collective-permute-start | bytes 786440 | tf_op jit(solution)/shard_map/ppermute | solution.py:278
  68.2 28.0 %collective-permute-start.19 = (f32[2,256,128]{2,1,0:T(8,128)S(1)}, f32[2,256,128]{2,1,0:T(8,128)S(1)}, u32[]{:S(2)}, u32[]{:S(2)}) collective-permute-start(f32[2,256,128]{2,1,0:T(8,128)S(1)} %shard_map.85.refs_9_), channel_id=1, source_target_pairs={{0,32},{32,0},{64,96},{96,64},{1,33},{33,1},{65,97},{97,65},{2,34}... | collective-permute-start | bytes 786440 | tf_op jit(solution)/shard_map/ppermute | solution.py:277
  71.9 24.4 %collective-permute-start.29 = (f32[2,256,128]{2,1,0:T(8,128)S(1)}, f32[2,256,128]{2,1,0:T(8,128)S(1)}, u32[]{:S(2)}, u32[]{:S(2)}) collective-permute-start(f32[2,256,128]{2,1,0:T(8,128)S(1)} %shard_map.86.refs_14_), channel_id=1, source_target_pairs={{0,96},{32,64},{64,32},{96,0},{1,97},{33,65},{65,33},{97,1},{2,98}... | collective-permute-start | bytes 786440 | tf_op jit(solution)/shard_map/ppermute | solution.py:278
  73.8 23.8 %collective-permute-start.28 = (f32[2,256,128]{2,1,0:T(8,128)S(1)}, f32[2,256,128]{2,1,0:T(8,128)S(1)}, u32[]{:S(2)}, u32[]{:S(2)}) collective-permute-start(f32[2,256,128]{2,1,0:T(8,128)S(1)} %shard_map.86.refs_14_), channel_id=1, source_target_pairs={{0,32},{32,0},{64,96},{96,64},{1,33},{33,1},{65,97},{97,65},{2,34}... | collective-permute-start | bytes 786440 | tf_op jit(solution)/shard_map/ppermute | solution.py:277
  74.7 7.5 %collective-permute-start.2 = (f32[16,256]{1,0:T(8,128)S(1)}, f32[16,256]{1,0:T(8,128)S(1)}, u32[]{:S(2)}, u32[]{:S(2)}) collective-permute-start(f32[16,256]{1,0:T(8,128)S(1)} %get-tuple-element.18), channel_id=1, source_target_pairs={{0,32},{32,0},{64,96},{96,64},{1,33},{33,1},{65,97},{97,65},{2,34}... | collective-permute-start | bytes 49160 | tf_op jit(solution)/shard_map/ppermute | solution.py:283
  82.2 4.9 %collective-permute-start.3 = (f32[16,256]{1,0:T(8,128)S(1)}, f32[16,256]{1,0:T(8,128)S(1)}, u32[]{:S(2)}, u32[]{:S(2)}) collective-permute-start(f32[16,256]{1,0:T(8,128)S(1)} %add.77), channel_id=1, source_target_pairs={{0,96},{32,64},{64,32},{96,0},{1,97},{33,65},{65,33},{97,1},{2,98}... | collective-permute-start | bytes 49160 | tf_op jit(solution)/shard_map/ppermute | solution.py:284
  87.1 7.6 %collective-permute-start.4 = (f32[16,256]{1,0:T(8,128)S(1)}, f32[16,256]{1,0:T(8,128)S(1)}, u32[]{:S(2)}, u32[]{:S(2)}) collective-permute-start(f32[16,256]{1,0:T(8,128)S(1)} %add.78), channel_id=1, source_target_pairs={{0,128},{128,0},{1,129},{129,1},{2,130},{130,2},{3,131},{131,3},{4... | collective-permute-start | bytes 49160 | tf_op jit(solution)/shard_map/ppermute | solution.py:285
  94.8 4.3 %collective-permute-start.13 = (f32[16,256]{1,0:T(8,128)S(1)}, f32[16,256]{1,0:T(8,128)S(1)}, u32[]{:S(2)}, u32[]{:S(2)}) collective-permute-start(f32[16,256]{1,0:T(8,128)S(1)} %add.79), channel_id=1, source_target_pairs={{0,31},{32,63},{64,95},{96,127},{128,159},{160,191},{192,223},{224... | collective-permute-start | bytes 49160 | tf_op jit(solution)/shard_map/ppermute | solution.py:287
  95.5 5.8 %collective-permute-start.12 = (f32[16,256]{1,0:T(8,128)S(1)}, f32[16,256]{1,0:T(8,128)S(1)}, u32[]{:S(2)}, u32[]{:S(2)}) collective-permute-start(f32[16,256]{1,0:T(8,128)S(1)} %add.79), channel_id=1, source_target_pairs={{0,30},{16,24},{32,62},{48,56},{64,94},{80,88},{96,126},{112,120},... | collective-permute-start | bytes 49160 | tf_op jit(solution)/shard_map/ppermute | solution.py:287
  96.2 42.5 %collective-permute-start.21 = (f32[1,256,128]{2,1,0:T(8,128)S(1)}, f32[1,256,128]{2,1,0:T(8,128)S(1)}, u32[]{:S(2)}, u32[]{:S(2)}) collective-permute-start(f32[1,256,128]{2,1,0:T(8,128)S(1)} %slice.84), channel_id=1, source_target_pairs={{0,32},{32,0},{64,96},{96,64},{1,33},{33,1},{65,97},{97,65},{2,34}... | collective-permute-start | bytes 393224 | tf_op jit(solution)/shard_map/ppermute | solution.py:279
  96.3 42.4 %collective-permute-start.22 = (f32[1,256,128]{2,1,0:T(8,128)S(1)}, f32[1,256,128]{2,1,0:T(8,128)S(1)}, u32[]{:S(2)}, u32[]{:S(2)}) collective-permute-start(f32[1,256,128]{2,1,0:T(8,128)S(1)} %slice.85), channel_id=1, source_target_pairs={{0,96},{32,64},{64,32},{96,0},{1,97},{33,65},{65,33},{97,1},{2,98}... | collective-permute-start | bytes 393224 | tf_op jit(solution)/shard_map/ppermute | solution.py:280
  97.6 41.0 %collective-permute-start.30 = (f32[1,256,128]{2,1,0:T(8,128)S(1)}, f32[1,256,128]{2,1,0:T(8,128)S(1)}, u32[]{:S(2)}, u32[]{:S(2)}) collective-permute-start(f32[1,256,128]{2,1,0:T(8,128)S(1)} %slice.90), channel_id=1, source_target_pairs={{0,32},{32,0},{64,96},{96,64},{1,33},{33,1},{65,97},{97,65},{2,34}... | collective-permute-start | bytes 393224 | tf_op jit(solution)/shard_map/ppermute | solution.py:279
  99.1 39.5 %collective-permute-start.31 = (f32[1,256,128]{2,1,0:T(8,128)S(1)}, f32[1,256,128]{2,1,0:T(8,128)S(1)}, u32[]{:S(2)}, u32[]{:S(2)}) collective-permute-start(f32[1,256,128]{2,1,0:T(8,128)S(1)} %slice.91), channel_id=1, source_target_pairs={{0,96},{32,64},{64,32},{96,0},{1,97},{33,65},{65,33},{97,1},{2,98}... | collective-permute-start | bytes 393224 | tf_op jit(solution)/shard_map/ppermute | solution.py:280
  101.2 0.7 collective-permute-start.11
  101.9 0.7 collective-permute-start.10
  102.6 0.7 collective-permute-start.9
  103.3 2.7 %collective-permute-start.8 = (f32[16,256]{1,0:T(8,128)S(1)}, f32[16,256]{1,0:T(8,128)S(1)}, u32[]{:S(2)}, u32[]{:S(2)}) collective-permute-start(f32[16,256]{1,0:T(8,128)S(1)} %add.79), channel_id=1, source_target_pairs={{0,8},{16,15},{8,9},{24,25},{4,6},{12,14},{20,22},{28,30},{32,40},... | collective-permute-start | bytes 49160 | tf_op jit(solution)/shard_map/ppermute | solution.py:287
  106.0 21.9 %collective-permute-start.7 = (f32[16,256]{1,0:T(8,128)S(1)}, f32[16,256]{1,0:T(8,128)S(1)}, u32[]{:S(2)}, u32[]{:S(2)}) collective-permute-start(f32[16,256]{1,0:T(8,128)S(1)} %add.79), channel_id=1, source_target_pairs={{0,4},{16,14},{8,7},{24,23},{4,5},{12,13},{20,21},{28,29},{10,11},... | collective-permute-start | bytes 49160 | tf_op jit(solution)/shard_map/ppermute | solution.py:287
  127.9 3.3 %collective-permute-start.6 = (f32[16,256]{1,0:T(8,128)S(1)}, f32[16,256]{1,0:T(8,128)S(1)}, u32[]{:S(2)}, u32[]{:S(2)}) collective-permute-start(f32[16,256]{1,0:T(8,128)S(1)} %add.79), channel_id=1, source_target_pairs={{0,2},{16,12},{8,6},{24,22},{4,3},{12,11},{20,19},{28,27},{2,1},{6... | collective-permute-start | bytes 49160 | tf_op jit(solution)/shard_map/ppermute | solution.py:287
  131.2 7.4 %collective-permute-start.5 = (f32[16,256]{1,0:T(8,128)S(1)}, f32[16,256]{1,0:T(8,128)S(1)}, u32[]{:S(2)}, u32[]{:S(2)}) collective-permute-start(f32[16,256]{1,0:T(8,128)S(1)} %add.79), channel_id=1, source_target_pairs={{0,1},{16,8},{8,4},{24,20},{4,2},{12,10},{20,18},{28,26},{2,3},{6,... | collective-permute-start | bytes 49160 | tf_op jit(solution)/shard_map/ppermute | solution.py:287

commit v2 on v0

v2 whole, which is shorter than its diff:
```python
import functools
import jax
import jax.numpy as jnp
import numpy as np
from jax import lax
from jax.experimental import pallas as pl
from jax.experimental.pallas import tpu as pltpu
from jax.sharding import Mesh, PartitionSpec as P

cfl_limit = 0.9
BRICK = ("x", "zl", "core")
VM = pl.BlockSpec(memory_space=pltpu.VMEM)
SM = pl.BlockSpec(memory_space=pltpu.SMEM)
F32 = jnp.float32


def grant(mib):
    return pltpu.CompilerParams(vmem_limit_bytes=mib * 1024 * 1024)


def factors(lev, vel, dif):
    inv = [jnp.left_shift(1, lev[0, d]).astype(F32) for d in range(4)]
    total = sum(vel[d] * inv[d] + 2.0 * dif[d] * inv[d] * inv[d] for d in range(4))
    delta = cfl_limit / jnp.full((1, 128), total, F32)
    adv = [delta * (vel[d] * inv[d]) for d in range(4)]
    dfs = [delta * (dif[d] * inv[d] * inv[d]) for d in range(4)]
    center = 1.0 - sum(adv[d] + 2.0 * dfs[d] for d in range(4))
    return center, [adv[d] + dfs[d] for d in range(4)], dfs


def lane_id(shape):
    return lax.broadcasted_iota(jnp.int32, shape, len(shape) - 1)


def step_row(ref, p, i, fac):
    center, lo, hi = fac
    before, after = lax.rem(p + 15, 16), lax.rem(p + 1, 16)
    u = ref[p, i]
    out = center * u + lo[0] * ref[before, i] + hi[0] * ref[after, i]
    out = out + lo[1] * ref[p, (i + 15) % 16] + hi[1] * ref[p, (i + 1) % 16]
    out = out + lo[2] * pltpu.roll(u, 1, 0) + hi[2] * pltpu.roll(u, 15, 0)
    return out + lo[3] * pltpu.roll(u, 1, 1) + hi[3] * pltpu.roll(u, 127, 1)


def take_slot(packed_ref, slot, out_ref, at):
    for b in range(2):
        for h in range(2):
            out_ref[at, 8 * b : 8 * b + 8, 128 * h : 128 * h + 128] = packed_ref[b, pl.ds(8 * h + slot, 8, stride=16), :]


def put_slot(packed_ref, slot, value):
    for b in range(2):
        for h in range(2):
            packed_ref[b, pl.ds(8 * h + slot, 8, stride=16), :] = value[8 * b : 8 * b + 8, 128 * h : 128 * h + 128]


def ends_kernel(x_ref, full_ref, lo_ref, hi_ref, mid_ref, packed_ref, sems):
    lane = lane_id((128, 128))
    copies = [pltpu.make_async_copy(x_ref.at[pl.ds(4 * k, 4)], full_ref.at[pl.ds(4 * k, 4)], sems.at[k]) for k in range(4)]
    for copy in copies:
        copy.start()
    for b in range(2):
        acc = jnp.zeros((128, 128), F32)
        for c in range(16):
            if c % 8 == 0:
                copies[2 * b + c // 8].wait()
            block = full_ref[8 * b + c // 2, 8 * (c % 2) : 8 * (c % 2) + 8].reshape(128, 128)
            acc = jnp.where(lax.shift_right_logical(lane, 3) == c, pltpu.roll(block, (4 + 8 * c) % 128, 1), acc)
        packed_ref[b] = acc.T
    for slot, (out_ref, at) in enumerate(
        ((mid_ref, 0), (mid_ref, 1), (hi_ref, 0), (hi_ref, 1), (lo_ref, 0), (lo_ref, 1), (lo_ref, 2), (mid_ref, 2))
    ):
        take_slot(packed_ref, slot, out_ref, at)


def first_kernel(lev, vel, dif, x_ref, u_ref):
    fac = factors(lev, vel, dif)

    def plane(p, _):
        for i in range(16):
            u_ref[p, i] = step_row(x_ref, p, i, fac)
        return 0

    lax.fori_loop(0, 16, plane, 0)


def layer_step(u, below, above, center, lo, hi):
    def wide(v):
        return jnp.concatenate([v, v], axis=1)

    lane = lane_id((16, 256)) & 15
    out = wide(center) * u + wide(lo[0]) * pltpu.roll(u, 1, 0) + wide(hi[0]) * pltpu.roll(u, 15, 0)
    out = out + wide(lo[1]) * pltpu.roll(u, 16, 1) + wide(hi[1]) * pltpu.roll(u, 240, 1)
    down = jnp.where(lane == 0, pltpu.roll(u, 241, 1), pltpu.roll(u, 1, 1))
    up = jnp.where(lane == 15, pltpu.roll(u, 15, 1), pltpu.roll(u, 255, 1))
    out = out + wide(lo[2]) * down + wide(hi[2]) * up
    return out + wide(lo[3]) * below + wide(hi[3]) * above


def layers_kernel(lev, vel, dif, wgt, pos, lo_ref, hi_ref, mid_ref, left_ref, right_ref, edge_ref, shared_ref, packed_ref):
    fac = factors(lev, vel, dif)
    weight = wgt[0].astype(F32)

    def step(seq):
        return [layer_step(seq[k], seq[k - 1], seq[k + 1], *fac) for k in range(1, len(seq) - 1)]

    low = step(step([left_ref[0], left_ref[1], lo_ref[0], lo_ref[1], lo_ref[2], mid_ref[2]]))
    high = step(step([mid_ref[0], mid_ref[1], hi_ref[0], hi_ref[1], right_ref[0], right_ref[1], right_ref[2]]))
    packed_ref[...] = jnp.zeros_like(packed_ref)
    for slot, value in enumerate((high[0], high[1], low[0], low[1], high[2])):
        put_slot(packed_ref, slot, weight * value)
    edge_ref[...] = packed_ref[...].reshape(256, 128)
    shared = jnp.where((pos[1] & 1) == 1, weight * high[2], weight * low[0])
    shared_ref[0:16] = shared[:, :128]
    shared_ref[16:32] = shared[:, 128:]


def partners(y):
    return y, y ^ 1, 3 - y, y ^ 2


def second_kernel(chunk, lev, vel, dif, wgt, pos, u_ref, edge_ref, shared_ref, *outs):
    fac = factors(lev, vel, dif)
    weight = wgt[0].astype(F32)
    for target, out_ref in zip(partners(pos[0]), outs):

        def body(r, _, target=target, out_ref=out_ref):
            p = 4 * target + 2 * chunk + r
            base = pl.multiple_of(272 * r, 16)
            for i in range(16):
                out_ref[pl.ds(base + 16 * i, 16), :] = weight * step_row(u_ref, p, i, fac)
            out_ref[pl.ds(base + 256, 16), :] = edge_ref[pl.ds(pl.multiple_of(16 * p, 16), 16), :]
            return 0

        lax.fori_loop(0, 2, body, 0)
        if out_ref.shape[0] > 544:
            out_ref[544:] = shared_ref[...]


def surplus_rows(a_ref, b_ref, mat_ref, o_ref, packed_ref):
    packed_ref[...] = jnp.zeros_like(packed_ref)
    for n in range(2):
        at = slice(272 * n + 256, 272 * n + 272)
        packed_ref[16 * n : 16 * n + 16] = a_ref[at] + b_ref[at]
    turned = packed_ref[...].T
    lane = lane_id((1, 128))
    edge = (lane < 2) | (lane > 125)
    ramp = lane.astype(F32) * (1.0 / 128.0)
    for n in range(2):
        for h in range(2):
            at = slice(272 * n + 128 * h, 272 * n + 128 * h + 128)
            ends = pltpu.roll(turned, 126 - 8 * (2 * n + h), 1)
            full = jnp.where(edge, ends, a_ref[at] + b_ref[at]) - ramp * ends[:, 2:3]
            o_ref[256 * n + 128 * h : 256 * n + 128 * h + 128] = jnp.dot(
                full, mat_ref[...], precision=lax.Precision.HIGHEST, preferred_element_type=F32
            )


def surplus_kernel(a_ref, b_ref, mat_ref, o_ref, shared_ref, packed_ref):
    shared_ref[...] = a_ref[544:] + b_ref[544:]
    surplus_rows(a_ref, b_ref, mat_ref, o_ref, packed_ref)


def surplus_fix_kernel(pos, table, a_ref, b_ref, mat_ref, shared_ref, *rest):
    got, (o_ref, packed_ref) = rest[:-2], rest[-2:]
    surplus_rows(a_ref, b_ref, mat_ref, o_ref, packed_ref)
    at = 32 * pos[0] + pos[1]
    fix = table[len(got), at] * shared_ref[...]
    for k, ref in enumerate(got):
        fix = fix + table[k, at] * ref[...]
    o_ref[512:] = fix


def last_kernel(pos, *refs):
    pieces, (out_ref, packed_ref, turned_ref) = refs[:-3], refs[-3:]
    fix = sum(ref[512:] for ref in pieces[4:])
    for b in range(2):
        for h in range(2):
            packed_ref[b, pl.ds(8 * h, 8, stride=16), :] = fix[16 * h + 8 * b : 16 * h + 8 * b + 8]
        turned_ref[b] = packed_ref[b].T
    first = lane_id((1, 128)) == 0
    for chunk in range(2):
        for target, src in zip(partners(pos[0]), pieces[4 * chunk : 4 * chunk + 4]):
            turned = turned_ref[lax.shift_right_logical(target, 1)]
            for r in range(2):
                p = 4 * target + 2 * chunk + r
                for h in range(2):
                    k = (2 * p + h) & 15
                    fixed = pltpu.roll(turned, (128 - 8 * k) & 127, 1)
                    part = src[256 * r + 128 * h : 256 * r + 128 * h + 128, :] + jnp.where(first, fixed, 0.0)
                    out_ref[p, 8 * h : 8 * h + 8] = part.reshape(8, 16, 128)


def surplus_matrix():
    m = np.eye(128, dtype=np.float32)
    for j in range(1, 128):
        s = j & -j
        m[j - s, j] -= 0.5
        if j + s < 128:
            m[j + s, j] -= 0.5
    return m


def after(value, *others):
    return lax.optimization_barrier((value,) + others)[0]


def tree_edges(n, replicas):
    edges = []
    for b in range(1, n):
        s = b & -b
        if s == 1:
            edges.append((b - 1, b, -0.5))
        elif (b + s) % n == b - s:
            edges.append((b - s, b, -1.0))
        else:
            edges += [(b - s, b, -0.5), ((b + s) % n, b, -0.5)]
    degree = [sum(e[0] == b for e in edges) for b in range(n)]
    colours = max(degree + [sum(e[1] == b for e in edges) for b in range(n)])
    colours = -(-colours // replicas) * replicas
    out, into, used = {}, {}, {}

    def swap_path(v, side, c, d):
        path, here, colour = [], (side, v), c
        while True:
            key = (out if here[0] == 0 else into).get((here[1], colour))
            if key is None:
                break
            path.append((key, colour))
            here = (1 - here[0], key[1] if here[0] == 0 else key[0])
            colour = d if colour == c else c
        for key, col in path:
            del out[(key[0], col)], into[(key[1], col)]
        for key, col in path:
            new = d if col == c else c
            out[(key[0], new)] = into[(key[1], new)] = key
            used[key] = new

    for src, dst, _ in sorted(edges, key=lambda e: (-degree[e[0]], e)):
        free_src = [c for c in range(colours) if (src, c) not in out]
        free_dst = [c for c in range(colours) if (dst, c) not in into]
        both = [c for c in free_src if c in free_dst]
        colour = both[0] if both else free_src[0]
        if not both:
            swap_path(dst, 1, colour, free_dst[0])
        out[(src, colour)] = into[(dst, colour)] = (src, dst)
        used[(src, dst)] = colour
    count = colours // replicas
    rounds = [[] for _ in range(count)]
    table = np.zeros((count + 1, replicas * n), np.float32)
    for src, dst, factor in edges:
        k, y = divmod(used[(src, dst)], replicas)
        rounds[k].append((y * n + src, y * n + dst))
        table[k, y * n + dst] = factor
    table[count, 1:n:2] = -0.5
    return rounds, table


def local(initial, levels, weights, velocity, diffusivity):
    others = [[(i, partners(i)[k]) for i in range(4)] for k in (1, 2, 3)]
    pair = [(0, 1), (1, 0)]
    n = lax.axis_size(BRICK)
    up = [(i, (i + 1) % n) for i in range(n)]
    down = [(i, (i - 1) % n) for i in range(n)]
    x = initial[0]
    pos = jnp.stack([lax.axis_index("y"), lax.axis_index(BRICK)]).astype(jnp.int32)
    scalars = (levels, velocity, diffusivity, weights, pos)

    def struct(*shape):
        return jax.ShapeDtypeStruct(shape, F32)

    full, lo, hi, mid = pl.pallas_call(
        ends_kernel,
        out_shape=(struct(*x.shape), struct(3, 16, 256), struct(2, 16, 256), struct(3, 16, 256)),
        in_specs=[pl.BlockSpec(memory_space=pltpu.HBM)],
        out_specs=(VM,) * 4,
        scratch_shapes=[pltpu.VMEM((2, 128, 128), F32), pltpu.SemaphoreType.DMA((4,))],
        compiler_params=grant(4),
    )(x)
    left = lax.ppermute(hi, BRICK, up)
    right = lax.ppermute(lo, BRICK, down)
    cost = pl.CostEstimate(flops=10000000, bytes_accessed=4 << 20, transcendentals=0)
    u = pl.pallas_call(
        first_kernel,
        out_shape=struct(*x.shape),
        in_specs=[SM] * 3 + [VM],
        out_specs=VM,
        compiler_params=grant(6),
        cost_estimate=cost,
    )(levels, velocity, diffusivity, full)
    left, right = after((left, right), u)
    edges, shared = pl.pallas_call(
        layers_kernel,
        out_shape=(struct(256, 128), struct(32, 128)),
        scratch_shapes=[pltpu.VMEM((2, 128, 128), F32)],
        in_specs=[SM] * 5 + [VM] * 5,
        out_specs=(VM,) * 2,
        compiler_params=grant(2),
    )(*scalars, lo, hi, mid, left, right)

    def second(c, value):
        return pl.pallas_call(
            functools.partial(second_kernel, c),
            out_shape=(struct(544 if c else 576, 128),) * 4,
            in_specs=[SM] * 5 + [VM] * 3,
            out_specs=(VM,) * 4,
            compiler_params=grant(5),
            cost_estimate=cost,
        )(*scalars, value, edges, shared)

    def to_others(values):
        return [lax.ppermute(value, "y", perm) for value, perm in zip(values, others)]

    matrix = jnp.asarray(surplus_matrix())
    rounds, table = tree_edges(n, 4)
    parts0 = second(0, u)
    got0 = to_others(parts0[1:])
    parts1 = second(1, after(u, parts0[0]))
    got1 = to_others(after(parts1[1:], got0[0]))
    summed0 = parts0[0] + got0[0] + got0[1] + got0[2]
    other0 = lax.ppermute(summed0, "zh", pair)
    summed1 = parts1[0] + got1[0] + got1[1] + got1[2]
    other1 = lax.ppermute(summed1, "zh", pair)
    own0, shared = pl.pallas_call(
        surplus_kernel,
        out_shape=(struct(512, 128), struct(32, 128)),
        in_specs=[VM] * 3,
        out_specs=(VM,) * 2,
        scratch_shapes=[pltpu.VMEM((128, 128), F32)],
        compiler_params=grant(2),
    )(summed0, after(other0, summed1), matrix)
    pieces0 = [own0] + to_others([own0] * 3)
    got = [lax.ppermute(shared, ("y",) + BRICK, r) for r in rounds]
    own1 = pl.pallas_call(
        surplus_fix_kernel,
        out_shape=struct(544, 128),
        in_specs=[SM] * 2 + [VM] * (4 + len(got)),
        out_specs=VM,
        scratch_shapes=[pltpu.VMEM((128, 128), F32)],
        compiler_params=grant(2),
    )(pos, jnp.asarray(table), summed1, after(other1, *pieces0), matrix, shared, *got)
    pieces = pieces0 + [own1] + to_others([own1] * 3)

    return pl.pallas_call(
        last_kernel,
        out_shape=struct(16, 16, 16, 128),
        in_specs=[SM] + [VM] * len(pieces),
        out_specs=VM,
        scratch_shapes=[pltpu.VMEM((2, 128, 128), F32)] * 2,
        compiler_params=grant(8),
    )(pos, *pieces)


def solution(mesh):
    wide = Mesh(mesh.devices.reshape(2, 4, 4, 4, 2), ("zh", "y", "x", "zl", "core"))
    comp = ("zh", "y")
    return jax.shard_map(
        local,
        mesh=wide,
        in_specs=(P(comp, None, None, None, BRICK), P(comp, None), P(comp), P(), P()),
        out_specs=P(None, None, None, BRICK),
        check_vma=False,
    )
```

time: 470 us -> 98 us (0.21); the launches traced: 463 us -> 97.8 us
  local copies, waits for them, and re-layouts: 144 us -> 1.64 us
  waiting for transfers between devices: 180 us -> 46.3 us
  blocking collectives: 59.3 us -> 0 us
  other arithmetic: 48.8 us -> 0.25 us
  starting transfers between devices: 15.9 us -> 36 us
  between operations: 15.1 us -> 0.83 us
  Pallas kernels: 0 us -> 12.7 us
    psum x1 -> x0, waiting for transfers between devices: 133 us -> none  [local(): return lax.psum(term, 'comp')]
    scatter x12 -> x0, local copies, waits for them, and re-layouts: 66.2 us -> none  [surplus_lines(): result = result.reshape(row_count, line_len // (2 * stride), 2 * stride)....]
    all_to_all x1 -> x0, blocking collectives: 59.3 us -> none  [local(): lax.all_to_all(rows, 'brick', split_axis=0, concat_axis=1, tiled=True)]
    slice x31 -> x0, local copies, waits for them, and re-layouts: 47.6 us -> none  [the longest x12 14.4 us: substep_wide(): lower = jnp.roll(center, 1, axis=axis_num)]
    all_to_all x1 -> x0, waiting for transfers between devices: 47.2 us -> none  [local(): lax.all_to_all(lines, 'brick', split_axis=1, concat_axis=0, tiled=True)]
    ppermute x4 -> x18, waiting for transfers between devices: 0.01 us -> 46.3 us  [the longest x12 25.8 us: to_others(): lax.ppermute(value, 'y', perm)]
    add x2, other arithmetic: 28.1 us -> 0.18 us  [the longest x1 0.09 us: local(): summed0 = parts0[0] + got0[0] + got0[1] + got0[2]]
    ppermute x4 -> x18, starting transfers between devices: 9.31 us -> 36 us  [the longest x12 17.4 us: to_others(): lax.ppermute(value, 'y', perm)]
  transfers between devices with their start and end apart: 6 -> 18, of which waited for: 2 -> 9; matrix products, arithmetic and copies ran while one was open for 4% -> 0% of each run, Pallas kernels for 0% -> 5%
where the time goes in v2:
time: 98 us; the launch traced here: 97.8 us
  waiting for transfers between devices  46.3 us (47%)
  starting transfers between devices  36 us (37%)
  Pallas kernels  12.7 us (13%)
  local copies, waits for them, and re-layouts  1.64 us (2%)
    ppermute x12, waiting for transfers between devices, to_others(): lax.ppermute(value, 'y', perm)  25.8 us
    ppermute x12, starting transfers between devices, to_others(): lax.ppermute(value, 'y', perm)  17.4 us
    ppermute x1, waiting for transfers between devices, local(): other0 = lax.ppermute(summed0, 'zh', pair)  16 us
    ppermute x1, starting transfers between devices, local(): other0 = lax.ppermute(summed0, 'zh', pair)  6.08 us
    ppermute x2, waiting for transfers between devices, local(): got = [lax.ppermute(shared, ('y',) + BRICK, r) for r in rounds]  4.53 us
    ppermute x1, starting transfers between devices, local(): right = lax.ppermute(lo, BRICK, down)  4.43 us
    ppermute x2, starting transfers between devices, local(): got = [lax.ppermute(shared, ('y',) + BRICK, r) for r in rounds]  4.34 us
    ppermute x1, starting transfers between devices, local(): other1 = lax.ppermute(summed1, 'zh', pair)  3.73 us
  transfers between devices with their start and end apart: 18, of which 9 were waited for; matrix products, arithmetic and copies ran while one was open for 0% of the time, Pallas kernels for 5%

profile of v2, /device:TPU:4, one launch (start us, length us, event | category | flops | bytes accessed | tf_op | source)
XLA Modules:
  0.0 97.8 jit_solution(14735645563943692298)
XLA Ops:
  0.0 1.6 %copy-done = f32[1,16,16,16,128]{4,3,2,1,0:T(8,128)S(1)} copy-done((f32[1,16,16,16,128]{4,3,2,1,0:T(8,128)S(1)}, f32[1,16,16,16,128]{4,3,2,1,0:T(8,128)}, u32[]{:S(2)}) %copy-start) | copy-done | bytes 2097176
  1.6 1.2 %shard_map.73 = (f32[16,16,16,128]{3,2,1,0:T(8,128)S(1)}, f32[3,16,256]{2,1,0:T(8,128)S(1)}, f32[2,16,256]{2,1,0:T(8,128)S(1)}, f32[3,16,256]{2,1,0:T(8,128)S(1)}) custom-call(f32[16,16,16,128]{3,2,1,0:T(8,128)S(1)} %bitcast.3), custom_call_target="tpu_custom_call" | custom-call | tf_op jit(solution)/shard_map/pallas_call | solution.py:272
  2.8 0.1 collective-permute-start
  2.9 4.4 %collective-permute-start.1 = (f32[3,16,256]{2,1,0:T(8,128)S(1)}, f32[3,16,256]{2,1,0:T(8,128)S(1)}, u32[]{:S(2)}, u32[]{:S(2)}) collective-permute-start(f32[3,16,256]{2,1,0:T(8,128)S(1)} %get-tuple-element.30.lo_ref), channel_id=1, source_target_pairs={{0,31},{1,0},{2,1},{3,2},{4,3},{5,4},{6,5},{7,6},{8,7},{9,8},{10,9... | collective-permute-start | bytes 147464 | tf_op jit(solution)/shard_map/ppermute | solution.py:281
  7.3 0.1 pad_add_fusion.pos
  8.1 2.8 %shard_map.74.u_ref = f32[16,16,16,128]{3,2,1,0:T(8,128)S(1)} custom-call(s32[1,4]{1,0:T(1,128)S(1)} %copy-done.2, f32[4]{0:T(128)S(1)} %copy-done.3, f32[4]{0:T(128)S(1)} %copy-done.4, f32[16,16,16,128]{3,2,1,0:T(8,128)S(1)} %get-tuple-element.29.x_ref), custom_call_target="tpu_custom_call" | custom-call | flops 10000000 | bytes 4194304 | tf_op jit(solution)/shard_map/pallas_call | solution.py:283
  10.9 0.0 collective-permute-done.left_ref
  10.9 1.0 %shard_map.75 = (f32[256,128]{1,0:T(8,128)S(1)}, f32[32,128]{1,0:T(8,128)S(1)}) custom-call(s32[1,4]{1,0:T(1,128)S(1)} %copy-done.2, f32[4]{0:T(128)S(1)} %copy-done.3, f32[4]{0:T(128)S(1)} %copy-done.4, s32[1]{0:T(128)S(6)} %copy.8.wgt, s32[2]{0:T(128)S(1)} %pad_add_fusion.pos, f32[3,16,256]{2,1,0:T(8,128)S(1)} %get-tuple-element.30.lo_ref, ...), custom_call_target="tpu_custom_call" | custom-call | tf_op jit(solution)/shard_map/pallas_call | solution.py:292
  11.9 1.7 %shard_map.76 = (f32[576,128]{1,0:T(8,128)S(1)}, f32[576,128]{1,0:T(8,128)S(1)}, f32[576,128]{1,0:T(8,128)S(1)}, f32[576,128]{1,0:T(8,128)S(1)}) custom-call(s32[1,4]{1,0:T(1,128)S(1)} %copy-done.2, f32[4]{0:T(128)S(1)} %copy-done.3, f32[4]{0:T(128)S(1)} %copy-done.4, s32[1]{0:T(128)S(6)} %copy.8.wgt, s32[2]{0:T(128)S(1)} %pad_add_fusion.pos, ...), custom_call_target="tpu_custom_call" | custom-call | flops 10000000 | bytes 4194304 | tf_op jit(solution)/shard_map/pallas_call | solution.py:302
  13.6 1.7 %collective-permute-start.2 = (f32[576,128]{1,0:T(8,128)S(1)}, f32[576,128]{1,0:T(8,128)S(1)}, u32[]{:S(2)}, u32[]{:S(2)}) collective-permute-start(f32[576,128]{1,0:T(8,128)S(1)} %get-tuple-element.38), channel_id=1, source_target_pairs={{0,32},{32,0},{64,96},{96,64},{1,33},{33,1},{65,97},{97,65},{2,34}... | collective-permute-start | bytes 884744 | tf_op jit(solution)/shard_map/ppermute | solution.py:312
  15.3 2.9 %collective-permute-start.4 = (f32[576,128]{1,0:T(8,128)S(1)}, f32[576,128]{1,0:T(8,128)S(1)}, u32[]{:S(2)}, u32[]{:S(2)}) collective-permute-start(f32[576,128]{1,0:T(8,128)S(1)} %get-tuple-element.40), channel_id=1, source_target_pairs={{0,64},{32,96},{64,0},{96,32},{1,65},{33,97},{65,1},{97,33},{2,66}... | collective-permute-start | bytes 884744 | tf_op jit(solution)/shard_map/ppermute | solution.py:312
  18.2 0.2 collective-permute-start.3
  18.4 1.7 %shard_map.77 = (f32[544,128]{1,0:T(8,128)S(1)}, f32[544,128]{1,0:T(8,128)S(1)}, f32[544,128]{1,0:T(8,128)S(1)}, f32[544,128]{1,0:T(8,128)S(1)}) custom-call(s32[1,4]{1,0:T(1,128)S(1)} %copy-done.2, f32[4]{0:T(128)S(1)} %copy-done.3, f32[4]{0:T(128)S(1)} %copy-done.4, s32[1]{0:T(128)S(6)} %copy.8.wgt, s32[2]{0:T(128)S(1)} %pad_add_fusion.pos, ...), custom_call_target="tpu_custom_call" | custom-call | flops 10000000 | bytes 4194304 | tf_op jit(solution)/shard_map/pallas_call | solution.py:302
  20.1 0.0 copy-start.5
  20.2 3.5 %collective-permute-done.2 = f32[576,128]{1,0:T(8,128)S(1)} collective-permute-done((f32[576,128]{1,0:T(8,128)S(1)}, f32[576,128]{1,0:T(8,128)S(1)}, u32[]{:S(2)}, u32[]{:S(2)}) %collective-permute-start.2) | collective-permute-done | bytes 294944 | tf_op jit(solution)/shard_map/ppermute | solution.py:312
  23.7 3.2 %collective-permute-start.8 = (f32[544,128]{1,0:T(8,128)S(1)}, f32[544,128]{1,0:T(8,128)S(1)}, u32[]{:S(2)}, u32[]{:S(2)}) collective-permute-start(f32[544,128]{1,0:T(8,128)S(1)} %get-tuple-element.48), channel_id=1, source_target_pairs={{0,64},{32,96},{64,0},{96,32},{1,65},{33,97},{65,1},{97,33},{2,66}... | collective-permute-start | bytes 835592 | tf_op jit(solution)/shard_map/ppermute | solution.py:312
  26.9 1.1 %collective-permute-start.7 = (f32[544,128]{1,0:T(8,128)S(1)}, f32[544,128]{1,0:T(8,128)S(1)}, u32[]{:S(2)}, u32[]{:S(2)}) collective-permute-start(f32[544,128]{1,0:T(8,128)S(1)} %get-tuple-element.47), channel_id=1, source_target_pairs={{0,96},{32,64},{64,32},{96,0},{1,97},{33,65},{65,33},{97,1},{2,98}... | collective-permute-start | bytes 835592 | tf_op jit(solution)/shard_map/ppermute | solution.py:312
  27.9 0.0 collective-permute-start.6
  27.9 4.6 %collective-permute-done.4 = f32[576,128]{1,0:T(8,128)S(1)} collective-permute-done((f32[576,128]{1,0:T(8,128)S(1)}, f32[576,128]{1,0:T(8,128)S(1)}, u32[]{:S(2)}, u32[]{:S(2)}) %collective-permute-start.4) | collective-permute-done | bytes 294944 | tf_op jit(solution)/shard_map/ppermute | solution.py:312
  32.5 7.8 %collective-permute-done.3 = f32[576,128]{1,0:T(8,128)S(1)} collective-permute-done((f32[576,128]{1,0:T(8,128)S(1)}, f32[576,128]{1,0:T(8,128)S(1)}, u32[]{:S(2)}, u32[]{:S(2)}) %collective-permute-start.3) | collective-permute-done | bytes 294944 | tf_op jit(solution)/shard_map/ppermute | solution.py:312
  40.3 0.1 add_add_fusion.a_ref
  40.4 6.1 %collective-permute-start.5 = (f32[576,128]{1,0:T(8,128)S(1)}, f32[576,128]{1,0:T(8,128)S(1)}, u32[]{:S(2)}, u32[]{:S(2)}) collective-permute-start(f32[576,128]{1,0:T(8,128)S(1)} %add_add_fusion.a_ref), channel_id=1, source_target_pairs={{0,128},{128,0},{1,129},{129,1},{2,130},{130,2},{3,131},{131,3},{4... | collective-permute-start | bytes 884744 | tf_op jit(solution)/shard_map/ppermute | solution.py:321
  46.5 0.0 collective-permute-done.8
  46.5 0.0 collective-permute-done.7
  46.5 0.0 collective-permute-done.6
  46.5 0.1 add_add_fusion.1.a_ref
  46.6 3.7 %collective-permute-start.12 = (f32[544,128]{1,0:T(8,128)S(1)}, f32[544,128]{1,0:T(8,128)S(1)}, u32[]{:S(2)}, u32[]{:S(2)}) collective-permute-start(f32[544,128]{1,0:T(8,128)S(1)} %add_add_fusion.1.a_ref), channel_id=1, source_target_pairs={{0,128},{128,0},{1,129},{129,1},{2,130},{130,2},{3,131},{131,3},{4... | collective-permute-start | bytes 835592 | tf_op jit(solution)/shard_map/ppermute | solution.py:323
  50.3 16.0 %collective-permute-done.5.b_ref = f32[576,128]{1,0:T(8,128)S(1)} collective-permute-done((f32[576,128]{1,0:T(8,128)S(1)}, f32[576,128]{1,0:T(8,128)S(1)}, u32[]{:S(2)}, u32[]{:S(2)}) %collective-permute-start.5) | collective-permute-done | bytes 294944 | tf_op jit(solution)/shard_map/ppermute | solution.py:321
  66.3 0.6 shard_map.78
  66.9 0.1 collective-permute-start.9
  67.0 0.3 collective-permute-start.10
  67.4 3.7 %collective-permute-start.11 = (f32[512,128]{1,0:T(8,128)S(1)}, f32[512,128]{1,0:T(8,128)S(1)}, u32[]{:S(2)}, u32[]{:S(2)}) collective-permute-start(f32[512,128]{1,0:T(8,128)S(1)} %get-tuple-element.50.refs_0_), channel_id=1, source_target_pairs={{0,64},{32,96},{64,0},{96,32},{1,65},{33,97},{65,1},{97,33},{2,66}... | collective-permute-start | bytes 786440 | tf_op jit(solution)/shard_map/ppermute | solution.py:312
  71.1 2.4 %collective-permute-start.13 = (f32[32,128]{1,0:T(8,128)S(1)}, f32[32,128]{1,0:T(8,128)S(1)}, u32[]{:S(2)}, u32[]{:S(2)}) collective-permute-start(f32[32,128]{1,0:T(8,128)S(1)} %get-tuple-element.52.shared_ref), channel_id=1, source_target_pairs={{0,1},{32,34},{4,2},{2,3},{64,68},{8,4},{36,37},{68,70},{40,38},{6... | collective-permute-start | bytes 49160 | tf_op jit(solution)/shard_map/ppermute | solution.py:333
  73.6 2.4 %collective-permute-done.9.refs_1_ = f32[512,128]{1,0:T(8,128)S(1)} collective-permute-done((f32[512,128]{1,0:T(8,128)S(1)}, f32[512,128]{1,0:T(8,128)S(1)}, u32[]{:S(2)}, u32[]{:S(2)}) %collective-permute-start.9) | collective-permute-done | bytes 262176 | tf_op jit(solution)/shard_map/ppermute | solution.py:312
  76.0 1.9 %collective-permute-start.14 = (f32[32,128]{1,0:T(8,128)S(1)}, f32[32,128]{1,0:T(8,128)S(1)}, u32[]{:S(2)}, u32[]{:S(2)}) collective-permute-start(f32[32,128]{1,0:T(8,128)S(1)} %get-tuple-element.52.shared_ref), channel_id=1, source_target_pairs={{8,12},{0,16},{16,18},{48,52},{80,88},{32,56},{24,28},{64,92},{96,... | collective-permute-start | bytes 49160 | tf_op jit(solution)/shard_map/ppermute | solution.py:333
  77.9 0.7 collective-permute-done.10.refs_2_
  78.6 0.0 collective-permute-done.11.refs_3_
  78.6 0.0 collective-permute-done.12.b_ref
  78.6 0.0 collective-permute-done.13.rest_0_
  78.6 4.5 %collective-permute-done.14.rest_1_ = f32[32,128]{1,0:T(8,128)S(1)} collective-permute-done((f32[32,128]{1,0:T(8,128)S(1)}, f32[32,128]{1,0:T(8,128)S(1)}, u32[]{:S(2)}, u32[]{:S(2)}) %collective-permute-start.14) | collective-permute-done | bytes 16416 | tf_op jit(solution)/shard_map/ppermute | solution.py:333
  83.1 1.2 %shard_map.79.refs_4_ = f32[544,128]{1,0:T(8,128)S(1)} custom-call(s32[2]{0:T(128)S(1)} %pad_add_fusion.pos, f32[3,128]{1,0:T(4,128)S(1)} %copy-done.5, f32[544,128]{1,0:T(8,128)S(1)} %add_add_fusion.1.a_ref, f32[544,128]{1,0:T(8,128)S(1)} %collective-permute-done.12.b_ref, f32[128,128]{1,0:T(8,128)S(1)} %copy-done.1, ...), custom_call_target="tpu_custom_call" | custom-call | tf_op jit(solution)/shard_map/pallas_call | solution.py:334
  84.3 0.1 collective-permute-start.15
  84.4 0.1 collective-permute-start.16
  84.5 4.0 %collective-permute-start.17 = (f32[544,128]{1,0:T(8,128)S(1)}, f32[544,128]{1,0:T(8,128)S(1)}, u32[]{:S(2)}, u32[]{:S(2)}) collective-permute-start(f32[544,128]{1,0:T(8,128)S(1)} %shard_map.79.refs_4_), channel_id=1, source_target_pairs={{0,64},{32,96},{64,0},{96,32},{1,65},{33,97},{65,1},{97,33},{2,66}... | collective-permute-start | bytes 835592 | tf_op jit(solution)/shard_map/ppermute | solution.py:312
  88.5 2.5 %collective-permute-done.15.refs_5_ = f32[544,128]{1,0:T(8,128)S(1)} collective-permute-done((f32[544,128]{1,0:T(8,128)S(1)}, f32[544,128]{1,0:T(8,128)S(1)}, u32[]{:S(2)}, u32[]{:S(2)}) %collective-permute-start.15) | collective-permute-done | bytes 278560 | tf_op jit(solution)/shard_map/ppermute | solution.py:312
  90.9 4.3 %collective-permute-done.16.refs_6_ = f32[544,128]{1,0:T(8,128)S(1)} collective-permute-done((f32[544,128]{1,0:T(8,128)S(1)}, f32[544,128]{1,0:T(8,128)S(1)}, u32[]{:S(2)}, u32[]{:S(2)}) %collective-permute-start.16) | collective-permute-done | bytes 278560 | tf_op jit(solution)/shard_map/ppermute | solution.py:312
  95.2 0.0 collective-permute-done.17.refs_7_
  95.2 2.6 %shard_map.80 = f32[16,16,16,128]{3,2,1,0:T(8,128)} custom-call(s32[2]{0:T(128)S(1)} %pad_add_fusion.pos, f32[512,128]{1,0:T(8,128)S(1)} %get-tuple-element.50.refs_0_, f32[512,128]{1,0:T(8,128)S(1)} %collective-permute-done.9.refs_1_, f32[512,128]{1,0:T(8,128)S(1)} %collective-permute-done.10.refs_2_, f32[512,128]{1,0:T(8,128)S(1)} %collective-permute-done.11.refs_3_, ...), custom_call_target="tpu_custom_call" | custom-call | tf_op jit(solution)/shard_map/pallas_call | solution.py:344
  (11 shorter events, 0.0 us)
Async XLA Ops:
  0.0 8.1 %copy-start.2 = (s32[1,4]{1,0:T(1,128)S(1)}, s32[1,4]{1,0:T(1,128)}, u32[]{:S(2)}) copy-start(s32[1,4]{1,0:T(1,128)} %lev.7) | copy-start | bytes 52
  0.0 8.1 %copy-start.3 = (f32[4]{0:T(128)S(1)}, f32[4]{0:T(128)}, u32[]{:S(2)}) copy-start(f32[4]{0:T(128)} %vel.7) | copy-start | bytes 52
  0.0 8.1 %copy-start.4 = (f32[4]{0:T(128)S(1)}, f32[4]{0:T(128)}, u32[]{:S(2)}) copy-start(f32[4]{0:T(128)} %dif.7) | copy-start | bytes 52
  0.0 1.6 %copy-start = (f32[1,16,16,16,128]{4,3,2,1,0:T(8,128)S(1)}, f32[1,16,16,16,128]{4,3,2,1,0:T(8,128)}, u32[]{:S(2)}) copy-start(f32[1,16,16,16,128]{4,3,2,1,0:T(8,128)} %param.7) | copy-start | bytes 6291460
  2.8 8.1 %collective-permute-start = (f32[2,16,256]{2,1,0:T(8,128)S(1)}, f32[2,16,256]{2,1,0:T(8,128)S(1)}, u32[]{:S(2)}, u32[]{:S(2)}) collective-permute-start(f32[2,16,256]{2,1,0:T(8,128)S(1)} %get-tuple-element.31.hi_ref), channel_id=1, source_target_pairs={{0,1},{1,2},{2,3},{3,4},{4,5},{5,6},{6,7},{7,8},{8,9},{9,10},{10,1... | collective-permute-start | bytes 98312 | tf_op jit(solution)/shard_map/ppermute | solution.py:280
  2.9 8.0 %collective-permute-start.1 = (f32[3,16,256]{2,1,0:T(8,128)S(1)}, f32[3,16,256]{2,1,0:T(8,128)S(1)}, u32[]{:S(2)}, u32[]{:S(2)}) collective-permute-start(f32[3,16,256]{2,1,0:T(8,128)S(1)} %get-tuple-element.30.lo_ref), channel_id=1, source_target_pairs={{0,31},{1,0},{2,1},{3,2},{4,3},{5,4},{6,5},{7,6},{8,7},{9,8},{10,9... | collective-permute-start | bytes 147464 | tf_op jit(solution)/shard_map/ppermute | solution.py:281
  13.6 10.0 %collective-permute-start.2 = (f32[576,128]{1,0:T(8,128)S(1)}, f32[576,128]{1,0:T(8,128)S(1)}, u32[]{:S(2)}, u32[]{:S(2)}) collective-permute-start(f32[576,128]{1,0:T(8,128)S(1)} %get-tuple-element.38), channel_id=1, source_target_pairs={{0,32},{32,0},{64,96},{96,64},{1,33},{33,1},{65,97},{97,65},{2,34}... | collective-permute-start | bytes 884744 | tf_op jit(solution)/shard_map/ppermute | solution.py:312
  15.3 17.2 %collective-permute-start.4 = (f32[576,128]{1,0:T(8,128)S(1)}, f32[576,128]{1,0:T(8,128)S(1)}, u32[]{:S(2)}, u32[]{:S(2)}) collective-permute-start(f32[576,128]{1,0:T(8,128)S(1)} %get-tuple-element.40), channel_id=1, source_target_pairs={{0,64},{32,96},{64,0},{96,32},{1,65},{33,97},{65,1},{97,33},{2,66}... | collective-permute-start | bytes 884744 | tf_op jit(solution)/shard_map/ppermute | solution.py:312
  18.2 22.1 %collective-permute-start.3 = (f32[576,128]{1,0:T(8,128)S(1)}, f32[576,128]{1,0:T(8,128)S(1)}, u32[]{:S(2)}, u32[]{:S(2)}) collective-permute-start(f32[576,128]{1,0:T(8,128)S(1)} %get-tuple-element.39), channel_id=1, source_target_pairs={{0,96},{32,64},{64,32},{96,0},{1,97},{33,65},{65,33},{97,1},{2,98}... | collective-permute-start | bytes 884744 | tf_op jit(solution)/shard_map/ppermute | solution.py:312
  18.4 47.9 %copy-start.1 = (f32[128,128]{1,0:T(8,128)S(1)}, f32[128,128]{1,0:T(8,128)}, u32[]{:S(2)}) copy-start(f32[128,128]{1,0:T(8,128)} %constant.23.clone.mat_ref) | copy-start | bytes 196612
  20.1 63.0 %copy-start.5 = (f32[3,128]{1,0:T(4,128)S(1)}, f32[3,128]{1,0:T(4,128)}, u32[]{:S(2)}) copy-start(f32[3,128]{1,0:T(4,128)} %constant.24.clone.table) | copy-start | bytes 4612
  23.7 22.8 %collective-permute-start.8 = (f32[544,128]{1,0:T(8,128)S(1)}, f32[544,128]{1,0:T(8,128)S(1)}, u32[]{:S(2)}, u32[]{:S(2)}) collective-permute-start(f32[544,128]{1,0:T(8,128)S(1)} %get-tuple-element.48), channel_id=1, source_target_pairs={{0,64},{32,96},{64,0},{96,32},{1,65},{33,97},{65,1},{97,33},{2,66}... | collective-permute-start | bytes 835592 | tf_op jit(solution)/shard_map/ppermute | solution.py:312
  26.9 19.6 %collective-permute-start.7 = (f32[544,128]{1,0:T(8,128)S(1)}, f32[544,128]{1,0:T(8,128)S(1)}, u32[]{:S(2)}, u32[]{:S(2)}) collective-permute-start(f32[544,128]{1,0:T(8,128)S(1)} %get-tuple-element.47), channel_id=1, source_target_pairs={{0,96},{32,64},{64,32},{96,0},{1,97},{33,65},{65,33},{97,1},{2,98}... | collective-permute-start | bytes 835592 | tf_op jit(solution)/shard_map/ppermute | solution.py:312
  27.9 18.6 %collective-permute-start.6 = (f32[544,128]{1,0:T(8,128)S(1)}, f32[544,128]{1,0:T(8,128)S(1)}, u32[]{:S(2)}, u32[]{:S(2)}) collective-permute-start(f32[544,128]{1,0:T(8,128)S(1)} %get-tuple-element.46), channel_id=1, source_target_pairs={{0,32},{32,0},{64,96},{96,64},{1,33},{33,1},{65,97},{97,65},{2,34}... | collective-permute-start | bytes 835592 | tf_op jit(solution)/shard_map/ppermute | solution.py:312
  40.4 25.9 %collective-permute-start.5 = (f32[576,128]{1,0:T(8,128)S(1)}, f32[576,128]{1,0:T(8,128)S(1)}, u32[]{:S(2)}, u32[]{:S(2)}) collective-permute-start(f32[576,128]{1,0:T(8,128)S(1)} %add_add_fusion.a_ref), channel_id=1, source_target_pairs={{0,128},{128,0},{1,129},{129,1},{2,130},{130,2},{3,131},{131,3},{4... | collective-permute-start | bytes 884744 | tf_op jit(solution)/shard_map/ppermute | solution.py:321
  46.6 32.0 %collective-permute-start.12 = (f32[544,128]{1,0:T(8,128)S(1)}, f32[544,128]{1,0:T(8,128)S(1)}, u32[]{:S(2)}, u32[]{:S(2)}) collective-permute-start(f32[544,128]{1,0:T(8,128)S(1)} %add_add_fusion.1.a_ref), channel_id=1, source_target_pairs={{0,128},{128,0},{1,129},{129,1},{2,130},{130,2},{3,131},{131,3},{4... | collective-permute-start | bytes 835592 | tf_op jit(solution)/shard_map/ppermute | solution.py:323
  66.9 9.0 %collective-permute-start.9 = (f32[512,128]{1,0:T(8,128)S(1)}, f32[512,128]{1,0:T(8,128)S(1)}, u32[]{:S(2)}, u32[]{:S(2)}) collective-permute-start(f32[512,128]{1,0:T(8,128)S(1)} %get-tuple-element.50.refs_0_), channel_id=1, source_target_pairs={{0,32},{32,0},{64,96},{96,64},{1,33},{33,1},{65,97},{97,65},{2,34}... | collective-permute-start | bytes 786440 | tf_op jit(solution)/shard_map/ppermute | solution.py:312
  67.0 11.5 %collective-permute-start.10 = (f32[512,128]{1,0:T(8,128)S(1)}, f32[512,128]{1,0:T(8,128)S(1)}, u32[]{:S(2)}, u32[]{:S(2)}) collective-permute-start(f32[512,128]{1,0:T(8,128)S(1)} %get-tuple-element.50.refs_0_), channel_id=1, source_target_pairs={{0,96},{32,64},{64,32},{96,0},{1,97},{33,65},{65,33},{97,1},{2,98}... | collective-permute-start | bytes 786440 | tf_op jit(solution)/shard_map/ppermute | solution.py:312
  67.4 11.2 %collective-permute-start.11 = (f32[512,128]{1,0:T(8,128)S(1)}, f32[512,128]{1,0:T(8,128)S(1)}, u32[]{:S(2)}, u32[]{:S(2)}) collective-permute-start(f32[512,128]{1,0:T(8,128)S(1)} %get-tuple-element.50.refs_0_), channel_id=1, source_target_pairs={{0,64},{32,96},{64,0},{96,32},{1,65},{33,97},{65,1},{97,33},{2,66}... | collective-permute-start | bytes 786440 | tf_op jit(solution)/shard_map/ppermute | solution.py:312
  71.1 7.5 %collective-permute-start.13 = (f32[32,128]{1,0:T(8,128)S(1)}, f32[32,128]{1,0:T(8,128)S(1)}, u32[]{:S(2)}, u32[]{:S(2)}) collective-permute-start(f32[32,128]{1,0:T(8,128)S(1)} %get-tuple-element.52.shared_ref), channel_id=1, source_target_pairs={{0,1},{32,34},{4,2},{2,3},{64,68},{8,4},{36,37},{68,70},{40,38},{6... | collective-permute-start | bytes 49160 | tf_op jit(solution)/shard_map/ppermute | solution.py:333
  76.0 7.1 %collective-permute-start.14 = (f32[32,128]{1,0:T(8,128)S(1)}, f32[32,128]{1,0:T(8,128)S(1)}, u32[]{:S(2)}, u32[]{:S(2)}) collective-permute-start(f32[32,128]{1,0:T(8,128)S(1)} %get-tuple-element.52.shared_ref), channel_id=1, source_target_pairs={{8,12},{0,16},{16,18},{48,52},{80,88},{32,56},{24,28},{64,92},{96,... | collective-permute-start | bytes 49160 | tf_op jit(solution)/shard_map/ppermute | solution.py:333
  84.3 6.6 %collective-permute-start.15 = (f32[544,128]{1,0:T(8,128)S(1)}, f32[544,128]{1,0:T(8,128)S(1)}, u32[]{:S(2)}, u32[]{:S(2)}) collective-permute-start(f32[544,128]{1,0:T(8,128)S(1)} %shard_map.79.refs_4_), channel_id=1, source_target_pairs={{0,32},{32,0},{64,96},{96,64},{1,33},{33,1},{65,97},{97,65},{2,34}... | collective-permute-start | bytes 835592 | tf_op jit(solution)/shard_map/ppermute | solution.py:312
  84.4 10.8 %collective-permute-start.16 = (f32[544,128]{1,0:T(8,128)S(1)}, f32[544,128]{1,0:T(8,128)S(1)}, u32[]{:S(2)}, u32[]{:S(2)}) collective-permute-start(f32[544,128]{1,0:T(8,128)S(1)} %shard_map.79.refs_4_), channel_id=1, source_target_pairs={{0,96},{32,64},{64,32},{96,0},{1,97},{33,65},{65,33},{97,1},{2,98}... | collective-permute-start | bytes 835592 | tf_op jit(solution)/shard_map/ppermute | solution.py:312
  84.5 10.7 %collective-permute-start.17 = (f32[544,128]{1,0:T(8,128)S(1)}, f32[544,128]{1,0:T(8,128)S(1)}, u32[]{:S(2)}, u32[]{:S(2)}) collective-permute-start(f32[544,128]{1,0:T(8,128)S(1)} %shard_map.79.refs_4_), channel_id=1, source_target_pairs={{0,64},{32,96},{64,0},{96,32},{1,65},{33,97},{65,1},{97,33},{2,66}... | collective-permute-start | bytes 835592 | tf_op jit(solution)/shard_map/ppermute | solution.py:312

commit v3 on v2

--- a/solution.py
+++ b/solution.py
@@ -12,6 +12,7 @@
 VM = pl.BlockSpec(memory_space=pltpu.VMEM)
 SM = pl.BlockSpec(memory_space=pltpu.SMEM)
 F32 = jnp.float32
+CHUNKS = ((0, 1), (1, 2), (3, 1))
 
 
 def grant(mib):
@@ -54,17 +55,12 @@
             packed_ref[b, pl.ds(8 * h + slot, 8, stride=16), :] = value[8 * b : 8 * b + 8, 128 * h : 128 * h + 128]
 
 
-def ends_kernel(x_ref, full_ref, lo_ref, hi_ref, mid_ref, packed_ref, sems):
+def ends_kernel(x_ref, lo_ref, hi_ref, mid_ref, packed_ref):
     lane = lane_id((128, 128))
-    copies = [pltpu.make_async_copy(x_ref.at[pl.ds(4 * k, 4)], full_ref.at[pl.ds(4 * k, 4)], sems.at[k]) for k in range(4)]
-    for copy in copies:
-        copy.start()
     for b in range(2):
         acc = jnp.zeros((128, 128), F32)
         for c in range(16):
-            if c % 8 == 0:
-                copies[2 * b + c // 8].wait()
-            block = full_ref[8 * b + c // 2, 8 * (c % 2) : 8 * (c % 2) + 8].reshape(128, 128)
+            block = x_ref[8 * b + c // 2, 8 * (c % 2) : 8 * (c % 2) + 8].reshape(128, 128)
             acc = jnp.where(lax.shift_right_logical(lane, 3) == c, pltpu.roll(block, (4 + 8 * c) % 128, 1), acc)
         packed_ref[b] = acc.T
     for slot, (out_ref, at) in enumerate(
@@ -125,28 +121,29 @@
     for target, out_ref in zip(partners(pos[0]), outs):
 
         def body(r, _, target=target, out_ref=out_ref):
-            p = 4 * target + 2 * chunk + r
+            p = 4 * target + CHUNKS[chunk][0] + r
             base = pl.multiple_of(272 * r, 16)
             for i in range(16):
                 out_ref[pl.ds(base + 16 * i, 16), :] = weight * step_row(u_ref, p, i, fac)
             out_ref[pl.ds(base + 256, 16), :] = edge_ref[pl.ds(pl.multiple_of(16 * p, 16), 16), :]
             return 0
 
-        lax.fori_loop(0, 2, body, 0)
-        if out_ref.shape[0] > 544:
-            out_ref[544:] = shared_ref[...]
+        lax.fori_loop(0, CHUNKS[chunk][1], body, 0)
+        if chunk == 0:
+            out_ref[272 * CHUNKS[0][1] :] = shared_ref[...]
 
 
 def surplus_rows(a_ref, b_ref, mat_ref, o_ref, packed_ref):
+    planes = a_ref.shape[0] // 272
     packed_ref[...] = jnp.zeros_like(packed_ref)
-    for n in range(2):
+    for n in range(planes):
         at = slice(272 * n + 256, 272 * n + 272)
         packed_ref[16 * n : 16 * n + 16] = a_ref[at] + b_ref[at]
     turned = packed_ref[...].T
     lane = lane_id((1, 128))
     edge = (lane < 2) | (lane > 125)
     ramp = lane.astype(F32) * (1.0 / 128.0)
-    for n in range(2):
+    for n in range(planes):
         for h in range(2):
             at = slice(272 * n + 128 * h, 272 * n + 128 * h + 128)
             ends = pltpu.roll(turned, 126 - 8 * (2 * n + h), 1)
@@ -154,41 +151,60 @@
             o_ref[256 * n + 128 * h : 256 * n + 128 * h + 128] = jnp.dot(
                 full, mat_ref[...], precision=lax.Precision.HIGHEST, preferred_element_type=F32
             )
-
-
-def surplus_kernel(a_ref, b_ref, mat_ref, o_ref, shared_ref, packed_ref):
-    shared_ref[...] = a_ref[544:] + b_ref[544:]
+    return 272 * planes, 256 * planes
+
+
+def surplus_kernel(a_ref, b_ref, mat_ref, o_ref, packed_ref):
     surplus_rows(a_ref, b_ref, mat_ref, o_ref, packed_ref)
 
 
 def surplus_fix_kernel(pos, table, a_ref, b_ref, mat_ref, shared_ref, *rest):
     got, (o_ref, packed_ref) = rest[:-2], rest[-2:]
-    surplus_rows(a_ref, b_ref, mat_ref, o_ref, packed_ref)
+    _, end = surplus_rows(a_ref, b_ref, mat_ref, o_ref, packed_ref)
     at = 32 * pos[0] + pos[1]
     fix = table[len(got), at] * shared_ref[...]
     for k, ref in enumerate(got):
         fix = fix + table[k, at] * ref[...]
-    o_ref[512:] = fix
-
-
-def last_kernel(pos, *refs):
-    pieces, (out_ref, packed_ref, turned_ref) = refs[:-3], refs[-3:]
-    fix = sum(ref[512:] for ref in pieces[4:])
+    o_ref[end:] = fix
+
+
+def write_planes(chunks, y, pieces, turned_ref, out_ref, block_ref, sems):
+    first = lane_id((1, 128)) == 0
+    start, count = CHUNKS[chunks[0]][0], sum(CHUNKS[c][1] for c in chunks)
+    copies = []
+    for t, target in enumerate(partners(y)):
+        turned = turned_ref[lax.shift_right_logical(target, 1)]
+        at = 0
+        for c, refs in zip(chunks, pieces):
+            for r in range(CHUNKS[c][1]):
+                for h in range(2):
+                    k = (2 * (4 * target + start + at) + h) & 15
+                    fixed = pltpu.roll(turned, (128 - 8 * k) & 127, 1)
+                    part = refs[t][256 * r + 128 * h : 256 * r + 128 * h + 128, :] + jnp.where(first, fixed, 0.0)
+                    block_ref[count * t + at, 8 * h : 8 * h + 8] = part.reshape(8, 16, 128)
+                at += 1
+        copy = pltpu.make_async_copy(
+            block_ref.at[pl.ds(count * t, count)], out_ref.at[pl.ds(4 * target + start, count)], sems.at[t]
+        )
+        copy.start()
+        copies.append(copy)
+    for copy in copies:
+        copy.wait()
+
+
+def early_kernel(pos, *refs):
+    pieces, (out_ref, turned_ref, packed_ref, block_ref, sems) = refs[:8], refs[8:]
+    fix = sum(ref[256 * CHUNKS[1][1] :] for ref in pieces[4:])
     for b in range(2):
         for h in range(2):
             packed_ref[b, pl.ds(8 * h, 8, stride=16), :] = fix[16 * h + 8 * b : 16 * h + 8 * b + 8]
         turned_ref[b] = packed_ref[b].T
-    first = lane_id((1, 128)) == 0
-    for chunk in range(2):
-        for target, src in zip(partners(pos[0]), pieces[4 * chunk : 4 * chunk + 4]):
-            turned = turned_ref[lax.shift_right_logical(target, 1)]
-            for r in range(2):
-                p = 4 * target + 2 * chunk + r
-                for h in range(2):
-                    k = (2 * p + h) & 15
-                    fixed = pltpu.roll(turned, (128 - 8 * k) & 127, 1)
-                    part = src[256 * r + 128 * h : 256 * r + 128 * h + 128, :] + jnp.where(first, fixed, 0.0)
-                    out_ref[p, 8 * h : 8 * h + 8] = part.reshape(8, 16, 128)
+    write_planes((0, 1), pos[0], (pieces[:4], pieces[4:]), turned_ref, out_ref, block_ref, sems)
+
+
+def last_kernel(pos, *refs):
+    pieces, (turned_ref, _, out_ref, block_ref, sems) = refs[:4], refs[4:]
+    write_planes((2,), pos[0], (pieces,), turned_ref, out_ref, block_ref, sems)
 
 
 def surplus_matrix():
@@ -269,12 +285,12 @@
     def struct(*shape):
         return jax.ShapeDtypeStruct(shape, F32)
 
-    full, lo, hi, mid = pl.pallas_call(
+    lo, hi, mid = pl.pallas_call(
         ends_kernel,
-        out_shape=(struct(*x.shape), struct(3, 16, 256), struct(2, 16, 256), struct(3, 16, 256)),
-        in_specs=[pl.BlockSpec(memory_space=pltpu.HBM)],
-        out_specs=(VM,) * 4,
-        scratch_shapes=[pltpu.VMEM((2, 128, 128), F32), pltpu.SemaphoreType.DMA((4,))],
+        out_shape=(struct(3, 16, 256), struct(2, 16, 256), struct(3, 16, 256)),
+        in_specs=[VM],
+        out_specs=(VM,) * 3,
+        scratch_shapes=[pltpu.VMEM((2, 128, 128), F32)],
         compiler_params=grant(4),
     )(x)
     left = lax.ppermute(hi, BRICK, up)
@@ -287,7 +303,7 @@
         out_specs=VM,
         compiler_params=grant(6),
         cost_estimate=cost,
-    )(levels, velocity, diffusivity, full)
+    )(levels, velocity, diffusivity, x)
     left, right = after((left, right), u)
     edges, shared = pl.pallas_call(
         layers_kernel,
@@ -301,7 +317,7 @@
     def second(c, value):
         return pl.pallas_call(
             functools.partial(second_kernel, c),
-            out_shape=(struct(544 if c else 576, 128),) * 4,
+            out_shape=(struct(272 * CHUNKS[c][1] + (0 if c else 32), 128),) * 4,
             in_specs=[SM] * 5 + [VM] * 3,
             out_specs=(VM,) * 4,
             compiler_params=grant(5),
@@ -311,44 +327,72 @@
     def to_others(values):
         return [lax.ppermute(value, "y", perm) for value, perm in zip(values, others)]
 
+    def surplus(kernel, out, *args, scalar=0):
+        return pl.pallas_call(
+            kernel,
+            out_shape=out,
+            in_specs=[SM] * scalar + [VM] * (len(args) - scalar),
+            out_specs=jax.tree.map(lambda _: VM, out),
+            scratch_shapes=[pltpu.VMEM((128, 128), F32)],
+            compiler_params=grant(3),
+        )(*args)
+
     matrix = jnp.asarray(surplus_matrix())
     rounds, table = tree_edges(n, 4)
-    parts0 = second(0, u)
-    got0 = to_others(parts0[1:])
-    parts1 = second(1, after(u, parts0[0]))
-    got1 = to_others(after(parts1[1:], got0[0]))
-    summed0 = parts0[0] + got0[0] + got0[1] + got0[2]
-    other0 = lax.ppermute(summed0, "zh", pair)
-    summed1 = parts1[0] + got1[0] + got1[1] + got1[2]
-    other1 = lax.ppermute(summed1, "zh", pair)
-    own0, shared = pl.pallas_call(
-        surplus_kernel,
-        out_shape=(struct(512, 128), struct(32, 128)),
-        in_specs=[VM] * 3,
-        out_specs=(VM,) * 2,
-        scratch_shapes=[pltpu.VMEM((128, 128), F32)],
-        compiler_params=grant(2),
-    )(summed0, after(other0, summed1), matrix)
+    sizes = [256 * count for _, count in CHUNKS]
+    value, gate, summed, partner = u, (), [], []
+    for c in range(3):
+        parts = second(c, value)
+        value = after(u, parts[0])
+        got = to_others(after(parts[1:], *gate))
+        gate = (got[0],)
+        summed.append(parts[0] + got[0] + got[1] + got[2])
+        partner.append(lax.ppermute(summed[c], "zh", pair))
+    shared = summed[0][-32:] + partner[0][-32:]
+    own0 = surplus(surplus_kernel, struct(sizes[0], 128), summed[0], after(partner[0], summed[2]), matrix)
     pieces0 = [own0] + to_others([own0] * 3)
     got = [lax.ppermute(shared, ("y",) + BRICK, r) for r in rounds]
-    own1 = pl.pallas_call(
+    own1 = surplus(
         surplus_fix_kernel,
-        out_shape=struct(544, 128),
-        in_specs=[SM] * 2 + [VM] * (4 + len(got)),
-        out_specs=VM,
-        scratch_shapes=[pltpu.VMEM((128, 128), F32)],
-        compiler_params=grant(2),
-    )(pos, jnp.asarray(table), summed1, after(other1, *pieces0), matrix, shared, *got)
-    pieces = pieces0 + [own1] + to_others([own1] * 3)
-
+        struct(sizes[1] + 32, 128),
+        pos,
+        jnp.asarray(table),
+        summed[1],
+        after(partner[1], *pieces0),
+        matrix,
+        shared,
+        *got,
+        scalar=2,
+    )
+    pieces1 = [own1] + to_others([own1] * 3)
+    own2 = surplus(surplus_kernel, struct(sizes[2], 128), summed[2], after(partner[2], own1), matrix)
+    pieces2 = [own2] + to_others([own2] * 3)
+
+    hbm = pl.BlockSpec(memory_space=pl.ANY)
+    whole = struct(16, 16, 16, 128)
+    early = CHUNKS[0][1] + CHUNKS[1][1]
+    out, turned = pl.pallas_call(
+        early_kernel,
+        out_shape=(whole, struct(2, 128, 128)),
+        in_specs=[SM] + [VM] * 8,
+        out_specs=(hbm, VM),
+        scratch_shapes=[
+            pltpu.VMEM((2, 128, 128), F32),
+            pltpu.VMEM((4 * early, 16, 16, 128), F32),
+            pltpu.SemaphoreType.DMA((4,)),
+        ],
+        compiler_params=grant(6),
+        cost_estimate=cost,
+    )(pos, *pieces0, *pieces1)
     return pl.pallas_call(
         last_kernel,
-        out_shape=struct(16, 16, 16, 128),
-        in_specs=[SM] + [VM] * len(pieces),
-        out_specs=VM,
-        scratch_shapes=[pltpu.VMEM((2, 128, 128), F32)] * 2,
-        compiler_params=grant(8),
-    )(pos, *pieces)
+        out_shape=whole,
+        in_specs=[SM] + [VM] * 5 + [hbm],
+        out_specs=hbm,
+        scratch_shapes=[pltpu.VMEM((4 * CHUNKS[2][1], 16, 16, 128), F32), pltpu.SemaphoreType.DMA((4,))],
+        input_output_aliases={6: 0},
+        compiler_params=grant(4),
+    )(pos, *pieces2, turned, out)
 
 
 def solution(mesh):

time: 98 us -> 87.1 us (0.89)
  the two profiles are of different devices: /device:TPU:4 before, /device:TPU:32 now
where the time goes in v3:
time: 87.1 us; the launch traced here: 87 us
  starting transfers between devices  52.8 us (61%)
  waiting for transfers between devices  17.4 us (20%)
  Pallas kernels  13.8 us (16%)
  local copies, waits for them, and re-layouts  1.65 us (2%)
  between operations  1.07 us (1%)
    ppermute x18, starting transfers between devices, to_others(): lax.ppermute(value, 'y', perm)  32.3 us
    ppermute x3, starting transfers between devices, local(): partner.append(lax.ppermute(summed[c], 'zh', pair))  16.1 us
    ppermute x18, waiting for transfers between devices, to_others(): lax.ppermute(value, 'y', perm)  9.12 us
    ppermute x3, waiting for transfers between devices, local(): partner.append(lax.ppermute(summed[c], 'zh', pair))  6.04 us
    pallas_call x3, Pallas kernels, second(): pl.pallas_call(functools.partial(second_kernel, c), out_shape=(struct(272...  3.68 us
    pallas_call x1, Pallas kernels, local(): pl.pallas_call(first_kernel, out_shape=struct(*x.shape), in_specs=[SM] *...  2.77 us
    ppermute x2, starting transfers between devices, local(): got = [lax.ppermute(shared, ('y',) + BRICK, r) for r in rounds]  2.57 us
    ppermute x2, waiting for transfers between devices, local(): got = [lax.ppermute(shared, ('y',) + BRICK, r) for r in rounds]  2.23 us
  transfers between devices with their start and end apart: 25, of which 9 were waited for; matrix products, arithmetic and copies ran while one was open for 0% of the time, Pallas kernels for 10%

profile of v3, /device:TPU:32, one launch (start us, length us, event | category | flops | bytes accessed | tf_op | source)
XLA Modules:
  0.0 87.0 jit_solution(11160976338596340758)
XLA Ops:
  0.0 1.6 %copy-done = f32[1,16,16,16,128]{4,3,2,1,0:T(8,128)S(1)} copy-done((f32[1,16,16,16,128]{4,3,2,1,0:T(8,128)S(1)}, f32[1,16,16,16,128]{4,3,2,1,0:T(8,128)}, u32[]{:S(2)}) %copy-start) | copy-done | bytes 2097176
  1.6 0.7 shard_map.74
  2.4 0.1 collective-permute-start
  2.5 1.7 %collective-permute-start.1 = (f32[3,16,256]{2,1,0:T(8,128)S(1)}, f32[3,16,256]{2,1,0:T(8,128)S(1)}, u32[]{:S(2)}, u32[]{:S(2)}) collective-permute-start(f32[3,16,256]{2,1,0:T(8,128)S(1)} %get-tuple-element.40.lo_ref), channel_id=1, source_target_pairs={{0,31},{1,0},{2,1},{3,2},{4,3},{5,4},{6,5},{7,6},{8,7},{9,8},{10,9... | collective-permute-start | bytes 147464 | tf_op jit(solution)/shard_map/ppermute | solution.py:297
  4.2 0.1 pad_add_fusion.pos
  5.0 2.8 %shard_map.73.u_ref = f32[16,16,16,128]{3,2,1,0:T(8,128)S(1)} custom-call(s32[1,4]{1,0:T(1,128)S(1)} %copy-done.3, f32[4]{0:T(128)S(1)} %copy-done.4, f32[4]{0:T(128)S(1)} %copy-done.5, f32[16,16,16,128]{3,2,1,0:T(8,128)S(1)} %bitcast.4), custom_call_target="tpu_custom_call" | custom-call | flops 10000000 | bytes 4194304 | tf_op jit(solution)/shard_map/pallas_call | solution.py:299
  7.7 0.0 collective-permute-done.left_ref
  7.8 1.0 %shard_map.75 = (f32[256,128]{1,0:T(8,128)S(1)}, f32[32,128]{1,0:T(8,128)S(1)}) custom-call(s32[1,4]{1,0:T(1,128)S(1)} %copy-done.3, f32[4]{0:T(128)S(1)} %copy-done.4, f32[4]{0:T(128)S(1)} %copy-done.5, s32[1]{0:T(128)S(6)} %copy.10.wgt, s32[2]{0:T(128)S(1)} %pad_add_fusion.pos, f32[3,16,256]{2,1,0:T(8,128)S(1)} %get-tuple-element.40.lo_ref, ...), custom_call_target="tpu_custom_call" | custom-call | tf_op jit(solution)/shard_map/pallas_call | solution.py:308
  8.8 1.0 %shard_map.76 = (f32[304,128]{1,0:T(8,128)S(1)}, f32[304,128]{1,0:T(8,128)S(1)}, f32[304,128]{1,0:T(8,128)S(1)}, f32[304,128]{1,0:T(8,128)S(1)}) custom-call(s32[1,4]{1,0:T(1,128)S(1)} %copy-done.3, f32[4]{0:T(128)S(1)} %copy-done.4, f32[4]{0:T(128)S(1)} %copy-done.5, s32[1]{0:T(128)S(6)} %copy.10.wgt, s32[2]{0:T(128)S(1)} %pad_add_fusion.pos, ...), custom_call_target="tpu_custom_call" | custom-call | flops 10000000 | bytes 4194304 | tf_op jit(solution)/shard_map/pallas_call | solution.py:318
  9.8 1.7 %collective-permute-start.2 = (f32[304,128]{1,0:T(8,128)S(1)}, f32[304,128]{1,0:T(8,128)S(1)}, u32[]{:S(2)}, u32[]{:S(2)}) collective-permute-start(f32[304,128]{1,0:T(8,128)S(1)} %get-tuple-element.61), channel_id=1, source_target_pairs={{0,32},{32,0},{64,96},{96,64},{1,33},{33,1},{65,97},{97,65},{2,34}... | collective-permute-start | bytes 466952 | tf_op jit(solution)/shard_map/ppermute | solution.py:328
  11.5 2.2 %collective-permute-start.11 = (f32[304,128]{1,0:T(8,128)S(1)}, f32[304,128]{1,0:T(8,128)S(1)}, u32[]{:S(2)}, u32[]{:S(2)}) collective-permute-start(f32[304,128]{1,0:T(8,128)S(1)} %get-tuple-element.68), channel_id=1, source_target_pairs={{0,96},{32,64},{64,32},{96,0},{1,97},{33,65},{65,33},{97,1},{2,98}... | collective-permute-start | bytes 466952 | tf_op jit(solution)/shard_map/ppermute | solution.py:328
  13.7 0.7 collective-permute-start.12
  14.4 1.7 %shard_map.77 = (f32[544,128]{1,0:T(8,128)S(1)}, f32[544,128]{1,0:T(8,128)S(1)}, f32[544,128]{1,0:T(8,128)S(1)}, f32[544,128]{1,0:T(8,128)S(1)}) custom-call(s32[1,4]{1,0:T(1,128)S(1)} %copy-done.3, f32[4]{0:T(128)S(1)} %copy-done.4, f32[4]{0:T(128)S(1)} %copy-done.5, s32[1]{0:T(128)S(6)} %copy.10.wgt, s32[2]{0:T(128)S(1)} %pad_add_fusion.pos, ...), custom_call_target="tpu_custom_call" | custom-call | flops 10000000 | bytes 4194304 | tf_op jit(solution)/shard_map/pallas_call | solution.py:318
  16.1 0.2 collective-permute-done.2
  16.3 2.0 %collective-permute-start.3 = (f32[544,128]{1,0:T(8,128)S(1)}, f32[544,128]{1,0:T(8,128)S(1)}, u32[]{:S(2)}, u32[]{:S(2)}) collective-permute-start(f32[544,128]{1,0:T(8,128)S(1)} %get-tuple-element.62), channel_id=1, source_target_pairs={{0,32},{32,0},{64,96},{96,64},{1,33},{33,1},{65,97},{97,65},{2,34}... | collective-permute-start | bytes 835592 | tf_op jit(solution)/shard_map/ppermute | solution.py:328
  18.3 2.0 %collective-permute-start.8 = (f32[544,128]{1,0:T(8,128)S(1)}, f32[544,128]{1,0:T(8,128)S(1)}, u32[]{:S(2)}, u32[]{:S(2)}) collective-permute-start(f32[544,128]{1,0:T(8,128)S(1)} %get-tuple-element.66), channel_id=1, source_target_pairs={{0,96},{32,64},{64,32},{96,0},{1,97},{33,65},{65,33},{97,1},{2,98}... | collective-permute-start | bytes 835592 | tf_op jit(solution)/shard_map/ppermute | solution.py:328
  20.4 0.9 %collective-permute-start.9 = (f32[544,128]{1,0:T(8,128)S(1)}, f32[544,128]{1,0:T(8,128)S(1)}, u32[]{:S(2)}, u32[]{:S(2)}) collective-permute-start(f32[544,128]{1,0:T(8,128)S(1)} %get-tuple-element.67), channel_id=1, source_target_pairs={{0,64},{32,96},{64,0},{96,32},{1,65},{33,97},{65,1},{97,33},{2,66}... | collective-permute-start | bytes 835592 | tf_op jit(solution)/shard_map/ppermute | solution.py:328
  21.2 1.0 %shard_map.78 = (f32[272,128]{1,0:T(8,128)S(1)}, f32[272,128]{1,0:T(8,128)S(1)}, f32[272,128]{1,0:T(8,128)S(1)}, f32[272,128]{1,0:T(8,128)S(1)}) custom-call(s32[1,4]{1,0:T(1,128)S(1)} %copy-done.3, f32[4]{0:T(128)S(1)} %copy-done.4, f32[4]{0:T(128)S(1)} %copy-done.5, s32[1]{0:T(128)S(6)} %copy.10.wgt, s32[2]{0:T(128)S(1)} %pad_add_fusion.pos, ...), custom_call_target="tpu_custom_call" | custom-call | flops 10000000 | bytes 4194304 | tf_op jit(solution)/shard_map/pallas_call | solution.py:318
  22.2 0.0 copy-start.6
  22.3 0.3 collective-permute-done.12
  22.6 6.0 %collective-permute-start.13 = (f32[304,128]{1,0:T(8,128)S(1)}, f32[304,128]{1,0:T(8,128)S(1)}, u32[]{:S(2)}, u32[]{:S(2)}) collective-permute-start(f32[304,128]{1,0:T(8,128)S(1)} %add_add_fusion.1.a_ref), channel_id=1, source_target_pairs={{0,128},{128,0},{1,129},{129,1},{2,130},{130,2},{3,131},{131,3},{4... | collective-permute-start | bytes 466952 | tf_op jit(solution)/shard_map/ppermute | solution.py:350
  28.6 0.6 collective-permute-start.4
  29.2 1.9 %collective-permute-start.5 = (f32[272,128]{1,0:T(8,128)S(1)}, f32[272,128]{1,0:T(8,128)S(1)}, u32[]{:S(2)}, u32[]{:S(2)}) collective-permute-start(f32[272,128]{1,0:T(8,128)S(1)} %get-tuple-element.64), channel_id=1, source_target_pairs={{0,96},{32,64},{64,32},{96,0},{1,97},{33,65},{65,33},{97,1},{2,98}... | collective-permute-start | bytes 417800 | tf_op jit(solution)/shard_map/ppermute | solution.py:328
  31.1 2.3 %collective-permute-done.8 = f32[544,128]{1,0:T(8,128)S(1)} collective-permute-done((f32[544,128]{1,0:T(8,128)S(1)}, f32[544,128]{1,0:T(8,128)S(1)}, u32[]{:S(2)}, u32[]{:S(2)}) %collective-permute-start.8) | collective-permute-done | bytes 278560 | tf_op jit(solution)/shard_map/ppermute | solution.py:328
  33.4 3.1 %collective-permute-start.6 = (f32[272,128]{1,0:T(8,128)S(1)}, f32[272,128]{1,0:T(8,128)S(1)}, u32[]{:S(2)}, u32[]{:S(2)}) collective-permute-start(f32[272,128]{1,0:T(8,128)S(1)} %get-tuple-element.65), channel_id=1, source_target_pairs={{0,64},{32,96},{64,0},{96,32},{1,65},{33,97},{65,1},{97,33},{2,66}... | collective-permute-start | bytes 417800 | tf_op jit(solution)/shard_map/ppermute | solution.py:328
  36.5 0.1 add_add_fusion.a_ref
  36.6 5.7 %collective-permute-start.10 = (f32[544,128]{1,0:T(8,128)S(1)}, f32[544,128]{1,0:T(8,128)S(1)}, u32[]{:S(2)}, u32[]{:S(2)}) collective-permute-start(f32[544,128]{1,0:T(8,128)S(1)} %add_add_fusion.a_ref), channel_id=1, source_target_pairs={{0,128},{128,0},{1,129},{129,1},{2,130},{130,2},{3,131},{131,3},{4... | collective-permute-start | bytes 835592 | tf_op jit(solution)/shard_map/ppermute | solution.py:350
  42.4 0.5 shard_map.79.refs_0_
  42.8 0.9 collective-permute-start.16
  43.7 3.3 %collective-permute-start.15 = (f32[256,128]{1,0:T(8,128)S(1)}, f32[256,128]{1,0:T(8,128)S(1)}, u32[]{:S(2)}, u32[]{:S(2)}) collective-permute-start(f32[256,128]{1,0:T(8,128)S(1)} %shard_map.79.refs_0_), channel_id=1, source_target_pairs={{0,96},{32,64},{64,32},{96,0},{1,97},{33,65},{65,33},{97,1},{2,98}... | collective-permute-start | bytes 393224 | tf_op jit(solution)/shard_map/ppermute | solution.py:328
  47.0 0.0 collective-permute-start.14
  47.0 0.7 collective-permute-start.18
  47.6 1.9 %collective-permute-done.16.refs_3_ = f32[256,128]{1,0:T(8,128)S(1)} collective-permute-done((f32[256,128]{1,0:T(8,128)S(1)}, f32[256,128]{1,0:T(8,128)S(1)}, u32[]{:S(2)}, u32[]{:S(2)}) %collective-permute-start.16) | collective-permute-done | bytes 131104 | tf_op jit(solution)/shard_map/ppermute | solution.py:328
  49.5 1.9 %collective-permute-start.17 = (f32[32,128]{1,0:T(8,128)S(1)}, f32[32,128]{1,0:T(8,128)S(1)}, u32[]{:S(2)}, u32[]{:S(2)}) collective-permute-start(f32[32,128]{1,0:T(8,128)S(1)} %slice_add_fusion.shared_ref), channel_id=1, source_target_pairs={{0,1},{32,34},{4,2},{2,3},{64,68},{8,4},{36,37},{68,70},{40,38},{6... | collective-permute-start | bytes 49160 | tf_op jit(solution)/shard_map/ppermute | solution.py:354
  51.4 1.5 %collective-permute-done.14.refs_1_ = f32[256,128]{1,0:T(8,128)S(1)} collective-permute-done((f32[256,128]{1,0:T(8,128)S(1)}, f32[256,128]{1,0:T(8,128)S(1)}, u32[]{:S(2)}, u32[]{:S(2)}) %collective-permute-start.14) | collective-permute-done | bytes 131104 | tf_op jit(solution)/shard_map/ppermute | solution.py:328
  52.9 2.2 %collective-permute-done.17.rest_0_ = f32[32,128]{1,0:T(8,128)S(1)} collective-permute-done((f32[32,128]{1,0:T(8,128)S(1)}, f32[32,128]{1,0:T(8,128)S(1)}, u32[]{:S(2)}, u32[]{:S(2)}) %collective-permute-start.17) | collective-permute-done | bytes 16416 | tf_op jit(solution)/shard_map/ppermute | solution.py:354
  55.1 1.2 %shard_map.80.refs_4_ = f32[544,128]{1,0:T(8,128)S(1)} custom-call(s32[2]{0:T(128)S(1)} %pad_add_fusion.pos, f32[3,128]{1,0:T(4,128)S(1)} %copy-done.6, f32[544,128]{1,0:T(8,128)S(1)} %add_add_fusion.a_ref, f32[544,128]{1,0:T(8,128)S(1)} %collective-permute-done.10.b_ref, f32[128,128]{1,0:T(8,128)S(1)} %copy-done.2, f32[32,128]{1,0:T(8,128)S(1)} %slice_add_fusion.shared_ref, ...), custom_call_target="tpu_custom_call" | custom-call | tf_op jit(solution)/shard_map/pallas_call | solution.py:331
  56.3 0.1 collective-permute-start.24
  56.4 8.2 %collective-permute-start.23 = (f32[544,128]{1,0:T(8,128)S(1)}, f32[544,128]{1,0:T(8,128)S(1)}, u32[]{:S(2)}, u32[]{:S(2)}) collective-permute-start(f32[544,128]{1,0:T(8,128)S(1)} %shard_map.80.refs_4_), channel_id=1, source_target_pairs={{0,96},{32,64},{64,32},{96,0},{1,97},{33,65},{65,33},{97,1},{2,98}... | collective-permute-start | bytes 835592 | tf_op jit(solution)/shard_map/ppermute | solution.py:328
  64.7 4.4 %collective-permute-start.7 = (f32[272,128]{1,0:T(8,128)S(1)}, f32[272,128]{1,0:T(8,128)S(1)}, u32[]{:S(2)}, u32[]{:S(2)}) collective-permute-start(f32[272,128]{1,0:T(8,128)S(1)} %add_add_fusion.2.a_ref), channel_id=1, source_target_pairs={{0,128},{128,0},{1,129},{129,1},{2,130},{130,2},{3,131},{131,3},{4... | collective-permute-start | bytes 417800 | tf_op jit(solution)/shard_map/ppermute | solution.py:350
  69.1 6.0 %collective-permute-done.7.b_ref = f32[272,128]{1,0:T(8,128)S(1)} collective-permute-done((f32[272,128]{1,0:T(8,128)S(1)}, f32[272,128]{1,0:T(8,128)S(1)}, u32[]{:S(2)}, u32[]{:S(2)}) %collective-permute-start.7) | collective-permute-done | bytes 139296 | tf_op jit(solution)/shard_map/ppermute | solution.py:350
  75.1 0.5 shard_map.81.refs_0_
  75.6 1.5 %collective-permute-start.21 = (f32[256,128]{1,0:T(8,128)S(1)}, f32[256,128]{1,0:T(8,128)S(1)}, u32[]{:S(2)}, u32[]{:S(2)}) collective-permute-start(f32[256,128]{1,0:T(8,128)S(1)} %shard_map.81.refs_0_), channel_id=1, source_target_pairs={{0,64},{32,96},{64,0},{96,32},{1,65},{33,97},{65,1},{97,33},{2,66}... | collective-permute-start | bytes 393224 | tf_op jit(solution)/shard_map/ppermute | solution.py:328
  77.1 3.2 %collective-permute-start.20 = (f32[256,128]{1,0:T(8,128)S(1)}, f32[256,128]{1,0:T(8,128)S(1)}, u32[]{:S(2)}, u32[]{:S(2)}) collective-permute-start(f32[256,128]{1,0:T(8,128)S(1)} %shard_map.81.refs_0_), channel_id=1, source_target_pairs={{0,96},{32,64},{64,32},{96,0},{1,97},{33,65},{65,33},{97,1},{2,98}... | collective-permute-start | bytes 393224 | tf_op jit(solution)/shard_map/ppermute | solution.py:328
  80.4 2.0 %shard_map.82 = (f32[16,16,16,128]{3,2,1,0:T(8,128)}, f32[2,128,128]{2,1,0:T(8,128)S(1)}) custom-call(s32[2]{0:T(128)S(1)} %pad_add_fusion.pos, f32[256,128]{1,0:T(8,128)S(1)} %shard_map.79.refs_0_, f32[256,128]{1,0:T(8,128)S(1)} %collective-permute-done.14.refs_1_, f32[256,128]{1,0:T(8,128)S(1)} %collective-permute-done.15.refs_2_, ...), custom_call_target="tpu_custom_call" | custom-call | flops 10000000 | bytes 4194304 | tf_op jit(solution)/shard_map/pallas_call | solution.py:374
  82.4 1.1 %collective-permute-done.20.refs_2_ = f32[256,128]{1,0:T(8,128)S(1)} collective-permute-done((f32[256,128]{1,0:T(8,128)S(1)}, f32[256,128]{1,0:T(8,128)S(1)}, u32[]{:S(2)}, u32[]{:S(2)}) %collective-permute-start.20) | collective-permute-done | bytes 131104 | tf_op jit(solution)/shard_map/ppermute | solution.py:328
  83.6 1.8 %collective-permute-done.19.refs_1_ = f32[256,128]{1,0:T(8,128)S(1)} collective-permute-done((f32[256,128]{1,0:T(8,128)S(1)}, f32[256,128]{1,0:T(8,128)S(1)}, u32[]{:S(2)}, u32[]{:S(2)}) %collective-permute-start.19) | collective-permute-done | bytes 131104 | tf_op jit(solution)/shard_map/ppermute | solution.py:328
  85.4 1.5 %shard_map.83 = f32[16,16,16,128]{3,2,1,0:T(8,128)} custom-call(s32[2]{0:T(128)S(1)} %pad_add_fusion.pos, f32[256,128]{1,0:T(8,128)S(1)} %shard_map.81.refs_0_, f32[256,128]{1,0:T(8,128)S(1)} %collective-permute-done.19.refs_1_, f32[256,128]{1,0:T(8,128)S(1)} %collective-permute-done.20.refs_2_, ...), custom_call_target="tpu_custom_call", output_to_operand_aliasing={{}: (6, {})} | custom-call | tf_op jit(solution)/shard_map/pallas_call | solution.py:387
  (32 shorter events, 0.2 us)
Async XLA Ops:
  0.0 4.9 %copy-start.5 = (f32[4]{0:T(128)S(1)}, f32[4]{0:T(128)}, u32[]{:S(2)}) copy-start(f32[4]{0:T(128)} %dif.9) | copy-start | bytes 52
  0.0 4.9 %copy-start.4 = (f32[4]{0:T(128)S(1)}, f32[4]{0:T(128)}, u32[]{:S(2)}) copy-start(f32[4]{0:T(128)} %vel.9) | copy-start | bytes 52
  0.0 4.9 %copy-start.3 = (s32[1,4]{1,0:T(1,128)S(1)}, s32[1,4]{1,0:T(1,128)}, u32[]{:S(2)}) copy-start(s32[1,4]{1,0:T(1,128)} %lev.9) | copy-start | bytes 52
  0.0 1.6 %copy-start = (f32[1,16,16,16,128]{4,3,2,1,0:T(8,128)S(1)}, f32[1,16,16,16,128]{4,3,2,1,0:T(8,128)}, u32[]{:S(2)}) copy-start(f32[1,16,16,16,128]{4,3,2,1,0:T(8,128)} %param.7) | copy-start | bytes 6291460
  1.6 3.3 %copy-start.1 = (f32[1,16,16,16,128]{4,3,2,1,0:T(8,128)S(1)}, f32[1,16,16,16,128]{4,3,2,1,0:T(8,128)}, u32[]{:S(2)}) copy-start(f32[1,16,16,16,128]{4,3,2,1,0:T(8,128)} %param.7) | copy-start | bytes 6291460
  2.4 5.4 %collective-permute-start = (f32[2,16,256]{2,1,0:T(8,128)S(1)}, f32[2,16,256]{2,1,0:T(8,128)S(1)}, u32[]{:S(2)}, u32[]{:S(2)}) collective-permute-start(f32[2,16,256]{2,1,0:T(8,128)S(1)} %get-tuple-element.41.hi_ref), channel_id=1, source_target_pairs={{0,1},{1,2},{2,3},{3,4},{4,5},{5,6},{6,7},{7,8},{8,9},{9,10},{10,1... | collective-permute-start | bytes 98312 | tf_op jit(solution)/shard_map/ppermute | solution.py:296
  2.5 5.3 %collective-permute-start.1 = (f32[3,16,256]{2,1,0:T(8,128)S(1)}, f32[3,16,256]{2,1,0:T(8,128)S(1)}, u32[]{:S(2)}, u32[]{:S(2)}) collective-permute-start(f32[3,16,256]{2,1,0:T(8,128)S(1)} %get-tuple-element.40.lo_ref), channel_id=1, source_target_pairs={{0,31},{1,0},{2,1},{3,2},{4,3},{5,4},{6,5},{7,6},{8,7},{9,8},{10,9... | collective-permute-start | bytes 147464 | tf_op jit(solution)/shard_map/ppermute | solution.py:297
  9.8 6.5 %collective-permute-start.2 = (f32[304,128]{1,0:T(8,128)S(1)}, f32[304,128]{1,0:T(8,128)S(1)}, u32[]{:S(2)}, u32[]{:S(2)}) collective-permute-start(f32[304,128]{1,0:T(8,128)S(1)} %get-tuple-element.61), channel_id=1, source_target_pairs={{0,32},{32,0},{64,96},{96,64},{1,33},{33,1},{65,97},{97,65},{2,34}... | collective-permute-start | bytes 466952 | tf_op jit(solution)/shard_map/ppermute | solution.py:328
  11.5 10.8 %collective-permute-start.11 = (f32[304,128]{1,0:T(8,128)S(1)}, f32[304,128]{1,0:T(8,128)S(1)}, u32[]{:S(2)}, u32[]{:S(2)}) collective-permute-start(f32[304,128]{1,0:T(8,128)S(1)} %get-tuple-element.68), channel_id=1, source_target_pairs={{0,96},{32,64},{64,32},{96,0},{1,97},{33,65},{65,33},{97,1},{2,98}... | collective-permute-start | bytes 466952 | tf_op jit(solution)/shard_map/ppermute | solution.py:328
  13.7 8.9 %collective-permute-start.12 = (f32[304,128]{1,0:T(8,128)S(1)}, f32[304,128]{1,0:T(8,128)S(1)}, u32[]{:S(2)}, u32[]{:S(2)}) collective-permute-start(f32[304,128]{1,0:T(8,128)S(1)} %get-tuple-element.69), channel_id=1, source_target_pairs={{0,64},{32,96},{64,0},{96,32},{1,65},{33,97},{65,1},{97,33},{2,66}... | collective-permute-start | bytes 466952 | tf_op jit(solution)/shard_map/ppermute | solution.py:328
  16.3 12.3 %collective-permute-start.3 = (f32[544,128]{1,0:T(8,128)S(1)}, f32[544,128]{1,0:T(8,128)S(1)}, u32[]{:S(2)}, u32[]{:S(2)}) collective-permute-start(f32[544,128]{1,0:T(8,128)S(1)} %get-tuple-element.62), channel_id=1, source_target_pairs={{0,32},{32,0},{64,96},{96,64},{1,33},{33,1},{65,97},{97,65},{2,34}... | collective-permute-start | bytes 835592 | tf_op jit(solution)/shard_map/ppermute | solution.py:328
  18.3 15.1 %collective-permute-start.8 = (f32[544,128]{1,0:T(8,128)S(1)}, f32[544,128]{1,0:T(8,128)S(1)}, u32[]{:S(2)}, u32[]{:S(2)}) collective-permute-start(f32[544,128]{1,0:T(8,128)S(1)} %get-tuple-element.66), channel_id=1, source_target_pairs={{0,96},{32,64},{64,32},{96,0},{1,97},{33,65},{65,33},{97,1},{2,98}... | collective-permute-start | bytes 835592 | tf_op jit(solution)/shard_map/ppermute | solution.py:328
  20.4 16.1 %collective-permute-start.9 = (f32[544,128]{1,0:T(8,128)S(1)}, f32[544,128]{1,0:T(8,128)S(1)}, u32[]{:S(2)}, u32[]{:S(2)}) collective-permute-start(f32[544,128]{1,0:T(8,128)S(1)} %get-tuple-element.67), channel_id=1, source_target_pairs={{0,64},{32,96},{64,0},{96,32},{1,65},{33,97},{65,1},{97,33},{2,66}... | collective-permute-start | bytes 835592 | tf_op jit(solution)/shard_map/ppermute | solution.py:328
  21.2 21.1 %copy-start.2 = (f32[128,128]{1,0:T(8,128)S(1)}, f32[128,128]{1,0:T(8,128)}, u32[]{:S(2)}) copy-start(f32[128,128]{1,0:T(8,128)} %constant.23.clone.mat_ref) | copy-start | bytes 196612
  22.2 32.9 %copy-start.6 = (f32[3,128]{1,0:T(4,128)S(1)}, f32[3,128]{1,0:T(4,128)}, u32[]{:S(2)}) copy-start(f32[3,128]{1,0:T(4,128)} %constant.24.clone.table) | copy-start | bytes 4612
  22.6 19.8 %collective-permute-start.13 = (f32[304,128]{1,0:T(8,128)S(1)}, f32[304,128]{1,0:T(8,128)S(1)}, u32[]{:S(2)}, u32[]{:S(2)}) collective-permute-start(f32[304,128]{1,0:T(8,128)S(1)} %add_add_fusion.1.a_ref), channel_id=1, source_target_pairs={{0,128},{128,0},{1,129},{129,1},{2,130},{130,2},{3,131},{131,3},{4... | collective-permute-start | bytes 466952 | tf_op jit(solution)/shard_map/ppermute | solution.py:350
  28.6 13.7 %collective-permute-start.4 = (f32[272,128]{1,0:T(8,128)S(1)}, f32[272,128]{1,0:T(8,128)S(1)}, u32[]{:S(2)}, u32[]{:S(2)}) collective-permute-start(f32[272,128]{1,0:T(8,128)S(1)} %get-tuple-element.63), channel_id=1, source_target_pairs={{0,32},{32,0},{64,96},{96,64},{1,33},{33,1},{65,97},{97,65},{2,34}... | collective-permute-start | bytes 417800 | tf_op jit(solution)/shard_map/ppermute | solution.py:328
  29.2 13.1 %collective-permute-start.5 = (f32[272,128]{1,0:T(8,128)S(1)}, f32[272,128]{1,0:T(8,128)S(1)}, u32[]{:S(2)}, u32[]{:S(2)}) collective-permute-start(f32[272,128]{1,0:T(8,128)S(1)} %get-tuple-element.64), channel_id=1, source_target_pairs={{0,96},{32,64},{64,32},{96,0},{1,97},{33,65},{65,33},{97,1},{2,98}... | collective-permute-start | bytes 417800 | tf_op jit(solution)/shard_map/ppermute | solution.py:328
  33.4 8.8 %collective-permute-start.6 = (f32[272,128]{1,0:T(8,128)S(1)}, f32[272,128]{1,0:T(8,128)S(1)}, u32[]{:S(2)}, u32[]{:S(2)}) collective-permute-start(f32[272,128]{1,0:T(8,128)S(1)} %get-tuple-element.65), channel_id=1, source_target_pairs={{0,64},{32,96},{64,0},{96,32},{1,65},{33,97},{65,1},{97,33},{2,66}... | collective-permute-start | bytes 417800 | tf_op jit(solution)/shard_map/ppermute | solution.py:328
  36.6 16.3 %collective-permute-start.10 = (f32[544,128]{1,0:T(8,128)S(1)}, f32[544,128]{1,0:T(8,128)S(1)}, u32[]{:S(2)}, u32[]{:S(2)}) collective-permute-start(f32[544,128]{1,0:T(8,128)S(1)} %add_add_fusion.a_ref), channel_id=1, source_target_pairs={{0,128},{128,0},{1,129},{129,1},{2,130},{130,2},{3,131},{131,3},{4... | collective-permute-start | bytes 835592 | tf_op jit(solution)/shard_map/ppermute | solution.py:350
  42.8 6.7 %collective-permute-start.16 = (f32[256,128]{1,0:T(8,128)S(1)}, f32[256,128]{1,0:T(8,128)S(1)}, u32[]{:S(2)}, u32[]{:S(2)}) collective-permute-start(f32[256,128]{1,0:T(8,128)S(1)} %shard_map.79.refs_0_), channel_id=1, source_target_pairs={{0,64},{32,96},{64,0},{96,32},{1,65},{33,97},{65,1},{97,33},{2,66}... | collective-permute-start | bytes 393224 | tf_op jit(solution)/shard_map/ppermute | solution.py:328
  43.7 7.7 %collective-permute-start.15 = (f32[256,128]{1,0:T(8,128)S(1)}, f32[256,128]{1,0:T(8,128)S(1)}, u32[]{:S(2)}, u32[]{:S(2)}) collective-permute-start(f32[256,128]{1,0:T(8,128)S(1)} %shard_map.79.refs_0_), channel_id=1, source_target_pairs={{0,96},{32,64},{64,32},{96,0},{1,97},{33,65},{65,33},{97,1},{2,98}... | collective-permute-start | bytes 393224 | tf_op jit(solution)/shard_map/ppermute | solution.py:328
  47.0 5.9 %collective-permute-start.14 = (f32[256,128]{1,0:T(8,128)S(1)}, f32[256,128]{1,0:T(8,128)S(1)}, u32[]{:S(2)}, u32[]{:S(2)}) collective-permute-start(f32[256,128]{1,0:T(8,128)S(1)} %shard_map.79.refs_0_), channel_id=1, source_target_pairs={{0,32},{32,0},{64,96},{96,64},{1,33},{33,1},{65,97},{97,65},{2,34}... | collective-permute-start | bytes 393224 | tf_op jit(solution)/shard_map/ppermute | solution.py:328
  47.0 5.9 %collective-permute-start.18 = (f32[32,128]{1,0:T(8,128)S(1)}, f32[32,128]{1,0:T(8,128)S(1)}, u32[]{:S(2)}, u32[]{:S(2)}) collective-permute-start(f32[32,128]{1,0:T(8,128)S(1)} %slice_add_fusion.shared_ref), channel_id=1, source_target_pairs={{8,12},{0,16},{16,18},{48,52},{80,88},{32,56},{24,28},{64,92},{96,... | collective-permute-start | bytes 49160 | tf_op jit(solution)/shard_map/ppermute | solution.py:354
  49.5 5.6 %collective-permute-start.17 = (f32[32,128]{1,0:T(8,128)S(1)}, f32[32,128]{1,0:T(8,128)S(1)}, u32[]{:S(2)}, u32[]{:S(2)}) collective-permute-start(f32[32,128]{1,0:T(8,128)S(1)} %slice_add_fusion.shared_ref), channel_id=1, source_target_pairs={{0,1},{32,34},{4,2},{2,3},{64,68},{8,4},{36,37},{68,70},{40,38},{6... | collective-permute-start | bytes 49160 | tf_op jit(solution)/shard_map/ppermute | solution.py:354
  56.3 24.1 %collective-permute-start.24 = (f32[544,128]{1,0:T(8,128)S(1)}, f32[544,128]{1,0:T(8,128)S(1)}, u32[]{:S(2)}, u32[]{:S(2)}) collective-permute-start(f32[544,128]{1,0:T(8,128)S(1)} %shard_map.80.refs_4_), channel_id=1, source_target_pairs={{0,64},{32,96},{64,0},{96,32},{1,65},{33,97},{65,1},{97,33},{2,66}... | collective-permute-start | bytes 835592 | tf_op jit(solution)/shard_map/ppermute | solution.py:328
  56.4 24.0 %collective-permute-start.23 = (f32[544,128]{1,0:T(8,128)S(1)}, f32[544,128]{1,0:T(8,128)S(1)}, u32[]{:S(2)}, u32[]{:S(2)}) collective-permute-start(f32[544,128]{1,0:T(8,128)S(1)} %shard_map.80.refs_4_), channel_id=1, source_target_pairs={{0,96},{32,64},{64,32},{96,0},{1,97},{33,65},{65,33},{97,1},{2,98}... | collective-permute-start | bytes 835592 | tf_op jit(solution)/shard_map/ppermute | solution.py:328
  64.6 15.7 %collective-permute-start.22 = (f32[544,128]{1,0:T(8,128)S(1)}, f32[544,128]{1,0:T(8,128)S(1)}, u32[]{:S(2)}, u32[]{:S(2)}) collective-permute-start(f32[544,128]{1,0:T(8,128)S(1)} %shard_map.80.refs_4_), channel_id=1, source_target_pairs={{0,32},{32,0},{64,96},{96,64},{1,33},{33,1},{65,97},{97,65},{2,34}... | collective-permute-start | bytes 835592 | tf_op jit(solution)/shard_map/ppermute | solution.py:328
  64.7 10.5 %collective-permute-start.7 = (f32[272,128]{1,0:T(8,128)S(1)}, f32[272,128]{1,0:T(8,128)S(1)}, u32[]{:S(2)}, u32[]{:S(2)}) collective-permute-start(f32[272,128]{1,0:T(8,128)S(1)} %add_add_fusion.2.a_ref), channel_id=1, source_target_pairs={{0,128},{128,0},{1,129},{129,1},{2,130},{130,2},{3,131},{131,3},{4... | collective-permute-start | bytes 417800 | tf_op jit(solution)/shard_map/ppermute | solution.py:350
  75.6 6.8 %collective-permute-start.21 = (f32[256,128]{1,0:T(8,128)S(1)}, f32[256,128]{1,0:T(8,128)S(1)}, u32[]{:S(2)}, u32[]{:S(2)}) collective-permute-start(f32[256,128]{1,0:T(8,128)S(1)} %shard_map.81.refs_0_), channel_id=1, source_target_pairs={{0,64},{32,96},{64,0},{96,32},{1,65},{33,97},{65,1},{97,33},{2,66}... | collective-permute-start | bytes 393224 | tf_op jit(solution)/shard_map/ppermute | solution.py:328
  77.1 6.4 %collective-permute-start.20 = (f32[256,128]{1,0:T(8,128)S(1)}, f32[256,128]{1,0:T(8,128)S(1)}, u32[]{:S(2)}, u32[]{:S(2)}) collective-permute-start(f32[256,128]{1,0:T(8,128)S(1)} %shard_map.81.refs_0_), channel_id=1, source_target_pairs={{0,96},{32,64},{64,32},{96,0},{1,97},{33,65},{65,33},{97,1},{2,98}... | collective-permute-start | bytes 393224 | tf_op jit(solution)/shard_map/ppermute | solution.py:328
  80.4 5.0 %collective-permute-start.19 = (f32[256,128]{1,0:T(8,128)S(1)}, f32[256,128]{1,0:T(8,128)S(1)}, u32[]{:S(2)}, u32[]{:S(2)}) collective-permute-start(f32[256,128]{1,0:T(8,128)S(1)} %shard_map.81.refs_0_), channel_id=1, source_target_pairs={{0,32},{32,0},{64,96},{96,64},{1,33},{33,1},{65,97},{97,65},{2,34}... | collective-permute-start | bytes 393224 | tf_op jit(solution)/shard_map/ppermute | solution.py:328

commit v4 on v3

--- a/solution.py
+++ b/solution.py
@@ -12,7 +12,7 @@
 VM = pl.BlockSpec(memory_space=pltpu.VMEM)
 SM = pl.BlockSpec(memory_space=pltpu.SMEM)
 F32 = jnp.float32
-CHUNKS = ((0, 1), (1, 2), (3, 1))
+CHUNKS = ((0, 1), (1, 1), (2, 2))
 
 
 def grant(mib):
@@ -133,78 +133,68 @@
             out_ref[272 * CHUNKS[0][1] :] = shared_ref[...]
 
 
-def surplus_rows(a_ref, b_ref, mat_ref, o_ref, packed_ref):
-    planes = a_ref.shape[0] // 272
-    packed_ref[...] = jnp.zeros_like(packed_ref)
+def surplus_rows(planes, a_ref, b_ref, mat_ref, o_ref, at, packed_ref):
     for n in range(planes):
-        at = slice(272 * n + 256, 272 * n + 272)
-        packed_ref[16 * n : 16 * n + 16] = a_ref[at] + b_ref[at]
+        rows = slice(272 * n + 256, 272 * n + 272)
+        packed_ref[16 * n : 16 * n + 16] = a_ref[rows] + b_ref[rows]
     turned = packed_ref[...].T
     lane = lane_id((1, 128))
     edge = (lane < 2) | (lane > 125)
     ramp = lane.astype(F32) * (1.0 / 128.0)
     for n in range(planes):
         for h in range(2):
-            at = slice(272 * n + 128 * h, 272 * n + 128 * h + 128)
+            rows = slice(272 * n + 128 * h, 272 * n + 128 * h + 128)
             ends = pltpu.roll(turned, 126 - 8 * (2 * n + h), 1)
-            full = jnp.where(edge, ends, a_ref[at] + b_ref[at]) - ramp * ends[:, 2:3]
-            o_ref[256 * n + 128 * h : 256 * n + 128 * h + 128] = jnp.dot(
+            full = jnp.where(edge, ends, a_ref[rows] + b_ref[rows]) - ramp * ends[:, 2:3]
+            o_ref[at + 256 * n + 128 * h : at + 256 * n + 128 * h + 128] = jnp.dot(
                 full, mat_ref[...], precision=lax.Precision.HIGHEST, preferred_element_type=F32
             )
-    return 272 * planes, 256 * planes
-
-
-def surplus_kernel(a_ref, b_ref, mat_ref, o_ref, packed_ref):
-    surplus_rows(a_ref, b_ref, mat_ref, o_ref, packed_ref)
+
+
+def surplus_pair_kernel(a_ref, b_ref, c_ref, d_ref, mat_ref, o_ref, packed_ref):
+    packed_ref[...] = jnp.zeros_like(packed_ref)
+    surplus_rows(1, a_ref, b_ref, mat_ref, o_ref, 0, packed_ref)
+    surplus_rows(1, c_ref, d_ref, mat_ref, o_ref, 256, packed_ref)
 
 
 def surplus_fix_kernel(pos, table, a_ref, b_ref, mat_ref, shared_ref, *rest):
     got, (o_ref, packed_ref) = rest[:-2], rest[-2:]
-    _, end = surplus_rows(a_ref, b_ref, mat_ref, o_ref, packed_ref)
+    packed_ref[...] = jnp.zeros_like(packed_ref)
+    surplus_rows(2, a_ref, b_ref, mat_ref, o_ref, 0, packed_ref)
     at = 32 * pos[0] + pos[1]
     fix = table[len(got), at] * shared_ref[...]
     for k, ref in enumerate(got):
         fix = fix + table[k, at] * ref[...]
-    o_ref[end:] = fix
-
-
-def write_planes(chunks, y, pieces, turned_ref, out_ref, block_ref, sems):
-    first = lane_id((1, 128)) == 0
-    start, count = CHUNKS[chunks[0]][0], sum(CHUNKS[c][1] for c in chunks)
-    copies = []
-    for t, target in enumerate(partners(y)):
-        turned = turned_ref[lax.shift_right_logical(target, 1)]
-        at = 0
-        for c, refs in zip(chunks, pieces):
-            for r in range(CHUNKS[c][1]):
-                for h in range(2):
-                    k = (2 * (4 * target + start + at) + h) & 15
-                    fixed = pltpu.roll(turned, (128 - 8 * k) & 127, 1)
-                    part = refs[t][256 * r + 128 * h : 256 * r + 128 * h + 128, :] + jnp.where(first, fixed, 0.0)
-                    block_ref[count * t + at, 8 * h : 8 * h + 8] = part.reshape(8, 16, 128)
-                at += 1
-        copy = pltpu.make_async_copy(
-            block_ref.at[pl.ds(count * t, count)], out_ref.at[pl.ds(4 * target + start, count)], sems.at[t]
-        )
-        copy.start()
-        copies.append(copy)
-    for copy in copies:
-        copy.wait()
-
-
-def early_kernel(pos, *refs):
-    pieces, (out_ref, turned_ref, packed_ref, block_ref, sems) = refs[:8], refs[8:]
-    fix = sum(ref[256 * CHUNKS[1][1] :] for ref in pieces[4:])
+    o_ref[512:] = fix
+
+
+def last_kernel(pos, *refs):
+    pieces, (out_ref, packed_ref, turned_ref, block_ref, sems) = (refs[:4], refs[4:8]), refs[8:]
+    fix = sum(ref[512:] for ref in pieces[1])
     for b in range(2):
         for h in range(2):
             packed_ref[b, pl.ds(8 * h, 8, stride=16), :] = fix[16 * h + 8 * b : 16 * h + 8 * b + 8]
         turned_ref[b] = packed_ref[b].T
-    write_planes((0, 1), pos[0], (pieces[:4], pieces[4:]), turned_ref, out_ref, block_ref, sems)
-
-
-def last_kernel(pos, *refs):
-    pieces, (turned_ref, _, out_ref, block_ref, sems) = refs[:4], refs[4:]
-    write_planes((2,), pos[0], (pieces,), turned_ref, out_ref, block_ref, sems)
+    first = lane_id((1, 128)) == 0
+    copies = []
+    for half in range(2):
+        for t, target in enumerate(partners(pos[0])):
+            turned = turned_ref[lax.shift_right_logical(target, 1)]
+            at = 8 * half + 2 * t
+            for r in range(2):
+                for h in range(2):
+                    k = (2 * (4 * target + 2 * half + r) + h) & 15
+                    fixed = pltpu.roll(turned, (128 - 8 * k) & 127, 1)
+                    rows = slice(256 * r + 128 * h, 256 * r + 128 * h + 128)
+                    part = pieces[half][t][rows, :] + jnp.where(first, fixed, 0.0)
+                    block_ref[at + r, 8 * h : 8 * h + 8] = part.reshape(8, 16, 128)
+            copy = pltpu.make_async_copy(
+                block_ref.at[pl.ds(at, 2)], out_ref.at[pl.ds(4 * target + 2 * half, 2)], sems.at[4 * half + t]
+            )
+            copy.start()
+            copies.append(copy)
+    for copy in copies:
+        copy.wait()
 
 
 def surplus_matrix():
@@ -339,7 +329,6 @@
 
     matrix = jnp.asarray(surplus_matrix())
     rounds, table = tree_edges(n, 4)
-    sizes = [256 * count for _, count in CHUNKS]
     value, gate, summed, partner = u, (), [], []
     for c in range(3):
         parts = second(c, value)
@@ -349,50 +338,43 @@
         summed.append(parts[0] + got[0] + got[1] + got[2])
         partner.append(lax.ppermute(summed[c], "zh", pair))
     shared = summed[0][-32:] + partner[0][-32:]
-    own0 = surplus(surplus_kernel, struct(sizes[0], 128), summed[0], after(partner[0], summed[2]), matrix)
+    got = [lax.ppermute(shared, ("y",) + BRICK, r) for r in rounds]
+    own0 = surplus(
+        surplus_pair_kernel,
+        struct(512, 128),
+        summed[0],
+        partner[0],
+        summed[1],
+        after(partner[1], summed[2]),
+        matrix,
+    )
     pieces0 = [own0] + to_others([own0] * 3)
-    got = [lax.ppermute(shared, ("y",) + BRICK, r) for r in rounds]
     own1 = surplus(
         surplus_fix_kernel,
-        struct(sizes[1] + 32, 128),
+        struct(544, 128),
         pos,
         jnp.asarray(table),
-        summed[1],
-        after(partner[1], *pieces0),
+        summed[2],
+        after(partner[2], *pieces0),
         matrix,
         shared,
         *got,
         scalar=2,
     )
     pieces1 = [own1] + to_others([own1] * 3)
-    own2 = surplus(surplus_kernel, struct(sizes[2], 128), summed[2], after(partner[2], own1), matrix)
-    pieces2 = [own2] + to_others([own2] * 3)
-
-    hbm = pl.BlockSpec(memory_space=pl.ANY)
-    whole = struct(16, 16, 16, 128)
-    early = CHUNKS[0][1] + CHUNKS[1][1]
-    out, turned = pl.pallas_call(
-        early_kernel,
-        out_shape=(whole, struct(2, 128, 128)),
+    return pl.pallas_call(
+        last_kernel,
+        out_shape=struct(16, 16, 16, 128),
         in_specs=[SM] + [VM] * 8,
-        out_specs=(hbm, VM),
+        out_specs=pl.BlockSpec(memory_space=pl.ANY),
         scratch_shapes=[
             pltpu.VMEM((2, 128, 128), F32),
-            pltpu.VMEM((4 * early, 16, 16, 128), F32),
-            pltpu.SemaphoreType.DMA((4,)),
+            pltpu.VMEM((2, 128, 128), F32),
+            pltpu.VMEM((16, 16, 16, 128), F32),
+            pltpu.SemaphoreType.DMA((8,)),
         ],
         compiler_params=grant(6),
-        cost_estimate=cost,
     )(pos, *pieces0, *pieces1)
-    return pl.pallas_call(
-        last_kernel,
-        out_shape=whole,
-        in_specs=[SM] + [VM] * 5 + [hbm],
-        out_specs=hbm,
-        scratch_shapes=[pltpu.VMEM((4 * CHUNKS[2][1], 16, 16, 128), F32), pltpu.SemaphoreType.DMA((4,))],
-        input_output_aliases={6: 0},
-        compiler_params=grant(4),
-    )(pos, *pieces2, turned, out)
 
 
 def solution(mesh):

time: 87.1 us -> 85.8 us (0.985)
  the two profiles are of different devices: /device:TPU:32 before, /device:TPU:68 now
where the time goes in v4:
time: 85.8 us; the launch traced here: 85.6 us
  starting transfers between devices  41.7 us (49%)
  waiting for transfers between devices  28.8 us (34%)
  Pallas kernels  12.3 us (14%)
  local copies, waits for them, and re-layouts  1.65 us (2%)
  between operations  1.01 us (1%)
    ppermute x15, waiting for transfers between devices, to_others(): lax.ppermute(value, 'y', perm)  24.8 us
    ppermute x15, starting transfers between devices, to_others(): lax.ppermute(value, 'y', perm)  22.7 us
    ppermute x3, starting transfers between devices, local(): partner.append(lax.ppermute(summed[c], 'zh', pair))  14.6 us
    ppermute x3, waiting for transfers between devices, local(): partner.append(lax.ppermute(summed[c], 'zh', pair))  4 us
    pallas_call x3, Pallas kernels, second(): pl.pallas_call(functools.partial(second_kernel, c), out_shape=(struct(272...  3.68 us
    pallas_call x1, Pallas kernels, local(): pl.pallas_call(first_kernel, out_shape=struct(*x.shape), in_specs=[SM] *...  2.77 us
    ppermute x2, starting transfers between devices, local(): got = [lax.ppermute(shared, ('y',) + BRICK, r) for r in rounds]  2.56 us
    pallas_call x1, Pallas kernels, local(): pl.pallas_call(last_kernel, out_shape=struct(16, 16, 16, 128), in_specs=[...  2.17 us
  transfers between devices with their start and end apart: 22, of which 9 were waited for; matrix products, arithmetic and copies ran while one was open for 0% of the time, Pallas kernels for 7%

profile of v4, /device:TPU:68, one launch (start us, length us, event | category | flops | bytes accessed | tf_op | source)
XLA Modules:
  0.0 85.6 jit_solution(11937950717244507565)
XLA Ops:
  0.0 1.6 %copy-done = f32[1,16,16,16,128]{4,3,2,1,0:T(8,128)S(1)} copy-done((f32[1,16,16,16,128]{4,3,2,1,0:T(8,128)S(1)}, f32[1,16,16,16,128]{4,3,2,1,0:T(8,128)}, u32[]{:S(2)}) %copy-start) | copy-done | bytes 2097176
  1.6 0.7 shard_map.74
  2.4 0.1 collective-permute-start
  2.5 1.7 %collective-permute-start.1 = (f32[3,16,256]{2,1,0:T(8,128)S(1)}, f32[3,16,256]{2,1,0:T(8,128)S(1)}, u32[]{:S(2)}, u32[]{:S(2)}) collective-permute-start(f32[3,16,256]{2,1,0:T(8,128)S(1)} %get-tuple-element.37.lo_ref), channel_id=1, source_target_pairs={{0,31},{1,0},{2,1},{3,2},{4,3},{5,4},{6,5},{7,6},{8,7},{9,8},{10,9... | collective-permute-start | bytes 147464 | tf_op jit(solution)/shard_map/ppermute | solution.py:287
  4.2 0.1 pad_add_fusion.pos
  5.0 2.8 %shard_map.73.u_ref = f32[16,16,16,128]{3,2,1,0:T(8,128)S(1)} custom-call(s32[1,4]{1,0:T(1,128)S(1)} %copy-done.3, f32[4]{0:T(128)S(1)} %copy-done.4, f32[4]{0:T(128)S(1)} %copy-done.5, f32[16,16,16,128]{3,2,1,0:T(8,128)S(1)} %bitcast.4), custom_call_target="tpu_custom_call" | custom-call | flops 10000000 | bytes 4194304 | tf_op jit(solution)/shard_map/pallas_call | solution.py:289
  7.8 1.0 %shard_map.75 = (f32[256,128]{1,0:T(8,128)S(1)}, f32[32,128]{1,0:T(8,128)S(1)}) custom-call(s32[1,4]{1,0:T(1,128)S(1)} %copy-done.3, f32[4]{0:T(128)S(1)} %copy-done.4, f32[4]{0:T(128)S(1)} %copy-done.5, s32[1]{0:T(128)S(6)} %copy.8.wgt, s32[2]{0:T(128)S(1)} %pad_add_fusion.pos, f32[3,16,256]{2,1,0:T(8,128)S(1)} %get-tuple-element.37.lo_ref, ...), custom_call_target="tpu_custom_call" | custom-call | tf_op jit(solution)/shard_map/pallas_call | solution.py:298
  8.8 1.0 %shard_map.76 = (f32[304,128]{1,0:T(8,128)S(1)}, f32[304,128]{1,0:T(8,128)S(1)}, f32[304,128]{1,0:T(8,128)S(1)}, f32[304,128]{1,0:T(8,128)S(1)}) custom-call(s32[1,4]{1,0:T(1,128)S(1)} %copy-done.3, f32[4]{0:T(128)S(1)} %copy-done.4, f32[4]{0:T(128)S(1)} %copy-done.5, s32[1]{0:T(128)S(6)} %copy.8.wgt, s32[2]{0:T(128)S(1)} %pad_add_fusion.pos, ...), custom_call_target="tpu_custom_call" | custom-call | flops 10000000 | bytes 4194304 | tf_op jit(solution)/shard_map/pallas_call | solution.py:308
  9.8 1.7 %collective-permute-start.2 = (f32[304,128]{1,0:T(8,128)S(1)}, f32[304,128]{1,0:T(8,128)S(1)}, u32[]{:S(2)}, u32[]{:S(2)}) collective-permute-start(f32[304,128]{1,0:T(8,128)S(1)} %get-tuple-element.48), channel_id=1, source_target_pairs={{0,32},{32,0},{64,96},{96,64},{1,33},{33,1},{65,97},{97,65},{2,34}... | collective-permute-start | bytes 466952 | tf_op jit(solution)/shard_map/ppermute | solution.py:318
  11.5 2.9 %collective-permute-start.4 = (f32[304,128]{1,0:T(8,128)S(1)}, f32[304,128]{1,0:T(8,128)S(1)}, u32[]{:S(2)}, u32[]{:S(2)}) collective-permute-start(f32[304,128]{1,0:T(8,128)S(1)} %get-tuple-element.50), channel_id=1, source_target_pairs={{0,64},{32,96},{64,0},{96,32},{1,65},{33,97},{65,1},{97,33},{2,66}... | collective-permute-start | bytes 466952 | tf_op jit(solution)/shard_map/ppermute | solution.py:318
  14.4 0.2 collective-permute-start.3
  14.6 1.0 %shard_map.77 = (f32[272,128]{1,0:T(8,128)S(1)}, f32[272,128]{1,0:T(8,128)S(1)}, f32[272,128]{1,0:T(8,128)S(1)}, f32[272,128]{1,0:T(8,128)S(1)}) custom-call(s32[1,4]{1,0:T(1,128)S(1)} %copy-done.3, f32[4]{0:T(128)S(1)} %copy-done.4, f32[4]{0:T(128)S(1)} %copy-done.5, s32[1]{0:T(128)S(6)} %copy.8.wgt, s32[2]{0:T(128)S(1)} %pad_add_fusion.pos, ...), custom_call_target="tpu_custom_call" | custom-call | flops 10000000 | bytes 4194304 | tf_op jit(solution)/shard_map/pallas_call | solution.py:308
  15.6 1.2 %collective-permute-done.2 = f32[304,128]{1,0:T(8,128)S(1)} collective-permute-done((f32[304,128]{1,0:T(8,128)S(1)}, f32[304,128]{1,0:T(8,128)S(1)}, u32[]{:S(2)}, u32[]{:S(2)}) %collective-permute-start.2) | collective-permute-done | bytes 155680 | tf_op jit(solution)/shard_map/ppermute | solution.py:318
  16.8 1.6 %collective-permute-start.6 = (f32[272,128]{1,0:T(8,128)S(1)}, f32[272,128]{1,0:T(8,128)S(1)}, u32[]{:S(2)}, u32[]{:S(2)}) collective-permute-start(f32[272,128]{1,0:T(8,128)S(1)} %get-tuple-element.56), channel_id=1, source_target_pairs={{0,32},{32,0},{64,96},{96,64},{1,33},{33,1},{65,97},{97,65},{2,34}... | collective-permute-start | bytes 417800 | tf_op jit(solution)/shard_map/ppermute | solution.py:318
  18.3 1.7 %shard_map.78 = (f32[544,128]{1,0:T(8,128)S(1)}, f32[544,128]{1,0:T(8,128)S(1)}, f32[544,128]{1,0:T(8,128)S(1)}, f32[544,128]{1,0:T(8,128)S(1)}) custom-call(s32[1,4]{1,0:T(1,128)S(1)} %copy-done.3, f32[4]{0:T(128)S(1)} %copy-done.4, f32[4]{0:T(128)S(1)} %copy-done.5, s32[1]{0:T(128)S(6)} %copy.8.wgt, s32[2]{0:T(128)S(1)} %pad_add_fusion.pos, ...), custom_call_target="tpu_custom_call" | custom-call | flops 10000000 | bytes 4194304 | tf_op jit(solution)/shard_map/pallas_call | solution.py:308
  20.0 0.0 copy-start.6
  20.1 3.0 %collective-permute-start.8 = (f32[272,128]{1,0:T(8,128)S(1)}, f32[272,128]{1,0:T(8,128)S(1)}, u32[]{:S(2)}, u32[]{:S(2)}) collective-permute-start(f32[272,128]{1,0:T(8,128)S(1)} %get-tuple-element.58), channel_id=1, source_target_pairs={{0,64},{32,96},{64,0},{96,32},{1,65},{33,97},{65,1},{97,33},{2,66}... | collective-permute-start | bytes 417800 | tf_op jit(solution)/shard_map/ppermute | solution.py:318
  23.0 0.2 collective-permute-start.7
  23.3 0.0 collective-permute-done.6
  23.3 3.3 %collective-permute-start.12 = (f32[544,128]{1,0:T(8,128)S(1)}, f32[544,128]{1,0:T(8,128)S(1)}, u32[]{:S(2)}, u32[]{:S(2)}) collective-permute-start(f32[544,128]{1,0:T(8,128)S(1)} %get-tuple-element.66), channel_id=1, source_target_pairs={{0,64},{32,96},{64,0},{96,32},{1,65},{33,97},{65,1},{97,33},{2,66}... | collective-permute-start | bytes 835592 | tf_op jit(solution)/shard_map/ppermute | solution.py:318
  26.6 0.0 collective-permute-done.4
  26.6 0.2 collective-permute-start.11
  26.7 0.0 collective-permute-done.3
  26.7 0.6 collective-permute-start.10
  27.4 1.5 %collective-permute-done.8 = f32[272,128]{1,0:T(8,128)S(1)} collective-permute-done((f32[272,128]{1,0:T(8,128)S(1)}, f32[272,128]{1,0:T(8,128)S(1)}, u32[]{:S(2)}, u32[]{:S(2)}) %collective-permute-start.8) | collective-permute-done | bytes 139296 | tf_op jit(solution)/shard_map/ppermute | solution.py:318
  28.9 5.4 %collective-permute-start.5 = (f32[304,128]{1,0:T(8,128)S(1)}, f32[304,128]{1,0:T(8,128)S(1)}, u32[]{:S(2)}, u32[]{:S(2)}) collective-permute-start(f32[304,128]{1,0:T(8,128)S(1)} %add_add_fusion.1.a_ref), channel_id=1, source_target_pairs={{0,128},{128,0},{1,129},{129,1},{2,130},{130,2},{3,131},{131,3},{4... | collective-permute-start | bytes 466952 | tf_op jit(solution)/shard_map/ppermute | solution.py:339
  34.3 2.7 %collective-permute-done.7 = f32[272,128]{1,0:T(8,128)S(1)} collective-permute-done((f32[272,128]{1,0:T(8,128)S(1)}, f32[272,128]{1,0:T(8,128)S(1)}, u32[]{:S(2)}, u32[]{:S(2)}) %collective-permute-start.7) | collective-permute-done | bytes 139296 | tf_op jit(solution)/shard_map/ppermute | solution.py:318
  37.1 4.7 %collective-permute-start.9 = (f32[272,128]{1,0:T(8,128)S(1)}, f32[272,128]{1,0:T(8,128)S(1)}, u32[]{:S(2)}, u32[]{:S(2)}) collective-permute-start(f32[272,128]{1,0:T(8,128)S(1)} %add_add_fusion.2.c_ref), channel_id=1, source_target_pairs={{0,128},{128,0},{1,129},{129,1},{2,130},{130,2},{3,131},{131,3},{4... | collective-permute-start | bytes 417800 | tf_op jit(solution)/shard_map/ppermute | solution.py:339
  41.8 0.0 collective-permute-done.12
  41.8 0.7 collective-permute-done.11
  42.5 0.0 collective-permute-done.10
  42.5 0.1 add_add_fusion.a_ref
  42.6 4.5 %collective-permute-start.16 = (f32[544,128]{1,0:T(8,128)S(1)}, f32[544,128]{1,0:T(8,128)S(1)}, u32[]{:S(2)}, u32[]{:S(2)}) collective-permute-start(f32[544,128]{1,0:T(8,128)S(1)} %add_add_fusion.a_ref), channel_id=1, source_target_pairs={{0,128},{128,0},{1,129},{129,1},{2,130},{130,2},{3,131},{131,3},{4... | collective-permute-start | bytes 835592 | tf_op jit(solution)/shard_map/ppermute | solution.py:339
  47.1 4.0 %collective-permute-done.9.d_ref = f32[272,128]{1,0:T(8,128)S(1)} collective-permute-done((f32[272,128]{1,0:T(8,128)S(1)}, f32[272,128]{1,0:T(8,128)S(1)}, u32[]{:S(2)}, u32[]{:S(2)}) %collective-permute-start.9) | collective-permute-done | bytes 139296 | tf_op jit(solution)/shard_map/ppermute | solution.py:339
  51.1 0.7 shard_map.79.refs_0_
  51.8 1.9 %collective-permute-start.13 = (f32[512,128]{1,0:T(8,128)S(1)}, f32[512,128]{1,0:T(8,128)S(1)}, u32[]{:S(2)}, u32[]{:S(2)}) collective-permute-start(f32[512,128]{1,0:T(8,128)S(1)} %shard_map.79.refs_0_), channel_id=1, source_target_pairs={{0,32},{32,0},{64,96},{96,64},{1,33},{33,1},{65,97},{97,65},{2,34}... | collective-permute-start | bytes 786440 | tf_op jit(solution)/shard_map/ppermute | solution.py:318
  53.7 0.0 collective-permute-start.14
  53.7 2.3 %collective-permute-start.15 = (f32[512,128]{1,0:T(8,128)S(1)}, f32[512,128]{1,0:T(8,128)S(1)}, u32[]{:S(2)}, u32[]{:S(2)}) collective-permute-start(f32[512,128]{1,0:T(8,128)S(1)} %shard_map.79.refs_0_), channel_id=1, source_target_pairs={{0,64},{32,96},{64,0},{96,32},{1,65},{33,97},{65,1},{97,33},{2,66}... | collective-permute-start | bytes 786440 | tf_op jit(solution)/shard_map/ppermute | solution.py:318
  56.0 1.9 %collective-permute-start.17 = (f32[32,128]{1,0:T(8,128)S(1)}, f32[32,128]{1,0:T(8,128)S(1)}, u32[]{:S(2)}, u32[]{:S(2)}) collective-permute-start(f32[32,128]{1,0:T(8,128)S(1)} %slice_add_fusion.shared_ref), channel_id=1, source_target_pairs={{0,1},{32,34},{4,2},{2,3},{64,68},{8,4},{36,37},{68,70},{40,38},{6... | collective-permute-start | bytes 49160 | tf_op jit(solution)/shard_map/ppermute | solution.py:341
  58.0 3.2 %collective-permute-done.13.refs_1_ = f32[512,128]{1,0:T(8,128)S(1)} collective-permute-done((f32[512,128]{1,0:T(8,128)S(1)}, f32[512,128]{1,0:T(8,128)S(1)}, u32[]{:S(2)}, u32[]{:S(2)}) %collective-permute-start.13) | collective-permute-done | bytes 262176 | tf_op jit(solution)/shard_map/ppermute | solution.py:318
  61.1 0.7 collective-permute-start.18
  61.8 4.8 %collective-permute-done.14.refs_2_ = f32[512,128]{1,0:T(8,128)S(1)} collective-permute-done((f32[512,128]{1,0:T(8,128)S(1)}, f32[512,128]{1,0:T(8,128)S(1)}, u32[]{:S(2)}, u32[]{:S(2)}) %collective-permute-start.14) | collective-permute-done | bytes 262176 | tf_op jit(solution)/shard_map/ppermute | solution.py:318
  66.7 1.2 %shard_map.80.refs_4_ = f32[544,128]{1,0:T(8,128)S(1)} custom-call(s32[2]{0:T(128)S(1)} %pad_add_fusion.pos, f32[3,128]{1,0:T(4,128)S(1)} %copy-done.6, f32[544,128]{1,0:T(8,128)S(1)} %add_add_fusion.a_ref, f32[544,128]{1,0:T(8,128)S(1)} %collective-permute-done.16.b_ref, f32[128,128]{1,0:T(8,128)S(1)} %copy-done.2, f32[32,128]{1,0:T(8,128)S(1)} %slice_add_fusion.shared_ref, ...), custom_call_target="tpu_custom_call" | custom-call | tf_op jit(solution)/shard_map/pallas_call | solution.py:321
  67.8 2.6 %collective-permute-start.19 = (f32[544,128]{1,0:T(8,128)S(1)}, f32[544,128]{1,0:T(8,128)S(1)}, u32[]{:S(2)}, u32[]{:S(2)}) collective-permute-start(f32[544,128]{1,0:T(8,128)S(1)} %shard_map.80.refs_4_), channel_id=1, source_target_pairs={{0,32},{32,0},{64,96},{96,64},{1,33},{33,1},{65,97},{97,65},{2,34}... | collective-permute-start | bytes 835592 | tf_op jit(solution)/shard_map/ppermute | solution.py:318
  70.5 2.2 %collective-permute-start.21 = (f32[544,128]{1,0:T(8,128)S(1)}, f32[544,128]{1,0:T(8,128)S(1)}, u32[]{:S(2)}, u32[]{:S(2)}) collective-permute-start(f32[544,128]{1,0:T(8,128)S(1)} %shard_map.80.refs_4_), channel_id=1, source_target_pairs={{0,64},{32,96},{64,0},{96,32},{1,65},{33,97},{65,1},{97,33},{2,66}... | collective-permute-start | bytes 835592 | tf_op jit(solution)/shard_map/ppermute | solution.py:318
  72.6 5.4 %collective-permute-done.19.refs_5_ = f32[544,128]{1,0:T(8,128)S(1)} collective-permute-done((f32[544,128]{1,0:T(8,128)S(1)}, f32[544,128]{1,0:T(8,128)S(1)}, u32[]{:S(2)}, u32[]{:S(2)}) %collective-permute-start.19) | collective-permute-done | bytes 278560 | tf_op jit(solution)/shard_map/ppermute | solution.py:318
  78.0 5.3 %collective-permute-done.20.refs_6_ = f32[544,128]{1,0:T(8,128)S(1)} collective-permute-done((f32[544,128]{1,0:T(8,128)S(1)}, f32[544,128]{1,0:T(8,128)S(1)}, u32[]{:S(2)}, u32[]{:S(2)}) %collective-permute-start.20) | collective-permute-done | bytes 278560 | tf_op jit(solution)/shard_map/ppermute | solution.py:318
  83.3 2.2 %shard_map.81 = f32[16,16,16,128]{3,2,1,0:T(8,128)} custom-call(s32[2]{0:T(128)S(1)} %pad_add_fusion.pos, f32[512,128]{1,0:T(8,128)S(1)} %shard_map.79.refs_0_, f32[512,128]{1,0:T(8,128)S(1)} %collective-permute-done.13.refs_1_, f32[512,128]{1,0:T(8,128)S(1)} %collective-permute-done.14.refs_2_, f32[512,128]{1,0:T(8,128)S(1)} %collective-permute-done.15.refs_3_, ...), custom_call_target="tpu_custom_call" | custom-call | tf_op jit(solution)/shard_map/pallas_call | solution.py:365
  (24 shorter events, 0.1 us)
Async XLA Ops:
  0.0 4.9 %copy-start.3 = (s32[1,4]{1,0:T(1,128)S(1)}, s32[1,4]{1,0:T(1,128)}, u32[]{:S(2)}) copy-start(s32[1,4]{1,0:T(1,128)} %lev.9) | copy-start | bytes 52
  0.0 4.9 %copy-start.4 = (f32[4]{0:T(128)S(1)}, f32[4]{0:T(128)}, u32[]{:S(2)}) copy-start(f32[4]{0:T(128)} %vel.9) | copy-start | bytes 52
  0.0 4.9 %copy-start.5 = (f32[4]{0:T(128)S(1)}, f32[4]{0:T(128)}, u32[]{:S(2)}) copy-start(f32[4]{0:T(128)} %dif.9) | copy-start | bytes 52
  0.0 1.6 %copy-start = (f32[1,16,16,16,128]{4,3,2,1,0:T(8,128)S(1)}, f32[1,16,16,16,128]{4,3,2,1,0:T(8,128)}, u32[]{:S(2)}) copy-start(f32[1,16,16,16,128]{4,3,2,1,0:T(8,128)} %param.7) | copy-start | bytes 6291460
  1.6 3.3 %copy-start.1 = (f32[1,16,16,16,128]{4,3,2,1,0:T(8,128)S(1)}, f32[1,16,16,16,128]{4,3,2,1,0:T(8,128)}, u32[]{:S(2)}) copy-start(f32[1,16,16,16,128]{4,3,2,1,0:T(8,128)} %param.7) | copy-start | bytes 6291460
  2.4 5.4 %collective-permute-start = (f32[2,16,256]{2,1,0:T(8,128)S(1)}, f32[2,16,256]{2,1,0:T(8,128)S(1)}, u32[]{:S(2)}, u32[]{:S(2)}) collective-permute-start(f32[2,16,256]{2,1,0:T(8,128)S(1)} %get-tuple-element.38.hi_ref), channel_id=1, source_target_pairs={{0,1},{1,2},{2,3},{3,4},{4,5},{5,6},{6,7},{7,8},{8,9},{9,10},{10,1... | collective-permute-start | bytes 98312 | tf_op jit(solution)/shard_map/ppermute | solution.py:286
  2.5 5.3 %collective-permute-start.1 = (f32[3,16,256]{2,1,0:T(8,128)S(1)}, f32[3,16,256]{2,1,0:T(8,128)S(1)}, u32[]{:S(2)}, u32[]{:S(2)}) collective-permute-start(f32[3,16,256]{2,1,0:T(8,128)S(1)} %get-tuple-element.37.lo_ref), channel_id=1, source_target_pairs={{0,31},{1,0},{2,1},{3,2},{4,3},{5,4},{6,5},{7,6},{8,7},{9,8},{10,9... | collective-permute-start | bytes 147464 | tf_op jit(solution)/shard_map/ppermute | solution.py:287
  9.8 6.9 %collective-permute-start.2 = (f32[304,128]{1,0:T(8,128)S(1)}, f32[304,128]{1,0:T(8,128)S(1)}, u32[]{:S(2)}, u32[]{:S(2)}) collective-permute-start(f32[304,128]{1,0:T(8,128)S(1)} %get-tuple-element.48), channel_id=1, source_target_pairs={{0,32},{32,0},{64,96},{96,64},{1,33},{33,1},{65,97},{97,65},{2,34}... | collective-permute-start | bytes 466952 | tf_op jit(solution)/shard_map/ppermute | solution.py:318
  11.5 15.1 %collective-permute-start.4 = (f32[304,128]{1,0:T(8,128)S(1)}, f32[304,128]{1,0:T(8,128)S(1)}, u32[]{:S(2)}, u32[]{:S(2)}) collective-permute-start(f32[304,128]{1,0:T(8,128)S(1)} %get-tuple-element.50), channel_id=1, source_target_pairs={{0,64},{32,96},{64,0},{96,32},{1,65},{33,97},{65,1},{97,33},{2,66}... | collective-permute-start | bytes 466952 | tf_op jit(solution)/shard_map/ppermute | solution.py:318
  14.4 12.4 %collective-permute-start.3 = (f32[304,128]{1,0:T(8,128)S(1)}, f32[304,128]{1,0:T(8,128)S(1)}, u32[]{:S(2)}, u32[]{:S(2)}) collective-permute-start(f32[304,128]{1,0:T(8,128)S(1)} %get-tuple-element.49), channel_id=1, source_target_pairs={{0,96},{32,64},{64,32},{96,0},{1,97},{33,65},{65,33},{97,1},{2,98}... | collective-permute-start | bytes 466952 | tf_op jit(solution)/shard_map/ppermute | solution.py:318
  16.8 6.5 %collective-permute-start.6 = (f32[272,128]{1,0:T(8,128)S(1)}, f32[272,128]{1,0:T(8,128)S(1)}, u32[]{:S(2)}, u32[]{:S(2)}) collective-permute-start(f32[272,128]{1,0:T(8,128)S(1)} %get-tuple-element.56), channel_id=1, source_target_pairs={{0,32},{32,0},{64,96},{96,64},{1,33},{33,1},{65,97},{97,65},{2,34}... | collective-permute-start | bytes 417800 | tf_op jit(solution)/shard_map/ppermute | solution.py:318
  18.3 32.7 %copy-start.2 = (f32[128,128]{1,0:T(8,128)S(1)}, f32[128,128]{1,0:T(8,128)}, u32[]{:S(2)}) copy-start(f32[128,128]{1,0:T(8,128)} %constant.23.clone.mat_ref) | copy-start | bytes 196612
  20.0 46.6 %copy-start.6 = (f32[3,128]{1,0:T(4,128)S(1)}, f32[3,128]{1,0:T(4,128)}, u32[]{:S(2)}) copy-start(f32[3,128]{1,0:T(4,128)} %constant.24.clone.table) | copy-start | bytes 4612
  20.1 8.8 %collective-permute-start.8 = (f32[272,128]{1,0:T(8,128)S(1)}, f32[272,128]{1,0:T(8,128)S(1)}, u32[]{:S(2)}, u32[]{:S(2)}) collective-permute-start(f32[272,128]{1,0:T(8,128)S(1)} %get-tuple-element.58), channel_id=1, source_target_pairs={{0,64},{32,96},{64,0},{96,32},{1,65},{33,97},{65,1},{97,33},{2,66}... | collective-permute-start | bytes 417800 | tf_op jit(solution)/shard_map/ppermute | solution.py:318
  23.0 14.0 %collective-permute-start.7 = (f32[272,128]{1,0:T(8,128)S(1)}, f32[272,128]{1,0:T(8,128)S(1)}, u32[]{:S(2)}, u32[]{:S(2)}) collective-permute-start(f32[272,128]{1,0:T(8,128)S(1)} %get-tuple-element.57), channel_id=1, source_target_pairs={{0,96},{32,64},{64,32},{96,0},{1,97},{33,65},{65,33},{97,1},{2,98}... | collective-permute-start | bytes 417800 | tf_op jit(solution)/shard_map/ppermute | solution.py:318
  23.3 18.5 %collective-permute-start.12 = (f32[544,128]{1,0:T(8,128)S(1)}, f32[544,128]{1,0:T(8,128)S(1)}, u32[]{:S(2)}, u32[]{:S(2)}) collective-permute-start(f32[544,128]{1,0:T(8,128)S(1)} %get-tuple-element.66), channel_id=1, source_target_pairs={{0,64},{32,96},{64,0},{96,32},{1,65},{33,97},{65,1},{97,33},{2,66}... | collective-permute-start | bytes 835592 | tf_op jit(solution)/shard_map/ppermute | solution.py:318
  26.6 15.9 %collective-permute-start.11 = (f32[544,128]{1,0:T(8,128)S(1)}, f32[544,128]{1,0:T(8,128)S(1)}, u32[]{:S(2)}, u32[]{:S(2)}) collective-permute-start(f32[544,128]{1,0:T(8,128)S(1)} %get-tuple-element.65), channel_id=1, source_target_pairs={{0,96},{32,64},{64,32},{96,0},{1,97},{33,65},{65,33},{97,1},{2,98}... | collective-permute-start | bytes 835592 | tf_op jit(solution)/shard_map/ppermute | solution.py:318
  26.7 15.8 %collective-permute-start.10 = (f32[544,128]{1,0:T(8,128)S(1)}, f32[544,128]{1,0:T(8,128)S(1)}, u32[]{:S(2)}, u32[]{:S(2)}) collective-permute-start(f32[544,128]{1,0:T(8,128)S(1)} %get-tuple-element.64), channel_id=1, source_target_pairs={{0,32},{32,0},{64,96},{96,64},{1,33},{33,1},{65,97},{97,65},{2,34}... | collective-permute-start | bytes 835592 | tf_op jit(solution)/shard_map/ppermute | solution.py:318
  28.9 22.2 %collective-permute-start.5 = (f32[304,128]{1,0:T(8,128)S(1)}, f32[304,128]{1,0:T(8,128)S(1)}, u32[]{:S(2)}, u32[]{:S(2)}) collective-permute-start(f32[304,128]{1,0:T(8,128)S(1)} %add_add_fusion.1.a_ref), channel_id=1, source_target_pairs={{0,128},{128,0},{1,129},{129,1},{2,130},{130,2},{3,131},{131,3},{4... | collective-permute-start | bytes 466952 | tf_op jit(solution)/shard_map/ppermute | solution.py:339
  37.1 14.0 %collective-permute-start.9 = (f32[272,128]{1,0:T(8,128)S(1)}, f32[272,128]{1,0:T(8,128)S(1)}, u32[]{:S(2)}, u32[]{:S(2)}) collective-permute-start(f32[272,128]{1,0:T(8,128)S(1)} %add_add_fusion.2.c_ref), channel_id=1, source_target_pairs={{0,128},{128,0},{1,129},{129,1},{2,130},{130,2},{3,131},{131,3},{4... | collective-permute-start | bytes 417800 | tf_op jit(solution)/shard_map/ppermute | solution.py:339
  42.6 24.0 %collective-permute-start.16 = (f32[544,128]{1,0:T(8,128)S(1)}, f32[544,128]{1,0:T(8,128)S(1)}, u32[]{:S(2)}, u32[]{:S(2)}) collective-permute-start(f32[544,128]{1,0:T(8,128)S(1)} %add_add_fusion.a_ref), channel_id=1, source_target_pairs={{0,128},{128,0},{1,129},{129,1},{2,130},{130,2},{3,131},{131,3},{4... | collective-permute-start | bytes 835592 | tf_op jit(solution)/shard_map/ppermute | solution.py:339
  51.8 9.3 %collective-permute-start.13 = (f32[512,128]{1,0:T(8,128)S(1)}, f32[512,128]{1,0:T(8,128)S(1)}, u32[]{:S(2)}, u32[]{:S(2)}) collective-permute-start(f32[512,128]{1,0:T(8,128)S(1)} %shard_map.79.refs_0_), channel_id=1, source_target_pairs={{0,32},{32,0},{64,96},{96,64},{1,33},{33,1},{65,97},{97,65},{2,34}... | collective-permute-start | bytes 786440 | tf_op jit(solution)/shard_map/ppermute | solution.py:318
  53.7 12.9 %collective-permute-start.14 = (f32[512,128]{1,0:T(8,128)S(1)}, f32[512,128]{1,0:T(8,128)S(1)}, u32[]{:S(2)}, u32[]{:S(2)}) collective-permute-start(f32[512,128]{1,0:T(8,128)S(1)} %shard_map.79.refs_0_), channel_id=1, source_target_pairs={{0,96},{32,64},{64,32},{96,0},{1,97},{33,65},{65,33},{97,1},{2,98}... | collective-permute-start | bytes 786440 | tf_op jit(solution)/shard_map/ppermute | solution.py:318
  53.7 12.9 %collective-permute-start.15 = (f32[512,128]{1,0:T(8,128)S(1)}, f32[512,128]{1,0:T(8,128)S(1)}, u32[]{:S(2)}, u32[]{:S(2)}) collective-permute-start(f32[512,128]{1,0:T(8,128)S(1)} %shard_map.79.refs_0_), channel_id=1, source_target_pairs={{0,64},{32,96},{64,0},{96,32},{1,65},{33,97},{65,1},{97,33},{2,66}... | collective-permute-start | bytes 786440 | tf_op jit(solution)/shard_map/ppermute | solution.py:318
  56.0 10.6 %collective-permute-start.17 = (f32[32,128]{1,0:T(8,128)S(1)}, f32[32,128]{1,0:T(8,128)S(1)}, u32[]{:S(2)}, u32[]{:S(2)}) collective-permute-start(f32[32,128]{1,0:T(8,128)S(1)} %slice_add_fusion.shared_ref), channel_id=1, source_target_pairs={{0,1},{32,34},{4,2},{2,3},{64,68},{8,4},{36,37},{68,70},{40,38},{6... | collective-permute-start | bytes 49160 | tf_op jit(solution)/shard_map/ppermute | solution.py:341
  61.1 5.5 %collective-permute-start.18 = (f32[32,128]{1,0:T(8,128)S(1)}, f32[32,128]{1,0:T(8,128)S(1)}, u32[]{:S(2)}, u32[]{:S(2)}) collective-permute-start(f32[32,128]{1,0:T(8,128)S(1)} %slice_add_fusion.shared_ref), channel_id=1, source_target_pairs={{8,12},{0,16},{16,18},{48,52},{80,88},{32,56},{24,28},{64,92},{96,... | collective-permute-start | bytes 49160 | tf_op jit(solution)/shard_map/ppermute | solution.py:341
  67.8 10.2 %collective-permute-start.19 = (f32[544,128]{1,0:T(8,128)S(1)}, f32[544,128]{1,0:T(8,128)S(1)}, u32[]{:S(2)}, u32[]{:S(2)}) collective-permute-start(f32[544,128]{1,0:T(8,128)S(1)} %shard_map.80.refs_4_), channel_id=1, source_target_pairs={{0,32},{32,0},{64,96},{96,64},{1,33},{33,1},{65,97},{97,65},{2,34}... | collective-permute-start | bytes 835592 | tf_op jit(solution)/shard_map/ppermute | solution.py:318
  70.5 12.8 %collective-permute-start.20 = (f32[544,128]{1,0:T(8,128)S(1)}, f32[544,128]{1,0:T(8,128)S(1)}, u32[]{:S(2)}, u32[]{:S(2)}) collective-permute-start(f32[544,128]{1,0:T(8,128)S(1)} %shard_map.80.refs_4_), channel_id=1, source_target_pairs={{0,96},{32,64},{64,32},{96,0},{1,97},{33,65},{65,33},{97,1},{2,98}... | collective-permute-start | bytes 835592 | tf_op jit(solution)/shard_map/ppermute | solution.py:318
  70.5 12.8 %collective-permute-start.21 = (f32[544,128]{1,0:T(8,128)S(1)}, f32[544,128]{1,0:T(8,128)S(1)}, u32[]{:S(2)}, u32[]{:S(2)}) collective-permute-start(f32[544,128]{1,0:T(8,128)S(1)} %shard_map.80.refs_4_), channel_id=1, source_target_pairs={{0,64},{32,96},{64,0},{96,32},{1,65},{33,97},{65,1},{97,33},{2,66}... | collective-permute-start | bytes 835592 | tf_op jit(solution)/shard_map/ppermute | solution.py:318

commit v5 on v4

--- a/solution.py
+++ b/solution.py
@@ -334,8 +334,8 @@
         parts = second(c, value)
         value = after(u, parts[0])
         got = to_others(after(parts[1:], *gate))
-        gate = (got[0],)
         summed.append(parts[0] + got[0] + got[1] + got[2])
+        gate = (summed[0],) if c else ()
         partner.append(lax.ppermute(summed[c], "zh", pair))
     shared = summed[0][-32:] + partner[0][-32:]
     got = [lax.ppermute(shared, ("y",) + BRICK, r) for r in rounds]

time: 85.8 us -> 84.7 us (0.987)
  the two profiles are of different devices: /device:TPU:68 before, /device:TPU:96 now
where the time goes in v5:
time: 84.7 us; the launch traced here: 84.5 us
  starting transfers between devices  38.3 us (45%)
  waiting for transfers between devices  31 us (37%)
  Pallas kernels  12.3 us (15%)
  local copies, waits for them, and re-layouts  1.65 us (2%)
  between operations  1.04 us (1%)
    ppermute x15, waiting for transfers between devices, to_others(): lax.ppermute(value, 'y', perm)  28.6 us
    ppermute x15, starting transfers between devices, to_others(): lax.ppermute(value, 'y', perm)  23.3 us
    ppermute x3, starting transfers between devices, local(): partner.append(lax.ppermute(summed[c], 'zh', pair))  11.3 us
    pallas_call x3, Pallas kernels, second(): pl.pallas_call(functools.partial(second_kernel, c), out_shape=(struct(272...  3.68 us
    pallas_call x1, Pallas kernels, local(): pl.pallas_call(first_kernel, out_shape=struct(*x.shape), in_specs=[SM] *...  2.77 us
    ppermute x3, waiting for transfers between devices, local(): partner.append(lax.ppermute(summed[c], 'zh', pair))  2.46 us
    pallas_call x1, Pallas kernels, local(): pl.pallas_call(last_kernel, out_shape=struct(16, 16, 16, 128), in_specs=[...  2.17 us
    ppermute x2, starting transfers between devices, local(): got = [lax.ppermute(shared, ('y',) + BRICK, r) for r in rounds]  1.93 us
  transfers between devices with their start and end apart: 22, of which 9 were waited for; matrix products, arithmetic and copies ran while one was open for 0% of the time, Pallas kernels for 7%

profile of v5, /device:TPU:96, one launch (start us, length us, event | category | flops | bytes accessed | tf_op | source)
XLA Modules:
  0.0 84.5 jit_solution(1149634677318040206)
XLA Ops:
  0.0 1.6 %copy-done = f32[1,16,16,16,128]{4,3,2,1,0:T(8,128)S(1)} copy-done((f32[1,16,16,16,128]{4,3,2,1,0:T(8,128)S(1)}, f32[1,16,16,16,128]{4,3,2,1,0:T(8,128)}, u32[]{:S(2)}) %copy-start) | copy-done | bytes 2097176
  1.6 0.7 shard_map.74
  2.4 0.1 collective-permute-start
  2.5 1.7 %collective-permute-start.1 = (f32[3,16,256]{2,1,0:T(8,128)S(1)}, f32[3,16,256]{2,1,0:T(8,128)S(1)}, u32[]{:S(2)}, u32[]{:S(2)}) collective-permute-start(f32[3,16,256]{2,1,0:T(8,128)S(1)} %get-tuple-element.37.lo_ref), channel_id=1, source_target_pairs={{0,31},{1,0},{2,1},{3,2},{4,3},{5,4},{6,5},{7,6},{8,7},{9,8},{10,9... | collective-permute-start | bytes 147464 | tf_op jit(solution)/shard_map/ppermute | solution.py:287
  4.2 0.1 pad_add_fusion.pos
  5.0 2.8 %shard_map.73.u_ref = f32[16,16,16,128]{3,2,1,0:T(8,128)S(1)} custom-call(s32[1,4]{1,0:T(1,128)S(1)} %copy-done.3, f32[4]{0:T(128)S(1)} %copy-done.4, f32[4]{0:T(128)S(1)} %copy-done.5, f32[16,16,16,128]{3,2,1,0:T(8,128)S(1)} %bitcast.4), custom_call_target="tpu_custom_call" | custom-call | flops 10000000 | bytes 4194304 | tf_op jit(solution)/shard_map/pallas_call | solution.py:289
  7.7 0.0 collective-permute-done.left_ref
  7.8 1.0 %shard_map.75 = (f32[256,128]{1,0:T(8,128)S(1)}, f32[32,128]{1,0:T(8,128)S(1)}) custom-call(s32[1,4]{1,0:T(1,128)S(1)} %copy-done.3, f32[4]{0:T(128)S(1)} %copy-done.4, f32[4]{0:T(128)S(1)} %copy-done.5, s32[1]{0:T(128)S(6)} %copy.8.wgt, s32[2]{0:T(128)S(1)} %pad_add_fusion.pos, f32[3,16,256]{2,1,0:T(8,128)S(1)} %get-tuple-element.37.lo_ref, ...), custom_call_target="tpu_custom_call" | custom-call | tf_op jit(solution)/shard_map/pallas_call | solution.py:298
  8.8 1.0 %shard_map.76 = (f32[304,128]{1,0:T(8,128)S(1)}, f32[304,128]{1,0:T(8,128)S(1)}, f32[304,128]{1,0:T(8,128)S(1)}, f32[304,128]{1,0:T(8,128)S(1)}) custom-call(s32[1,4]{1,0:T(1,128)S(1)} %copy-done.3, f32[4]{0:T(128)S(1)} %copy-done.4, f32[4]{0:T(128)S(1)} %copy-done.5, s32[1]{0:T(128)S(6)} %copy.8.wgt, s32[2]{0:T(128)S(1)} %pad_add_fusion.pos, ...), custom_call_target="tpu_custom_call" | custom-call | flops 10000000 | bytes 4194304 | tf_op jit(solution)/shard_map/pallas_call | solution.py:308
  9.8 3.3 %collective-permute-start.4 = (f32[304,128]{1,0:T(8,128)S(1)}, f32[304,128]{1,0:T(8,128)S(1)}, u32[]{:S(2)}, u32[]{:S(2)}) collective-permute-start(f32[304,128]{1,0:T(8,128)S(1)} %get-tuple-element.50), channel_id=1, source_target_pairs={{0,64},{32,96},{64,0},{96,32},{1,65},{33,97},{65,1},{97,33},{2,66}... | collective-permute-start | bytes 466952 | tf_op jit(solution)/shard_map/ppermute | solution.py:318
  13.1 1.1 %collective-permute-start.3 = (f32[304,128]{1,0:T(8,128)S(1)}, f32[304,128]{1,0:T(8,128)S(1)}, u32[]{:S(2)}, u32[]{:S(2)}) collective-permute-start(f32[304,128]{1,0:T(8,128)S(1)} %get-tuple-element.49), channel_id=1, source_target_pairs={{0,96},{32,64},{64,32},{96,0},{1,97},{33,65},{65,33},{97,1},{2,98}... | collective-permute-start | bytes 466952 | tf_op jit(solution)/shard_map/ppermute | solution.py:318
  14.2 0.0 collective-permute-start.2
  14.2 1.0 %shard_map.77 = (f32[272,128]{1,0:T(8,128)S(1)}, f32[272,128]{1,0:T(8,128)S(1)}, f32[272,128]{1,0:T(8,128)S(1)}, f32[272,128]{1,0:T(8,128)S(1)}) custom-call(s32[1,4]{1,0:T(1,128)S(1)} %copy-done.3, f32[4]{0:T(128)S(1)} %copy-done.4, f32[4]{0:T(128)S(1)} %copy-done.5, s32[1]{0:T(128)S(6)} %copy.8.wgt, s32[2]{0:T(128)S(1)} %pad_add_fusion.pos, ...), custom_call_target="tpu_custom_call" | custom-call | flops 10000000 | bytes 4194304 | tf_op jit(solution)/shard_map/pallas_call | solution.py:308
  15.2 3.7 %collective-permute-start.8 = (f32[272,128]{1,0:T(8,128)S(1)}, f32[272,128]{1,0:T(8,128)S(1)}, u32[]{:S(2)}, u32[]{:S(2)}) collective-permute-start(f32[272,128]{1,0:T(8,128)S(1)} %get-tuple-element.58), channel_id=1, source_target_pairs={{0,64},{32,96},{64,0},{96,32},{1,65},{33,97},{65,1},{97,33},{2,66}... | collective-permute-start | bytes 417800 | tf_op jit(solution)/shard_map/ppermute | solution.py:318
  18.9 1.1 %collective-permute-start.7 = (f32[272,128]{1,0:T(8,128)S(1)}, f32[272,128]{1,0:T(8,128)S(1)}, u32[]{:S(2)}, u32[]{:S(2)}) collective-permute-start(f32[272,128]{1,0:T(8,128)S(1)} %get-tuple-element.57), channel_id=1, source_target_pairs={{0,96},{32,64},{64,32},{96,0},{1,97},{33,65},{65,33},{97,1},{2,98}... | collective-permute-start | bytes 417800 | tf_op jit(solution)/shard_map/ppermute | solution.py:318
  19.9 1.7 %shard_map.78 = (f32[544,128]{1,0:T(8,128)S(1)}, f32[544,128]{1,0:T(8,128)S(1)}, f32[544,128]{1,0:T(8,128)S(1)}, f32[544,128]{1,0:T(8,128)S(1)}) custom-call(s32[1,4]{1,0:T(1,128)S(1)} %copy-done.3, f32[4]{0:T(128)S(1)} %copy-done.4, f32[4]{0:T(128)S(1)} %copy-done.5, s32[1]{0:T(128)S(6)} %copy.8.wgt, s32[2]{0:T(128)S(1)} %pad_add_fusion.pos, ...), custom_call_target="tpu_custom_call" | custom-call | flops 10000000 | bytes 4194304 | tf_op jit(solution)/shard_map/pallas_call | solution.py:308
  21.6 0.0 copy-start.6
  21.7 0.1 collective-permute-start.6
  21.8 0.0 collective-permute-done.3
  21.8 0.1 collective-permute-done.2
  21.9 3.6 %collective-permute-start.12 = (f32[544,128]{1,0:T(8,128)S(1)}, f32[544,128]{1,0:T(8,128)S(1)}, u32[]{:S(2)}, u32[]{:S(2)}) collective-permute-start(f32[544,128]{1,0:T(8,128)S(1)} %get-tuple-element.66), channel_id=1, source_target_pairs={{0,64},{32,96},{64,0},{96,32},{1,65},{33,97},{65,1},{97,33},{2,66}... | collective-permute-start | bytes 835592 | tf_op jit(solution)/shard_map/ppermute | solution.py:318
  25.5 1.1 %collective-permute-start.11 = (f32[544,128]{1,0:T(8,128)S(1)}, f32[544,128]{1,0:T(8,128)S(1)}, u32[]{:S(2)}, u32[]{:S(2)}) collective-permute-start(f32[544,128]{1,0:T(8,128)S(1)} %get-tuple-element.65), channel_id=1, source_target_pairs={{0,96},{32,64},{64,32},{96,0},{1,97},{33,65},{65,33},{97,1},{2,98}... | collective-permute-start | bytes 835592 | tf_op jit(solution)/shard_map/ppermute | solution.py:318
  26.6 0.0 collective-permute-done.8
  26.6 0.0 collective-permute-start.10
  26.6 2.6 %collective-permute-done.7 = f32[272,128]{1,0:T(8,128)S(1)} collective-permute-done((f32[272,128]{1,0:T(8,128)S(1)}, f32[272,128]{1,0:T(8,128)S(1)}, u32[]{:S(2)}, u32[]{:S(2)}) %collective-permute-start.7) | collective-permute-done | bytes 139296 | tf_op jit(solution)/shard_map/ppermute | solution.py:318
  29.2 0.0 collective-permute-done.6
  29.3 3.5 %collective-permute-start.9 = (f32[272,128]{1,0:T(8,128)S(1)}, f32[272,128]{1,0:T(8,128)S(1)}, u32[]{:S(2)}, u32[]{:S(2)}) collective-permute-start(f32[272,128]{1,0:T(8,128)S(1)} %add_add_fusion.2.c_ref), channel_id=1, source_target_pairs={{0,128},{128,0},{1,129},{129,1},{2,130},{130,2},{3,131},{131,3},{4... | collective-permute-start | bytes 417800 | tf_op jit(solution)/shard_map/ppermute | solution.py:339
  32.8 2.5 %collective-permute-start.5 = (f32[304,128]{1,0:T(8,128)S(1)}, f32[304,128]{1,0:T(8,128)S(1)}, u32[]{:S(2)}, u32[]{:S(2)}) collective-permute-start(f32[304,128]{1,0:T(8,128)S(1)} %add_add_fusion.1.a_ref), channel_id=1, source_target_pairs={{0,128},{128,0},{1,129},{129,1},{2,130},{130,2},{3,131},{131,3},{4... | collective-permute-start | bytes 466952 | tf_op jit(solution)/shard_map/ppermute | solution.py:339
  35.3 0.7 collective-permute-done.12
  36.0 4.2 %collective-permute-done.11 = f32[544,128]{1,0:T(8,128)S(1)} collective-permute-done((f32[544,128]{1,0:T(8,128)S(1)}, f32[544,128]{1,0:T(8,128)S(1)}, u32[]{:S(2)}, u32[]{:S(2)}) %collective-permute-start.11) | collective-permute-done | bytes 278560 | tf_op jit(solution)/shard_map/ppermute | solution.py:318
  40.2 0.1 add_add_fusion.a_ref
  40.3 5.2 %collective-permute-start.16 = (f32[544,128]{1,0:T(8,128)S(1)}, f32[544,128]{1,0:T(8,128)S(1)}, u32[]{:S(2)}, u32[]{:S(2)}) collective-permute-start(f32[544,128]{1,0:T(8,128)S(1)} %add_add_fusion.a_ref), channel_id=1, source_target_pairs={{0,128},{128,0},{1,129},{129,1},{2,130},{130,2},{3,131},{131,3},{4... | collective-permute-start | bytes 835592 | tf_op jit(solution)/shard_map/ppermute | solution.py:339
  45.5 2.5 %collective-permute-done.5.b_ref = f32[304,128]{1,0:T(8,128)S(1)} collective-permute-done((f32[304,128]{1,0:T(8,128)S(1)}, f32[304,128]{1,0:T(8,128)S(1)}, u32[]{:S(2)}, u32[]{:S(2)}) %collective-permute-start.5) | collective-permute-done | bytes 155680 | tf_op jit(solution)/shard_map/ppermute | solution.py:339
  48.0 0.7 shard_map.79.refs_0_
  48.7 2.2 %collective-permute-start.13 = (f32[512,128]{1,0:T(8,128)S(1)}, f32[512,128]{1,0:T(8,128)S(1)}, u32[]{:S(2)}, u32[]{:S(2)}) collective-permute-start(f32[512,128]{1,0:T(8,128)S(1)} %shard_map.79.refs_0_), channel_id=1, source_target_pairs={{0,32},{32,0},{64,96},{96,64},{1,33},{33,1},{65,97},{97,65},{2,34}... | collective-permute-start | bytes 786440 | tf_op jit(solution)/shard_map/ppermute | solution.py:318
  50.9 1.9 %collective-permute-start.14 = (f32[512,128]{1,0:T(8,128)S(1)}, f32[512,128]{1,0:T(8,128)S(1)}, u32[]{:S(2)}, u32[]{:S(2)}) collective-permute-start(f32[512,128]{1,0:T(8,128)S(1)} %shard_map.79.refs_0_), channel_id=1, source_target_pairs={{0,96},{32,64},{64,32},{96,0},{1,97},{33,65},{65,33},{97,1},{2,98}... | collective-permute-start | bytes 786440 | tf_op jit(solution)/shard_map/ppermute | solution.py:318
  52.7 1.2 %collective-permute-start.15 = (f32[512,128]{1,0:T(8,128)S(1)}, f32[512,128]{1,0:T(8,128)S(1)}, u32[]{:S(2)}, u32[]{:S(2)}) collective-permute-start(f32[512,128]{1,0:T(8,128)S(1)} %shard_map.79.refs_0_), channel_id=1, source_target_pairs={{0,64},{32,96},{64,0},{96,32},{1,65},{33,97},{65,1},{97,33},{2,66}... | collective-permute-start | bytes 786440 | tf_op jit(solution)/shard_map/ppermute | solution.py:318
  53.9 1.3 %collective-permute-start.17 = (f32[32,128]{1,0:T(8,128)S(1)}, f32[32,128]{1,0:T(8,128)S(1)}, u32[]{:S(2)}, u32[]{:S(2)}) collective-permute-start(f32[32,128]{1,0:T(8,128)S(1)} %slice_add_fusion.shared_ref), channel_id=1, source_target_pairs={{0,1},{32,34},{4,2},{2,3},{64,68},{8,4},{36,37},{68,70},{40,38},{6... | collective-permute-start | bytes 49160 | tf_op jit(solution)/shard_map/ppermute | solution.py:341
  55.2 2.8 %collective-permute-done.13.refs_1_ = f32[512,128]{1,0:T(8,128)S(1)} collective-permute-done((f32[512,128]{1,0:T(8,128)S(1)}, f32[512,128]{1,0:T(8,128)S(1)}, u32[]{:S(2)}, u32[]{:S(2)}) %collective-permute-start.13) | collective-permute-done | bytes 262176 | tf_op jit(solution)/shard_map/ppermute | solution.py:318
  58.0 0.7 collective-permute-start.18
  58.6 7.0 %collective-permute-done.14.refs_2_ = f32[512,128]{1,0:T(8,128)S(1)} collective-permute-done((f32[512,128]{1,0:T(8,128)S(1)}, f32[512,128]{1,0:T(8,128)S(1)}, u32[]{:S(2)}, u32[]{:S(2)}) %collective-permute-start.14) | collective-permute-done | bytes 262176 | tf_op jit(solution)/shard_map/ppermute | solution.py:318
  65.6 1.2 %shard_map.80.refs_4_ = f32[544,128]{1,0:T(8,128)S(1)} custom-call(s32[2]{0:T(128)S(1)} %pad_add_fusion.pos, f32[3,128]{1,0:T(4,128)S(1)} %copy-done.6, f32[544,128]{1,0:T(8,128)S(1)} %add_add_fusion.a_ref, f32[544,128]{1,0:T(8,128)S(1)} %collective-permute-done.16.b_ref, f32[128,128]{1,0:T(8,128)S(1)} %copy-done.2, f32[32,128]{1,0:T(8,128)S(1)} %slice_add_fusion.shared_ref, ...), custom_call_target="tpu_custom_call" | custom-call | tf_op jit(solution)/shard_map/pallas_call | solution.py:321
  66.8 0.1 collective-permute-start.19
  66.9 1.1 %collective-permute-start.20 = (f32[544,128]{1,0:T(8,128)S(1)}, f32[544,128]{1,0:T(8,128)S(1)}, u32[]{:S(2)}, u32[]{:S(2)}) collective-permute-start(f32[544,128]{1,0:T(8,128)S(1)} %shard_map.80.refs_4_), channel_id=1, source_target_pairs={{0,96},{32,64},{64,32},{96,0},{1,97},{33,65},{65,33},{97,1},{2,98}... | collective-permute-start | bytes 835592 | tf_op jit(solution)/shard_map/ppermute | solution.py:318
  68.0 3.0 %collective-permute-start.21 = (f32[544,128]{1,0:T(8,128)S(1)}, f32[544,128]{1,0:T(8,128)S(1)}, u32[]{:S(2)}, u32[]{:S(2)}) collective-permute-start(f32[544,128]{1,0:T(8,128)S(1)} %shard_map.80.refs_4_), channel_id=1, source_target_pairs={{0,64},{32,96},{64,0},{96,32},{1,65},{33,97},{65,1},{97,33},{2,66}... | collective-permute-start | bytes 835592 | tf_op jit(solution)/shard_map/ppermute | solution.py:318
  71.0 5.5 %collective-permute-done.19.refs_5_ = f32[544,128]{1,0:T(8,128)S(1)} collective-permute-done((f32[544,128]{1,0:T(8,128)S(1)}, f32[544,128]{1,0:T(8,128)S(1)}, u32[]{:S(2)}, u32[]{:S(2)}) %collective-permute-start.19) | collective-permute-done | bytes 278560 | tf_op jit(solution)/shard_map/ppermute | solution.py:318
  76.5 5.7 %collective-permute-done.20.refs_6_ = f32[544,128]{1,0:T(8,128)S(1)} collective-permute-done((f32[544,128]{1,0:T(8,128)S(1)}, f32[544,128]{1,0:T(8,128)S(1)}, u32[]{:S(2)}, u32[]{:S(2)}) %collective-permute-start.20) | collective-permute-done | bytes 278560 | tf_op jit(solution)/shard_map/ppermute | solution.py:318
  82.2 2.2 %shard_map.81 = f32[16,16,16,128]{3,2,1,0:T(8,128)} custom-call(s32[2]{0:T(128)S(1)} %pad_add_fusion.pos, f32[512,128]{1,0:T(8,128)S(1)} %shard_map.79.refs_0_, f32[512,128]{1,0:T(8,128)S(1)} %collective-permute-done.13.refs_1_, f32[512,128]{1,0:T(8,128)S(1)} %collective-permute-done.14.refs_2_, f32[512,128]{1,0:T(8,128)S(1)} %collective-permute-done.15.refs_3_, ...), custom_call_target="tpu_custom_call" | custom-call | tf_op jit(solution)/shard_map/pallas_call | solution.py:365
  (24 shorter events, 0.1 us)
Async XLA Ops:
  0.0 4.9 %copy-start.3 = (s32[1,4]{1,0:T(1,128)S(1)}, s32[1,4]{1,0:T(1,128)}, u32[]{:S(2)}) copy-start(s32[1,4]{1,0:T(1,128)} %lev.9) | copy-start | bytes 52
  0.0 4.9 %copy-start.4 = (f32[4]{0:T(128)S(1)}, f32[4]{0:T(128)}, u32[]{:S(2)}) copy-start(f32[4]{0:T(128)} %vel.9) | copy-start | bytes 52
  0.0 4.9 %copy-start.5 = (f32[4]{0:T(128)S(1)}, f32[4]{0:T(128)}, u32[]{:S(2)}) copy-start(f32[4]{0:T(128)} %dif.9) | copy-start | bytes 52
  0.0 1.6 %copy-start = (f32[1,16,16,16,128]{4,3,2,1,0:T(8,128)S(1)}, f32[1,16,16,16,128]{4,3,2,1,0:T(8,128)}, u32[]{:S(2)}) copy-start(f32[1,16,16,16,128]{4,3,2,1,0:T(8,128)} %param.7) | copy-start | bytes 6291460
  1.6 3.3 %copy-start.1 = (f32[1,16,16,16,128]{4,3,2,1,0:T(8,128)S(1)}, f32[1,16,16,16,128]{4,3,2,1,0:T(8,128)}, u32[]{:S(2)}) copy-start(f32[1,16,16,16,128]{4,3,2,1,0:T(8,128)} %param.7) | copy-start | bytes 6291460
  2.4 5.4 %collective-permute-start = (f32[2,16,256]{2,1,0:T(8,128)S(1)}, f32[2,16,256]{2,1,0:T(8,128)S(1)}, u32[]{:S(2)}, u32[]{:S(2)}) collective-permute-start(f32[2,16,256]{2,1,0:T(8,128)S(1)} %get-tuple-element.38.hi_ref), channel_id=1, source_target_pairs={{0,1},{1,2},{2,3},{3,4},{4,5},{5,6},{6,7},{7,8},{8,9},{9,10},{10,1... | collective-permute-start | bytes 98312 | tf_op jit(solution)/shard_map/ppermute | solution.py:286
  2.5 5.3 %collective-permute-start.1 = (f32[3,16,256]{2,1,0:T(8,128)S(1)}, f32[3,16,256]{2,1,0:T(8,128)S(1)}, u32[]{:S(2)}, u32[]{:S(2)}) collective-permute-start(f32[3,16,256]{2,1,0:T(8,128)S(1)} %get-tuple-element.37.lo_ref), channel_id=1, source_target_pairs={{0,31},{1,0},{2,1},{3,2},{4,3},{5,4},{6,5},{7,6},{8,7},{9,8},{10,9... | collective-permute-start | bytes 147464 | tf_op jit(solution)/shard_map/ppermute | solution.py:287
  9.8 11.8 %collective-permute-start.4 = (f32[304,128]{1,0:T(8,128)S(1)}, f32[304,128]{1,0:T(8,128)S(1)}, u32[]{:S(2)}, u32[]{:S(2)}) collective-permute-start(f32[304,128]{1,0:T(8,128)S(1)} %get-tuple-element.50), channel_id=1, source_target_pairs={{0,64},{32,96},{64,0},{96,32},{1,65},{33,97},{65,1},{97,33},{2,66}... | collective-permute-start | bytes 466952 | tf_op jit(solution)/shard_map/ppermute | solution.py:318
  13.1 8.7 %collective-permute-start.3 = (f32[304,128]{1,0:T(8,128)S(1)}, f32[304,128]{1,0:T(8,128)S(1)}, u32[]{:S(2)}, u32[]{:S(2)}) collective-permute-start(f32[304,128]{1,0:T(8,128)S(1)} %get-tuple-element.49), channel_id=1, source_target_pairs={{0,96},{32,64},{64,32},{96,0},{1,97},{33,65},{65,33},{97,1},{2,98}... | collective-permute-start | bytes 466952 | tf_op jit(solution)/shard_map/ppermute | solution.py:318
  14.2 7.7 %collective-permute-start.2 = (f32[304,128]{1,0:T(8,128)S(1)}, f32[304,128]{1,0:T(8,128)S(1)}, u32[]{:S(2)}, u32[]{:S(2)}) collective-permute-start(f32[304,128]{1,0:T(8,128)S(1)} %get-tuple-element.48), channel_id=1, source_target_pairs={{0,32},{32,0},{64,96},{96,64},{1,33},{33,1},{65,97},{97,65},{2,34}... | collective-permute-start | bytes 466952 | tf_op jit(solution)/shard_map/ppermute | solution.py:318
  15.2 11.4 %collective-permute-start.8 = (f32[272,128]{1,0:T(8,128)S(1)}, f32[272,128]{1,0:T(8,128)S(1)}, u32[]{:S(2)}, u32[]{:S(2)}) collective-permute-start(f32[272,128]{1,0:T(8,128)S(1)} %get-tuple-element.58), channel_id=1, source_target_pairs={{0,64},{32,96},{64,0},{96,32},{1,65},{33,97},{65,1},{97,33},{2,66}... | collective-permute-start | bytes 417800 | tf_op jit(solution)/shard_map/ppermute | solution.py:318
  18.9 10.4 %collective-permute-start.7 = (f32[272,128]{1,0:T(8,128)S(1)}, f32[272,128]{1,0:T(8,128)S(1)}, u32[]{:S(2)}, u32[]{:S(2)}) collective-permute-start(f32[272,128]{1,0:T(8,128)S(1)} %get-tuple-element.57), channel_id=1, source_target_pairs={{0,96},{32,64},{64,32},{96,0},{1,97},{33,65},{65,33},{97,1},{2,98}... | collective-permute-start | bytes 417800 | tf_op jit(solution)/shard_map/ppermute | solution.py:318
  19.9 28.0 %copy-start.2 = (f32[128,128]{1,0:T(8,128)S(1)}, f32[128,128]{1,0:T(8,128)}, u32[]{:S(2)}) copy-start(f32[128,128]{1,0:T(8,128)} %constant.23.clone.mat_ref) | copy-start | bytes 196612
  21.6 44.0 %copy-start.6 = (f32[3,128]{1,0:T(4,128)S(1)}, f32[3,128]{1,0:T(4,128)}, u32[]{:S(2)}) copy-start(f32[3,128]{1,0:T(4,128)} %constant.24.clone.table) | copy-start | bytes 4612
  21.7 7.6 %collective-permute-start.6 = (f32[272,128]{1,0:T(8,128)S(1)}, f32[272,128]{1,0:T(8,128)S(1)}, u32[]{:S(2)}, u32[]{:S(2)}) collective-permute-start(f32[272,128]{1,0:T(8,128)S(1)} %get-tuple-element.56), channel_id=1, source_target_pairs={{0,32},{32,0},{64,96},{96,64},{1,33},{33,1},{65,97},{97,65},{2,34}... | collective-permute-start | bytes 417800 | tf_op jit(solution)/shard_map/ppermute | solution.py:318
  21.9 14.1 %collective-permute-start.12 = (f32[544,128]{1,0:T(8,128)S(1)}, f32[544,128]{1,0:T(8,128)S(1)}, u32[]{:S(2)}, u32[]{:S(2)}) collective-permute-start(f32[544,128]{1,0:T(8,128)S(1)} %get-tuple-element.66), channel_id=1, source_target_pairs={{0,64},{32,96},{64,0},{96,32},{1,65},{33,97},{65,1},{97,33},{2,66}... | collective-permute-start | bytes 835592 | tf_op jit(solution)/shard_map/ppermute | solution.py:318
  25.5 14.6 %collective-permute-start.11 = (f32[544,128]{1,0:T(8,128)S(1)}, f32[544,128]{1,0:T(8,128)S(1)}, u32[]{:S(2)}, u32[]{:S(2)}) collective-permute-start(f32[544,128]{1,0:T(8,128)S(1)} %get-tuple-element.65), channel_id=1, source_target_pairs={{0,96},{32,64},{64,32},{96,0},{1,97},{33,65},{65,33},{97,1},{2,98}... | collective-permute-start | bytes 835592 | tf_op jit(solution)/shard_map/ppermute | solution.py:318
  26.6 13.6 %collective-permute-start.10 = (f32[544,128]{1,0:T(8,128)S(1)}, f32[544,128]{1,0:T(8,128)S(1)}, u32[]{:S(2)}, u32[]{:S(2)}) collective-permute-start(f32[544,128]{1,0:T(8,128)S(1)} %get-tuple-element.64), channel_id=1, source_target_pairs={{0,32},{32,0},{64,96},{96,64},{1,33},{33,1},{65,97},{97,65},{2,34}... | collective-permute-start | bytes 835592 | tf_op jit(solution)/shard_map/ppermute | solution.py:318
  29.3 16.2 %collective-permute-start.9 = (f32[272,128]{1,0:T(8,128)S(1)}, f32[272,128]{1,0:T(8,128)S(1)}, u32[]{:S(2)}, u32[]{:S(2)}) collective-permute-start(f32[272,128]{1,0:T(8,128)S(1)} %add_add_fusion.2.c_ref), channel_id=1, source_target_pairs={{0,128},{128,0},{1,129},{129,1},{2,130},{130,2},{3,131},{131,3},{4... | collective-permute-start | bytes 417800 | tf_op jit(solution)/shard_map/ppermute | solution.py:339
  32.8 15.2 %collective-permute-start.5 = (f32[304,128]{1,0:T(8,128)S(1)}, f32[304,128]{1,0:T(8,128)S(1)}, u32[]{:S(2)}, u32[]{:S(2)}) collective-permute-start(f32[304,128]{1,0:T(8,128)S(1)} %add_add_fusion.1.a_ref), channel_id=1, source_target_pairs={{0,128},{128,0},{1,129},{129,1},{2,130},{130,2},{3,131},{131,3},{4... | collective-permute-start | bytes 466952 | tf_op jit(solution)/shard_map/ppermute | solution.py:339
  40.3 25.3 %collective-permute-start.16 = (f32[544,128]{1,0:T(8,128)S(1)}, f32[544,128]{1,0:T(8,128)S(1)}, u32[]{:S(2)}, u32[]{:S(2)}) collective-permute-start(f32[544,128]{1,0:T(8,128)S(1)} %add_add_fusion.a_ref), channel_id=1, source_target_pairs={{0,128},{128,0},{1,129},{129,1},{2,130},{130,2},{3,131},{131,3},{4... | collective-permute-start | bytes 835592 | tf_op jit(solution)/shard_map/ppermute | solution.py:339
  48.7 9.3 %collective-permute-start.13 = (f32[512,128]{1,0:T(8,128)S(1)}, f32[512,128]{1,0:T(8,128)S(1)}, u32[]{:S(2)}, u32[]{:S(2)}) collective-permute-start(f32[512,128]{1,0:T(8,128)S(1)} %shard_map.79.refs_0_), channel_id=1, source_target_pairs={{0,32},{32,0},{64,96},{96,64},{1,33},{33,1},{65,97},{97,65},{2,34}... | collective-permute-start | bytes 786440 | tf_op jit(solution)/shard_map/ppermute | solution.py:318
  50.9 14.7 %collective-permute-start.14 = (f32[512,128]{1,0:T(8,128)S(1)}, f32[512,128]{1,0:T(8,128)S(1)}, u32[]{:S(2)}, u32[]{:S(2)}) collective-permute-start(f32[512,128]{1,0:T(8,128)S(1)} %shard_map.79.refs_0_), channel_id=1, source_target_pairs={{0,96},{32,64},{64,32},{96,0},{1,97},{33,65},{65,33},{97,1},{2,98}... | collective-permute-start | bytes 786440 | tf_op jit(solution)/shard_map/ppermute | solution.py:318
  52.7 12.9 %collective-permute-start.15 = (f32[512,128]{1,0:T(8,128)S(1)}, f32[512,128]{1,0:T(8,128)S(1)}, u32[]{:S(2)}, u32[]{:S(2)}) collective-permute-start(f32[512,128]{1,0:T(8,128)S(1)} %shard_map.79.refs_0_), channel_id=1, source_target_pairs={{0,64},{32,96},{64,0},{96,32},{1,65},{33,97},{65,1},{97,33},{2,66}... | collective-permute-start | bytes 786440 | tf_op jit(solution)/shard_map/ppermute | solution.py:318
  53.9 11.7 %collective-permute-start.17 = (f32[32,128]{1,0:T(8,128)S(1)}, f32[32,128]{1,0:T(8,128)S(1)}, u32[]{:S(2)}, u32[]{:S(2)}) collective-permute-start(f32[32,128]{1,0:T(8,128)S(1)} %slice_add_fusion.shared_ref), channel_id=1, source_target_pairs={{0,1},{32,34},{4,2},{2,3},{64,68},{8,4},{36,37},{68,70},{40,38},{6... | collective-permute-start | bytes 49160 | tf_op jit(solution)/shard_map/ppermute | solution.py:341
  58.0 7.6 %collective-permute-start.18 = (f32[32,128]{1,0:T(8,128)S(1)}, f32[32,128]{1,0:T(8,128)S(1)}, u32[]{:S(2)}, u32[]{:S(2)}) collective-permute-start(f32[32,128]{1,0:T(8,128)S(1)} %slice_add_fusion.shared_ref), channel_id=1, source_target_pairs={{8,12},{0,16},{16,18},{48,52},{80,88},{32,56},{24,28},{64,92},{96,... | collective-permute-start | bytes 49160 | tf_op jit(solution)/shard_map/ppermute | solution.py:341
  66.8 9.7 %collective-permute-start.19 = (f32[544,128]{1,0:T(8,128)S(1)}, f32[544,128]{1,0:T(8,128)S(1)}, u32[]{:S(2)}, u32[]{:S(2)}) collective-permute-start(f32[544,128]{1,0:T(8,128)S(1)} %shard_map.80.refs_4_), channel_id=1, source_target_pairs={{0,32},{32,0},{64,96},{96,64},{1,33},{33,1},{65,97},{97,65},{2,34}... | collective-permute-start | bytes 835592 | tf_op jit(solution)/shard_map/ppermute | solution.py:318
  66.9 15.3 %collective-permute-start.20 = (f32[544,128]{1,0:T(8,128)S(1)}, f32[544,128]{1,0:T(8,128)S(1)}, u32[]{:S(2)}, u32[]{:S(2)}) collective-permute-start(f32[544,128]{1,0:T(8,128)S(1)} %shard_map.80.refs_4_), channel_id=1, source_target_pairs={{0,96},{32,64},{64,32},{96,0},{1,97},{33,65},{65,33},{97,1},{2,98}... | collective-permute-start | bytes 835592 | tf_op jit(solution)/shard_map/ppermute | solution.py:318
  68.0 14.2 %collective-permute-start.21 = (f32[544,128]{1,0:T(8,128)S(1)}, f32[544,128]{1,0:T(8,128)S(1)}, u32[]{:S(2)}, u32[]{:S(2)}) collective-permute-start(f32[544,128]{1,0:T(8,128)S(1)} %shard_map.80.refs_4_), channel_id=1, source_target_pairs={{0,64},{32,96},{64,0},{96,32},{1,65},{33,97},{65,1},{97,33},{2,66}... | collective-permute-start | bytes 835592 | tf_op jit(solution)/shard_map/ppermute | solution.py:318

commit v6 on v5

--- a/solution.py
+++ b/solution.py
@@ -72,12 +72,13 @@
 def first_kernel(lev, vel, dif, x_ref, u_ref):
     fac = factors(lev, vel, dif)
 
-    def plane(p, _):
-        for i in range(16):
-            u_ref[p, i] = step_row(x_ref, p, i, fac)
+    def planes(k, _):
+        for j in range(4):
+            for i in range(16):
+                u_ref[4 * k + j, i] = step_row(x_ref, 4 * k + j, i, fac)
         return 0
 
-    lax.fori_loop(0, 16, plane, 0)
+    lax.fori_loop(0, 4, planes, 0)
 
 
 def layer_step(u, below, above, center, lo, hi):
@@ -116,19 +117,21 @@
 
 
 def second_kernel(chunk, lev, vel, dif, wgt, pos, u_ref, edge_ref, shared_ref, *outs):
-    fac = factors(lev, vel, dif)
     weight = wgt[0].astype(F32)
+    center, lo, hi = factors(lev, vel, dif)
+    fac = (weight * center, [weight * v for v in lo], [weight * v for v in hi])
     for target, out_ref in zip(partners(pos[0]), outs):
 
         def body(r, _, target=target, out_ref=out_ref):
             p = 4 * target + CHUNKS[chunk][0] + r
             base = pl.multiple_of(272 * r, 16)
             for i in range(16):
-                out_ref[pl.ds(base + 16 * i, 16), :] = weight * step_row(u_ref, p, i, fac)
+                out_ref[pl.ds(base + 16 * i, 16), :] = step_row(u_ref, p, i, fac)
             out_ref[pl.ds(base + 256, 16), :] = edge_ref[pl.ds(pl.multiple_of(16 * p, 16), 16), :]
             return 0
 
-        lax.fori_loop(0, CHUNKS[chunk][1], body, 0)
+        for r in range(CHUNKS[chunk][1]):
+            body(r, 0)
         if chunk == 0:
             out_ref[272 * CHUNKS[0][1] :] = shared_ref[...]
 
@@ -334,6 +337,8 @@
         parts = second(c, value)
         value = after(u, parts[0])
         got = to_others(after(parts[1:], *gate))
+        if c == 1:
+            got = after(got, partner[0])
         summed.append(parts[0] + got[0] + got[1] + got[2])
         gate = (summed[0],) if c else ()
         partner.append(lax.ppermute(summed[c], "zh", pair))

time: 84.7 us -> 82.7 us (0.976)
  the two profiles are of different devices: /device:TPU:96 before, /device:TPU:4 now
where the time goes in v6:
time: 82.7 us; the launch traced here: 81.1 us
  starting transfers between devices  42.9 us (52%)
  waiting for transfers between devices  24 us (29%)
  Pallas kernels  11.4 us (14%)
  local copies, waits for them, and re-layouts  1.64 us (2%)
  between operations  1 us (1%)
    ppermute x15, starting transfers between devices, to_others(): lax.ppermute(value, 'y', perm)  23 us
    ppermute x15, waiting for transfers between devices, to_others(): lax.ppermute(value, 'y', perm)  20.2 us
    ppermute x3, starting transfers between devices, local(): partner.append(lax.ppermute(summed[c], 'zh', pair))  10.5 us
    ppermute x2, starting transfers between devices, local(): got = [lax.ppermute(shared, ('y',) + BRICK, r) for r in rounds]  4.86 us
    ppermute x1, starting transfers between devices, local(): right = lax.ppermute(lo, BRICK, down)  4.43 us
    pallas_call x3, Pallas kernels, second(): pl.pallas_call(functools.partial(second_kernel, c), out_shape=(struct(272...  3.42 us
    pallas_call x1, Pallas kernels, local(): pl.pallas_call(last_kernel, out_shape=struct(16, 16, 16, 128), in_specs=[...  2.17 us
    pallas_call x1, Pallas kernels, local(): pl.pallas_call(first_kernel, out_shape=struct(*x.shape), in_specs=[SM] *...  2.15 us
  transfers between devices with their start and end apart: 22, of which 11 were waited for; matrix products, arithmetic and copies ran while one was open for 0% of the time, Pallas kernels for 7%

profile of v6, /device:TPU:4, one launch (start us, length us, event | category | flops | bytes accessed | tf_op | source)
XLA Modules:
  0.0 81.1 jit_solution(4411141266337497874)
XLA Ops:
  0.0 1.6 %copy-done = f32[1,16,16,16,128]{4,3,2,1,0:T(8,128)S(1)} copy-done((f32[1,16,16,16,128]{4,3,2,1,0:T(8,128)S(1)}, f32[1,16,16,16,128]{4,3,2,1,0:T(8,128)}, u32[]{:S(2)}) %copy-start) | copy-done | bytes 2097176
  1.6 0.7 shard_map.74
  2.4 0.1 collective-permute-start
  2.5 4.4 %collective-permute-start.1 = (f32[3,16,256]{2,1,0:T(8,128)S(1)}, f32[3,16,256]{2,1,0:T(8,128)S(1)}, u32[]{:S(2)}, u32[]{:S(2)}) collective-permute-start(f32[3,16,256]{2,1,0:T(8,128)S(1)} %get-tuple-element.40.lo_ref), channel_id=1, source_target_pairs={{0,31},{1,0},{2,1},{3,2},{4,3},{5,4},{6,5},{7,6},{8,7},{9,8},{10,9... | collective-permute-start | bytes 147464 | tf_op jit(solution)/shard_map/ppermute | solution.py:290
  6.9 0.1 pad_add_fusion.pos
  7.7 2.2 %shard_map.73.u_ref = f32[16,16,16,128]{3,2,1,0:T(8,128)S(1)} custom-call(s32[1,4]{1,0:T(1,128)S(1)} %copy-done.3, f32[4]{0:T(128)S(1)} %copy-done.4, f32[4]{0:T(128)S(1)} %copy-done.5, f32[16,16,16,128]{3,2,1,0:T(8,128)S(1)} %bitcast.4), custom_call_target="tpu_custom_call" | custom-call | flops 10000000 | bytes 4194304 | tf_op jit(solution)/shard_map/pallas_call | solution.py:292
  9.8 0.0 collective-permute-done.left_ref
  9.8 1.0 %shard_map.75 = (f32[256,128]{1,0:T(8,128)S(1)}, f32[32,128]{1,0:T(8,128)S(1)}) custom-call(s32[1,4]{1,0:T(1,128)S(1)} %copy-done.3, f32[4]{0:T(128)S(1)} %copy-done.4, f32[4]{0:T(128)S(1)} %copy-done.5, s32[1]{0:T(128)S(6)} %copy.8.wgt, s32[2]{0:T(128)S(1)} %pad_add_fusion.pos, f32[3,16,256]{2,1,0:T(8,128)S(1)} %get-tuple-element.40.lo_ref, ...), custom_call_target="tpu_custom_call" | custom-call | tf_op jit(solution)/shard_map/pallas_call | solution.py:301
  10.9 1.0 %shard_map.76 = (f32[304,128]{1,0:T(8,128)S(1)}, f32[304,128]{1,0:T(8,128)S(1)}, f32[304,128]{1,0:T(8,128)S(1)}, f32[304,128]{1,0:T(8,128)S(1)}) custom-call(s32[1,4]{1,0:T(1,128)S(1)} %copy-done.3, f32[4]{0:T(128)S(1)} %copy-done.4, f32[4]{0:T(128)S(1)} %copy-done.5, s32[1]{0:T(128)S(6)} %copy.8.wgt, s32[2]{0:T(128)S(1)} %pad_add_fusion.pos, ...), custom_call_target="tpu_custom_call" | custom-call | flops 10000000 | bytes 4194304 | tf_op jit(solution)/shard_map/pallas_call | solution.py:311
  11.9 3.3 %collective-permute-start.4 = (f32[304,128]{1,0:T(8,128)S(1)}, f32[304,128]{1,0:T(8,128)S(1)}, u32[]{:S(2)}, u32[]{:S(2)}) collective-permute-start(f32[304,128]{1,0:T(8,128)S(1)} %get-tuple-element.53), channel_id=1, source_target_pairs={{0,64},{32,96},{64,0},{96,32},{1,65},{33,97},{65,1},{97,33},{2,66}... | collective-permute-start | bytes 466952 | tf_op jit(solution)/shard_map/ppermute | solution.py:321
  15.2 1.1 %collective-permute-start.3 = (f32[304,128]{1,0:T(8,128)S(1)}, f32[304,128]{1,0:T(8,128)S(1)}, u32[]{:S(2)}, u32[]{:S(2)}) collective-permute-start(f32[304,128]{1,0:T(8,128)S(1)} %get-tuple-element.52), channel_id=1, source_target_pairs={{0,96},{32,64},{64,32},{96,0},{1,97},{33,65},{65,33},{97,1},{2,98}... | collective-permute-start | bytes 466952 | tf_op jit(solution)/shard_map/ppermute | solution.py:321
  16.2 1.0 %shard_map.77 = (f32[272,128]{1,0:T(8,128)S(1)}, f32[272,128]{1,0:T(8,128)S(1)}, f32[272,128]{1,0:T(8,128)S(1)}, f32[272,128]{1,0:T(8,128)S(1)}) custom-call(s32[1,4]{1,0:T(1,128)S(1)} %copy-done.3, f32[4]{0:T(128)S(1)} %copy-done.4, f32[4]{0:T(128)S(1)} %copy-done.5, s32[1]{0:T(128)S(6)} %copy.8.wgt, s32[2]{0:T(128)S(1)} %pad_add_fusion.pos, ...), custom_call_target="tpu_custom_call" | custom-call | flops 10000000 | bytes 4194304 | tf_op jit(solution)/shard_map/pallas_call | solution.py:311
  17.2 2.1 %collective-permute-start.6 = (f32[272,128]{1,0:T(8,128)S(1)}, f32[272,128]{1,0:T(8,128)S(1)}, u32[]{:S(2)}, u32[]{:S(2)}) collective-permute-start(f32[272,128]{1,0:T(8,128)S(1)} %get-tuple-element.59), channel_id=1, source_target_pairs={{0,32},{32,0},{64,96},{96,64},{1,33},{33,1},{65,97},{97,65},{2,34}... | collective-permute-start | bytes 417800 | tf_op jit(solution)/shard_map/ppermute | solution.py:321
  19.4 2.2 %collective-permute-start.7 = (f32[272,128]{1,0:T(8,128)S(1)}, f32[272,128]{1,0:T(8,128)S(1)}, u32[]{:S(2)}, u32[]{:S(2)}) collective-permute-start(f32[272,128]{1,0:T(8,128)S(1)} %get-tuple-element.60), channel_id=1, source_target_pairs={{0,96},{32,64},{64,32},{96,0},{1,97},{33,65},{65,33},{97,1},{2,98}... | collective-permute-start | bytes 417800 | tf_op jit(solution)/shard_map/ppermute | solution.py:321
  21.5 1.8 %collective-permute-done.3 = f32[304,128]{1,0:T(8,128)S(1)} collective-permute-done((f32[304,128]{1,0:T(8,128)S(1)}, f32[304,128]{1,0:T(8,128)S(1)}, u32[]{:S(2)}, u32[]{:S(2)}) %collective-permute-start.3) | collective-permute-done | bytes 155680 | tf_op jit(solution)/shard_map/ppermute | solution.py:321
  23.4 0.2 collective-permute-done.2
  23.6 6.8 %collective-permute-start.5 = (f32[304,128]{1,0:T(8,128)S(1)}, f32[304,128]{1,0:T(8,128)S(1)}, u32[]{:S(2)}, u32[]{:S(2)}) collective-permute-start(f32[304,128]{1,0:T(8,128)S(1)} %add_add_fusion.1.a_ref), channel_id=1, source_target_pairs={{0,128},{128,0},{1,129},{129,1},{2,130},{130,2},{3,131},{131,3},{4... | collective-permute-start | bytes 466952 | tf_op jit(solution)/shard_map/ppermute | solution.py:344
  30.3 1.2 %collective-permute-start.8 = (f32[272,128]{1,0:T(8,128)S(1)}, f32[272,128]{1,0:T(8,128)S(1)}, u32[]{:S(2)}, u32[]{:S(2)}) collective-permute-start(f32[272,128]{1,0:T(8,128)S(1)} %get-tuple-element.61), channel_id=1, source_target_pairs={{0,64},{32,96},{64,0},{96,32},{1,65},{33,97},{65,1},{97,33},{2,66}... | collective-permute-start | bytes 417800 | tf_op jit(solution)/shard_map/ppermute | solution.py:321
  31.5 1.4 %shard_map.78 = (f32[544,128]{1,0:T(8,128)S(1)}, f32[544,128]{1,0:T(8,128)S(1)}, f32[544,128]{1,0:T(8,128)S(1)}, f32[544,128]{1,0:T(8,128)S(1)}) custom-call(s32[1,4]{1,0:T(1,128)S(1)} %copy-done.3, f32[4]{0:T(128)S(1)} %copy-done.4, f32[4]{0:T(128)S(1)} %copy-done.5, s32[1]{0:T(128)S(6)} %copy.8.wgt, s32[2]{0:T(128)S(1)} %pad_add_fusion.pos, ...), custom_call_target="tpu_custom_call" | custom-call | flops 10000000 | bytes 4194304 | tf_op jit(solution)/shard_map/pallas_call | solution.py:311
  33.0 2.4 %collective-permute-start.12 = (f32[544,128]{1,0:T(8,128)S(1)}, f32[544,128]{1,0:T(8,128)S(1)}, u32[]{:S(2)}, u32[]{:S(2)}) collective-permute-start(f32[544,128]{1,0:T(8,128)S(1)} %get-tuple-element.72), channel_id=1, source_target_pairs={{0,64},{32,96},{64,0},{96,32},{1,65},{33,97},{65,1},{97,33},{2,66}... | collective-permute-start | bytes 835592 | tf_op jit(solution)/shard_map/ppermute | solution.py:321
  35.4 2.2 %collective-permute-start.11 = (f32[544,128]{1,0:T(8,128)S(1)}, f32[544,128]{1,0:T(8,128)S(1)}, u32[]{:S(2)}, u32[]{:S(2)}) collective-permute-start(f32[544,128]{1,0:T(8,128)S(1)} %get-tuple-element.71), channel_id=1, source_target_pairs={{0,96},{32,64},{64,32},{96,0},{1,97},{33,65},{65,33},{97,1},{2,98}... | collective-permute-start | bytes 835592 | tf_op jit(solution)/shard_map/ppermute | solution.py:321
  37.6 0.0 collective-permute-done.7
  37.6 0.0 collective-permute-start.10
  37.6 0.5 collective-permute-done.8
  38.1 2.0 %collective-permute-start.9 = (f32[272,128]{1,0:T(8,128)S(1)}, f32[272,128]{1,0:T(8,128)S(1)}, u32[]{:S(2)}, u32[]{:S(2)}) collective-permute-start(f32[272,128]{1,0:T(8,128)S(1)} %add_add_fusion.2.c_ref), channel_id=1, source_target_pairs={{0,128},{128,0},{1,129},{129,1},{2,130},{130,2},{3,131},{131,3},{4... | collective-permute-start | bytes 417800 | tf_op jit(solution)/shard_map/ppermute | solution.py:344
  40.1 2.8 %collective-permute-done.12 = f32[544,128]{1,0:T(8,128)S(1)} collective-permute-done((f32[544,128]{1,0:T(8,128)S(1)}, f32[544,128]{1,0:T(8,128)S(1)}, u32[]{:S(2)}, u32[]{:S(2)}) %collective-permute-start.12) | collective-permute-done | bytes 278560 | tf_op jit(solution)/shard_map/ppermute | solution.py:321
  42.9 2.9 %collective-permute-done.11 = f32[544,128]{1,0:T(8,128)S(1)} collective-permute-done((f32[544,128]{1,0:T(8,128)S(1)}, f32[544,128]{1,0:T(8,128)S(1)}, u32[]{:S(2)}, u32[]{:S(2)}) %collective-permute-start.11) | collective-permute-done | bytes 278560 | tf_op jit(solution)/shard_map/ppermute | solution.py:321
  45.9 0.0 collective-permute-done.10
  45.9 0.1 add_add_fusion.a_ref
  45.9 1.7 %collective-permute-start.16 = (f32[544,128]{1,0:T(8,128)S(1)}, f32[544,128]{1,0:T(8,128)S(1)}, u32[]{:S(2)}, u32[]{:S(2)}) collective-permute-start(f32[544,128]{1,0:T(8,128)S(1)} %add_add_fusion.a_ref), channel_id=1, source_target_pairs={{0,128},{128,0},{1,129},{129,1},{2,130},{130,2},{3,131},{131,3},{4... | collective-permute-start | bytes 835592 | tf_op jit(solution)/shard_map/ppermute | solution.py:344
  47.6 1.8 %collective-permute-done.9.d_ref = f32[272,128]{1,0:T(8,128)S(1)} collective-permute-done((f32[272,128]{1,0:T(8,128)S(1)}, f32[272,128]{1,0:T(8,128)S(1)}, u32[]{:S(2)}, u32[]{:S(2)}) %collective-permute-start.9) | collective-permute-done | bytes 139296 | tf_op jit(solution)/shard_map/ppermute | solution.py:344
  49.4 0.7 shard_map.79.refs_0_
  50.1 0.3 collective-permute-start.13
  50.4 0.9 %collective-permute-start.14 = (f32[512,128]{1,0:T(8,128)S(1)}, f32[512,128]{1,0:T(8,128)S(1)}, u32[]{:S(2)}, u32[]{:S(2)}) collective-permute-start(f32[512,128]{1,0:T(8,128)S(1)} %shard_map.79.refs_0_), channel_id=1, source_target_pairs={{0,96},{32,64},{64,32},{96,0},{1,97},{33,65},{65,33},{97,1},{2,98}... | collective-permute-start | bytes 786440 | tf_op jit(solution)/shard_map/ppermute | solution.py:321
  51.4 3.1 %collective-permute-start.15 = (f32[512,128]{1,0:T(8,128)S(1)}, f32[512,128]{1,0:T(8,128)S(1)}, u32[]{:S(2)}, u32[]{:S(2)}) collective-permute-start(f32[512,128]{1,0:T(8,128)S(1)} %shard_map.79.refs_0_), channel_id=1, source_target_pairs={{0,64},{32,96},{64,0},{96,32},{1,65},{33,97},{65,1},{97,33},{2,66}... | collective-permute-start | bytes 786440 | tf_op jit(solution)/shard_map/ppermute | solution.py:321
  54.5 1.6 %collective-permute-start.17 = (f32[32,128]{1,0:T(8,128)S(1)}, f32[32,128]{1,0:T(8,128)S(1)}, u32[]{:S(2)}, u32[]{:S(2)}) collective-permute-start(f32[32,128]{1,0:T(8,128)S(1)} %slice_add_fusion.shared_ref), channel_id=1, source_target_pairs={{0,1},{32,34},{4,2},{2,3},{64,68},{8,4},{36,37},{68,70},{40,38},{6... | collective-permute-start | bytes 49160 | tf_op jit(solution)/shard_map/ppermute | solution.py:346
  56.2 2.4 %collective-permute-done.13.refs_1_ = f32[512,128]{1,0:T(8,128)S(1)} collective-permute-done((f32[512,128]{1,0:T(8,128)S(1)}, f32[512,128]{1,0:T(8,128)S(1)}, u32[]{:S(2)}, u32[]{:S(2)}) %collective-permute-start.13) | collective-permute-done | bytes 262176 | tf_op jit(solution)/shard_map/ppermute | solution.py:321
  58.6 3.2 %collective-permute-start.18 = (f32[32,128]{1,0:T(8,128)S(1)}, f32[32,128]{1,0:T(8,128)S(1)}, u32[]{:S(2)}, u32[]{:S(2)}) collective-permute-start(f32[32,128]{1,0:T(8,128)S(1)} %slice_add_fusion.shared_ref), channel_id=1, source_target_pairs={{8,12},{0,16},{16,18},{48,52},{80,88},{32,56},{24,28},{64,92},{96,... | collective-permute-start | bytes 49160 | tf_op jit(solution)/shard_map/ppermute | solution.py:346
  61.8 1.9 %collective-permute-done.14.refs_2_ = f32[512,128]{1,0:T(8,128)S(1)} collective-permute-done((f32[512,128]{1,0:T(8,128)S(1)}, f32[512,128]{1,0:T(8,128)S(1)}, u32[]{:S(2)}, u32[]{:S(2)}) %collective-permute-start.14) | collective-permute-done | bytes 262176 | tf_op jit(solution)/shard_map/ppermute | solution.py:321
  63.7 0.0 collective-permute-done.15.refs_3_
  63.7 2.0 %collective-permute-done.18.rest_1_ = f32[32,128]{1,0:T(8,128)S(1)} collective-permute-done((f32[32,128]{1,0:T(8,128)S(1)}, f32[32,128]{1,0:T(8,128)S(1)}, u32[]{:S(2)}, u32[]{:S(2)}) %collective-permute-start.18) | collective-permute-done | bytes 16416 | tf_op jit(solution)/shard_map/ppermute | solution.py:346
  65.7 1.2 %shard_map.80.refs_4_ = f32[544,128]{1,0:T(8,128)S(1)} custom-call(s32[2]{0:T(128)S(1)} %pad_add_fusion.pos, f32[3,128]{1,0:T(4,128)S(1)} %copy-done.6, f32[544,128]{1,0:T(8,128)S(1)} %add_add_fusion.a_ref, f32[544,128]{1,0:T(8,128)S(1)} %collective-permute-done.16.b_ref, f32[128,128]{1,0:T(8,128)S(1)} %copy-done.2, f32[32,128]{1,0:T(8,128)S(1)} %slice_add_fusion.shared_ref, ...), custom_call_target="tpu_custom_call" | custom-call | tf_op jit(solution)/shard_map/pallas_call | solution.py:324
  66.9 0.1 collective-permute-start.19
  67.0 0.1 collective-permute-start.20
  67.1 4.0 %collective-permute-start.21 = (f32[544,128]{1,0:T(8,128)S(1)}, f32[544,128]{1,0:T(8,128)S(1)}, u32[]{:S(2)}, u32[]{:S(2)}) collective-permute-start(f32[544,128]{1,0:T(8,128)S(1)} %shard_map.80.refs_4_), channel_id=1, source_target_pairs={{0,64},{32,96},{64,0},{96,32},{1,65},{33,97},{65,1},{97,33},{2,66}... | collective-permute-start | bytes 835592 | tf_op jit(solution)/shard_map/ppermute | solution.py:321
  71.1 3.4 %collective-permute-done.19.refs_5_ = f32[544,128]{1,0:T(8,128)S(1)} collective-permute-done((f32[544,128]{1,0:T(8,128)S(1)}, f32[544,128]{1,0:T(8,128)S(1)}, u32[]{:S(2)}, u32[]{:S(2)}) %collective-permute-start.19) | collective-permute-done | bytes 278560 | tf_op jit(solution)/shard_map/ppermute | solution.py:321
  74.5 4.3 %collective-permute-done.20.refs_6_ = f32[544,128]{1,0:T(8,128)S(1)} collective-permute-done((f32[544,128]{1,0:T(8,128)S(1)}, f32[544,128]{1,0:T(8,128)S(1)}, u32[]{:S(2)}, u32[]{:S(2)}) %collective-permute-start.20) | collective-permute-done | bytes 278560 | tf_op jit(solution)/shard_map/ppermute | solution.py:321
  78.8 2.2 %shard_map.81 = f32[16,16,16,128]{3,2,1,0:T(8,128)} custom-call(s32[2]{0:T(128)S(1)} %pad_add_fusion.pos, f32[512,128]{1,0:T(8,128)S(1)} %shard_map.79.refs_0_, f32[512,128]{1,0:T(8,128)S(1)} %collective-permute-done.13.refs_1_, f32[512,128]{1,0:T(8,128)S(1)} %collective-permute-done.14.refs_2_, f32[512,128]{1,0:T(8,128)S(1)} %collective-permute-done.15.refs_3_, ...), custom_call_target="tpu_custom_call" | custom-call | tf_op jit(solution)/shard_map/pallas_call | solution.py:370
  (24 shorter events, 0.1 us)
Async XLA Ops:
  0.0 7.6 %copy-start.3 = (s32[1,4]{1,0:T(1,128)S(1)}, s32[1,4]{1,0:T(1,128)}, u32[]{:S(2)}) copy-start(s32[1,4]{1,0:T(1,128)} %lev.9) | copy-start | bytes 52
  0.0 7.6 %copy-start.4 = (f32[4]{0:T(128)S(1)}, f32[4]{0:T(128)}, u32[]{:S(2)}) copy-start(f32[4]{0:T(128)} %vel.9) | copy-start | bytes 52
  0.0 7.6 %copy-start.5 = (f32[4]{0:T(128)S(1)}, f32[4]{0:T(128)}, u32[]{:S(2)}) copy-start(f32[4]{0:T(128)} %dif.9) | copy-start | bytes 52
  0.0 1.6 %copy-start = (f32[1,16,16,16,128]{4,3,2,1,0:T(8,128)S(1)}, f32[1,16,16,16,128]{4,3,2,1,0:T(8,128)}, u32[]{:S(2)}) copy-start(f32[1,16,16,16,128]{4,3,2,1,0:T(8,128)} %param.7) | copy-start | bytes 6291460
  1.6 6.0 %copy-start.1 = (f32[1,16,16,16,128]{4,3,2,1,0:T(8,128)S(1)}, f32[1,16,16,16,128]{4,3,2,1,0:T(8,128)}, u32[]{:S(2)}) copy-start(f32[1,16,16,16,128]{4,3,2,1,0:T(8,128)} %param.7) | copy-start | bytes 6291460
  2.4 7.5 %collective-permute-start = (f32[2,16,256]{2,1,0:T(8,128)S(1)}, f32[2,16,256]{2,1,0:T(8,128)S(1)}, u32[]{:S(2)}, u32[]{:S(2)}) collective-permute-start(f32[2,16,256]{2,1,0:T(8,128)S(1)} %get-tuple-element.41.hi_ref), channel_id=1, source_target_pairs={{0,1},{1,2},{2,3},{3,4},{4,5},{5,6},{6,7},{7,8},{8,9},{9,10},{10,1... | collective-permute-start | bytes 98312 | tf_op jit(solution)/shard_map/ppermute | solution.py:289
  2.5 7.4 %collective-permute-start.1 = (f32[3,16,256]{2,1,0:T(8,128)S(1)}, f32[3,16,256]{2,1,0:T(8,128)S(1)}, u32[]{:S(2)}, u32[]{:S(2)}) collective-permute-start(f32[3,16,256]{2,1,0:T(8,128)S(1)} %get-tuple-element.40.lo_ref), channel_id=1, source_target_pairs={{0,31},{1,0},{2,1},{3,2},{4,3},{5,4},{6,5},{7,6},{8,7},{9,8},{10,9... | collective-permute-start | bytes 147464 | tf_op jit(solution)/shard_map/ppermute | solution.py:290
  11.9 9.6 %collective-permute-start.4 = (f32[304,128]{1,0:T(8,128)S(1)}, f32[304,128]{1,0:T(8,128)S(1)}, u32[]{:S(2)}, u32[]{:S(2)}) collective-permute-start(f32[304,128]{1,0:T(8,128)S(1)} %get-tuple-element.53), channel_id=1, source_target_pairs={{0,64},{32,96},{64,0},{96,32},{1,65},{33,97},{65,1},{97,33},{2,66}... | collective-permute-start | bytes 466952 | tf_op jit(solution)/shard_map/ppermute | solution.py:321
  15.2 8.2 %collective-permute-start.3 = (f32[304,128]{1,0:T(8,128)S(1)}, f32[304,128]{1,0:T(8,128)S(1)}, u32[]{:S(2)}, u32[]{:S(2)}) collective-permute-start(f32[304,128]{1,0:T(8,128)S(1)} %get-tuple-element.52), channel_id=1, source_target_pairs={{0,96},{32,64},{64,32},{96,0},{1,97},{33,65},{65,33},{97,1},{2,98}... | collective-permute-start | bytes 466952 | tf_op jit(solution)/shard_map/ppermute | solution.py:321
  16.2 7.3 %collective-permute-start.2 = (f32[304,128]{1,0:T(8,128)S(1)}, f32[304,128]{1,0:T(8,128)S(1)}, u32[]{:S(2)}, u32[]{:S(2)}) collective-permute-start(f32[304,128]{1,0:T(8,128)S(1)} %get-tuple-element.51), channel_id=1, source_target_pairs={{0,32},{32,0},{64,96},{96,64},{1,33},{33,1},{65,97},{97,65},{2,34}... | collective-permute-start | bytes 466952 | tf_op jit(solution)/shard_map/ppermute | solution.py:321
  17.2 18.1 %collective-permute-start.6 = (f32[272,128]{1,0:T(8,128)S(1)}, f32[272,128]{1,0:T(8,128)S(1)}, u32[]{:S(2)}, u32[]{:S(2)}) collective-permute-start(f32[272,128]{1,0:T(8,128)S(1)} %get-tuple-element.59), channel_id=1, source_target_pairs={{0,32},{32,0},{64,96},{96,64},{1,33},{33,1},{65,97},{97,65},{2,34}... | collective-permute-start | bytes 417800 | tf_op jit(solution)/shard_map/ppermute | solution.py:321
  19.4 18.3 %collective-permute-start.7 = (f32[272,128]{1,0:T(8,128)S(1)}, f32[272,128]{1,0:T(8,128)S(1)}, u32[]{:S(2)}, u32[]{:S(2)}) collective-permute-start(f32[272,128]{1,0:T(8,128)S(1)} %get-tuple-element.60), channel_id=1, source_target_pairs={{0,96},{32,64},{64,32},{96,0},{1,97},{33,65},{65,33},{97,1},{2,98}... | collective-permute-start | bytes 417800 | tf_op jit(solution)/shard_map/ppermute | solution.py:321
  23.6 14.5 %collective-permute-start.5 = (f32[304,128]{1,0:T(8,128)S(1)}, f32[304,128]{1,0:T(8,128)S(1)}, u32[]{:S(2)}, u32[]{:S(2)}) collective-permute-start(f32[304,128]{1,0:T(8,128)S(1)} %add_add_fusion.1.a_ref), channel_id=1, source_target_pairs={{0,128},{128,0},{1,129},{129,1},{2,130},{130,2},{3,131},{131,3},{4... | collective-permute-start | bytes 466952 | tf_op jit(solution)/shard_map/ppermute | solution.py:344
  30.3 7.8 %collective-permute-start.8 = (f32[272,128]{1,0:T(8,128)S(1)}, f32[272,128]{1,0:T(8,128)S(1)}, u32[]{:S(2)}, u32[]{:S(2)}) collective-permute-start(f32[272,128]{1,0:T(8,128)S(1)} %get-tuple-element.61), channel_id=1, source_target_pairs={{0,64},{32,96},{64,0},{96,32},{1,65},{33,97},{65,1},{97,33},{2,66}... | collective-permute-start | bytes 417800 | tf_op jit(solution)/shard_map/ppermute | solution.py:321
  31.5 17.9 %copy-start.2 = (f32[128,128]{1,0:T(8,128)S(1)}, f32[128,128]{1,0:T(8,128)}, u32[]{:S(2)}) copy-start(f32[128,128]{1,0:T(8,128)} %constant.23.clone.mat_ref) | copy-start | bytes 196612
  31.5 34.2 %copy-start.6 = (f32[3,128]{1,0:T(4,128)S(1)}, f32[3,128]{1,0:T(4,128)}, u32[]{:S(2)}) copy-start(f32[3,128]{1,0:T(4,128)} %constant.24.clone.table) | copy-start | bytes 4612
  33.0 10.0 %collective-permute-start.12 = (f32[544,128]{1,0:T(8,128)S(1)}, f32[544,128]{1,0:T(8,128)S(1)}, u32[]{:S(2)}, u32[]{:S(2)}) collective-permute-start(f32[544,128]{1,0:T(8,128)S(1)} %get-tuple-element.72), channel_id=1, source_target_pairs={{0,64},{32,96},{64,0},{96,32},{1,65},{33,97},{65,1},{97,33},{2,66}... | collective-permute-start | bytes 835592 | tf_op jit(solution)/shard_map/ppermute | solution.py:321
  35.4 10.5 %collective-permute-start.11 = (f32[544,128]{1,0:T(8,128)S(1)}, f32[544,128]{1,0:T(8,128)S(1)}, u32[]{:S(2)}, u32[]{:S(2)}) collective-permute-start(f32[544,128]{1,0:T(8,128)S(1)} %get-tuple-element.71), channel_id=1, source_target_pairs={{0,96},{32,64},{64,32},{96,0},{1,97},{33,65},{65,33},{97,1},{2,98}... | collective-permute-start | bytes 835592 | tf_op jit(solution)/shard_map/ppermute | solution.py:321
  37.6 8.2 %collective-permute-start.10 = (f32[544,128]{1,0:T(8,128)S(1)}, f32[544,128]{1,0:T(8,128)S(1)}, u32[]{:S(2)}, u32[]{:S(2)}) collective-permute-start(f32[544,128]{1,0:T(8,128)S(1)} %get-tuple-element.70), channel_id=1, source_target_pairs={{0,32},{32,0},{64,96},{96,64},{1,33},{33,1},{65,97},{97,65},{2,34}... | collective-permute-start | bytes 835592 | tf_op jit(solution)/shard_map/ppermute | solution.py:321
  38.1 11.3 %collective-permute-start.9 = (f32[272,128]{1,0:T(8,128)S(1)}, f32[272,128]{1,0:T(8,128)S(1)}, u32[]{:S(2)}, u32[]{:S(2)}) collective-permute-start(f32[272,128]{1,0:T(8,128)S(1)} %add_add_fusion.2.c_ref), channel_id=1, source_target_pairs={{0,128},{128,0},{1,129},{129,1},{2,130},{130,2},{3,131},{131,3},{4... | collective-permute-start | bytes 417800 | tf_op jit(solution)/shard_map/ppermute | solution.py:344
  45.9 17.8 %collective-permute-start.16 = (f32[544,128]{1,0:T(8,128)S(1)}, f32[544,128]{1,0:T(8,128)S(1)}, u32[]{:S(2)}, u32[]{:S(2)}) collective-permute-start(f32[544,128]{1,0:T(8,128)S(1)} %add_add_fusion.a_ref), channel_id=1, source_target_pairs={{0,128},{128,0},{1,129},{129,1},{2,130},{130,2},{3,131},{131,3},{4... | collective-permute-start | bytes 835592 | tf_op jit(solution)/shard_map/ppermute | solution.py:344
  50.1 8.5 %collective-permute-start.13 = (f32[512,128]{1,0:T(8,128)S(1)}, f32[512,128]{1,0:T(8,128)S(1)}, u32[]{:S(2)}, u32[]{:S(2)}) collective-permute-start(f32[512,128]{1,0:T(8,128)S(1)} %shard_map.79.refs_0_), channel_id=1, source_target_pairs={{0,32},{32,0},{64,96},{96,64},{1,33},{33,1},{65,97},{97,65},{2,34}... | collective-permute-start | bytes 786440 | tf_op jit(solution)/shard_map/ppermute | solution.py:321
  50.4 13.3 %collective-permute-start.14 = (f32[512,128]{1,0:T(8,128)S(1)}, f32[512,128]{1,0:T(8,128)S(1)}, u32[]{:S(2)}, u32[]{:S(2)}) collective-permute-start(f32[512,128]{1,0:T(8,128)S(1)} %shard_map.79.refs_0_), channel_id=1, source_target_pairs={{0,96},{32,64},{64,32},{96,0},{1,97},{33,65},{65,33},{97,1},{2,98}... | collective-permute-start | bytes 786440 | tf_op jit(solution)/shard_map/ppermute | solution.py:321
  51.4 12.3 %collective-permute-start.15 = (f32[512,128]{1,0:T(8,128)S(1)}, f32[512,128]{1,0:T(8,128)S(1)}, u32[]{:S(2)}, u32[]{:S(2)}) collective-permute-start(f32[512,128]{1,0:T(8,128)S(1)} %shard_map.79.refs_0_), channel_id=1, source_target_pairs={{0,64},{32,96},{64,0},{96,32},{1,65},{33,97},{65,1},{97,33},{2,66}... | collective-permute-start | bytes 786440 | tf_op jit(solution)/shard_map/ppermute | solution.py:321
  54.5 9.2 %collective-permute-start.17 = (f32[32,128]{1,0:T(8,128)S(1)}, f32[32,128]{1,0:T(8,128)S(1)}, u32[]{:S(2)}, u32[]{:S(2)}) collective-permute-start(f32[32,128]{1,0:T(8,128)S(1)} %slice_add_fusion.shared_ref), channel_id=1, source_target_pairs={{0,1},{32,34},{4,2},{2,3},{64,68},{8,4},{36,37},{68,70},{40,38},{6... | collective-permute-start | bytes 49160 | tf_op jit(solution)/shard_map/ppermute | solution.py:346
  58.6 7.1 %collective-permute-start.18 = (f32[32,128]{1,0:T(8,128)S(1)}, f32[32,128]{1,0:T(8,128)S(1)}, u32[]{:S(2)}, u32[]{:S(2)}) collective-permute-start(f32[32,128]{1,0:T(8,128)S(1)} %slice_add_fusion.shared_ref), channel_id=1, source_target_pairs={{8,12},{0,16},{16,18},{48,52},{80,88},{32,56},{24,28},{64,92},{96,... | collective-permute-start | bytes 49160 | tf_op jit(solution)/shard_map/ppermute | solution.py:346
  66.9 7.6 %collective-permute-start.19 = (f32[544,128]{1,0:T(8,128)S(1)}, f32[544,128]{1,0:T(8,128)S(1)}, u32[]{:S(2)}, u32[]{:S(2)}) collective-permute-start(f32[544,128]{1,0:T(8,128)S(1)} %shard_map.80.refs_4_), channel_id=1, source_target_pairs={{0,32},{32,0},{64,96},{96,64},{1,33},{33,1},{65,97},{97,65},{2,34}... | collective-permute-start | bytes 835592 | tf_op jit(solution)/shard_map/ppermute | solution.py:321
  67.0 11.7 %collective-permute-start.20 = (f32[544,128]{1,0:T(8,128)S(1)}, f32[544,128]{1,0:T(8,128)S(1)}, u32[]{:S(2)}, u32[]{:S(2)}) collective-permute-start(f32[544,128]{1,0:T(8,128)S(1)} %shard_map.80.refs_4_), channel_id=1, source_target_pairs={{0,96},{32,64},{64,32},{96,0},{1,97},{33,65},{65,33},{97,1},{2,98}... | collective-permute-start | bytes 835592 | tf_op jit(solution)/shard_map/ppermute | solution.py:321
  67.1 11.6 %collective-permute-start.21 = (f32[544,128]{1,0:T(8,128)S(1)}, f32[544,128]{1,0:T(8,128)S(1)}, u32[]{:S(2)}, u32[]{:S(2)}) collective-permute-start(f32[544,128]{1,0:T(8,128)S(1)} %shard_map.80.refs_4_), channel_id=1, source_target_pairs={{0,64},{32,96},{64,0},{96,32},{1,65},{33,97},{65,1},{97,33},{2,66}... | collective-permute-start | bytes 835592 | tf_op jit(solution)/shard_map/ppermute | solution.py:321

commit v7 on v6

--- a/solution.py
+++ b/solution.py
@@ -160,15 +160,10 @@
     surplus_rows(1, c_ref, d_ref, mat_ref, o_ref, 256, packed_ref)
 
 
-def surplus_fix_kernel(pos, table, a_ref, b_ref, mat_ref, shared_ref, *rest):
-    got, (o_ref, packed_ref) = rest[:-2], rest[-2:]
+def surplus_fix_kernel(a_ref, b_ref, mat_ref, fix_ref, o_ref, packed_ref):
     packed_ref[...] = jnp.zeros_like(packed_ref)
     surplus_rows(2, a_ref, b_ref, mat_ref, o_ref, 0, packed_ref)
-    at = 32 * pos[0] + pos[1]
-    fix = table[len(got), at] * shared_ref[...]
-    for k, ref in enumerate(got):
-        fix = fix + table[k, at] * ref[...]
-    o_ref[512:] = fix
+    o_ref[512:] = fix_ref[...]
 
 
 def last_kernel(pos, *refs):
@@ -354,17 +349,10 @@
         matrix,
     )
     pieces0 = [own0] + to_others([own0] * 3)
+    factor = jnp.asarray(table)[:, 32 * pos[0] + pos[1]]
+    fix = factor[len(got)] * shared + sum(factor[k] * value for k, value in enumerate(got))
     own1 = surplus(
-        surplus_fix_kernel,
-        struct(544, 128),
-        pos,
-        jnp.asarray(table),
-        summed[2],
-        after(partner[2], *pieces0),
-        matrix,
-        shared,
-        *got,
-        scalar=2,
+        surplus_fix_kernel, struct(544, 128), summed[2], after(partner[2], *pieces0), matrix, fix
     )
     pieces1 = [own1] + to_others([own1] * 3)
     return pl.pallas_call(

time: 82.7 us -> 91.2 us (1.10); the launches traced: 81.1 us -> 91 us
  waiting for transfers between devices: 24 us -> 33.8 us
  starting transfers between devices: 42.9 us -> 39.4 us
  local copies, waits for them, and re-layouts: 1.64 us -> 3.85 us
  other arithmetic: 0.21 us -> 2.06 us
    ppermute x15, waiting for transfers between devices: 20.2 us -> 28 us  [to_others(): lax.ppermute(value, 'y', perm)]
    ppermute x3, waiting for transfers between devices: 1.79 us -> 5.81 us  [local(): partner.append(lax.ppermute(summed[c], 'zh', pair))]
    ppermute x15, starting transfers between devices: 23 us -> 20.7 us  [to_others(): lax.ppermute(value, 'y', perm)]
    ppermute x2, waiting for transfers between devices: 2.01 us -> 0.01 us  [local(): got = [lax.ppermute(shared, ('y',) + BRICK, r) for r in rounds]]
    add x0 -> x1, other arithmetic: none -> 1.82 us  [local(): factor[len(got)] * shared]
    unnamed x14, local copies, waits for them, and re-layouts: 1.64 us -> 3.23 us
    ppermute x2, starting transfers between devices: 4.86 us -> 3.72 us  [local(): got = [lax.ppermute(shared, ('y',) + BRICK, r) for r in rounds]]
  transfers between devices with their start and end apart: 22 -> 22, of which waited for: 11 -> 10; matrix products, arithmetic and copies ran while one was open for 0% -> 3% of each run, Pallas kernels for 7% -> 6%
where the time goes in v7:
time: 91.2 us; the launch traced here: 91 us
  starting transfers between devices  39.4 us (43%)
  waiting for transfers between devices  33.8 us (37%)
  Pallas kernels  10.8 us (12%)
  local copies, waits for them, and re-layouts  3.85 us (4%)
  other arithmetic  2.06 us (2%)
  between operations  1.04 us (1%)
    ppermute x15, waiting for transfers between devices, to_others(): lax.ppermute(value, 'y', perm)  28 us
    ppermute x15, starting transfers between devices, to_others(): lax.ppermute(value, 'y', perm)  20.7 us
    ppermute x3, starting transfers between devices, local(): partner.append(lax.ppermute(summed[c], 'zh', pair))  10.5 us
    ppermute x3, waiting for transfers between devices, local(): partner.append(lax.ppermute(summed[c], 'zh', pair))  5.81 us
    ppermute x1, starting transfers between devices, local(): right = lax.ppermute(lo, BRICK, down)  4.43 us
    ppermute x2, starting transfers between devices, local(): got = [lax.ppermute(shared, ('y',) + BRICK, r) for r in rounds]  3.72 us
    pallas_call x3, Pallas kernels, second(): pl.pallas_call(functools.partial(second_kernel, c), out_shape=(struct(272...  3.32 us
    unnamed x14, local copies, waits for them, and re-layouts  3.23 us
  transfers between devices with their start and end apart: 22, of which 10 were waited for; matrix products, arithmetic and copies ran while one was open for 3% of the time, Pallas kernels for 6%

profile of v7, /device:TPU:4, one launch (start us, length us, event | category | flops | bytes accessed | tf_op | source)
XLA Modules:
  0.0 91.0 jit_solution(6690575172660833264)
XLA Ops:
  0.0 1.6 %copy-done = f32[1,16,16,16,128]{4,3,2,1,0:T(8,128)S(1)} copy-done((f32[1,16,16,16,128]{4,3,2,1,0:T(8,128)S(1)}, f32[1,16,16,16,128]{4,3,2,1,0:T(8,128)}, u32[]{:S(2)}) %copy-start) | copy-done | bytes 2097176
  1.6 0.7 shard_map.74
  2.4 0.1 collective-permute-start
  2.5 4.4 %collective-permute-start.1 = (f32[3,16,256]{2,1,0:T(8,128)S(1)}, f32[3,16,256]{2,1,0:T(8,128)S(1)}, u32[]{:S(2)}, u32[]{:S(2)}) collective-permute-start(f32[3,16,256]{2,1,0:T(8,128)S(1)} %get-tuple-element.40.lo_ref), channel_id=1, source_target_pairs={{0,31},{1,0},{2,1},{3,2},{4,3},{5,4},{6,5},{7,6},{8,7},{9,8},{10,9... | collective-permute-start | bytes 147464 | tf_op jit(solution)/shard_map/ppermute | solution.py:285
  6.9 0.1 pad_add_fusion.pos
  7.7 1.6 %copy-done.1 = f32[1,16,16,16,128]{4,3,2,1,0:T(8,128)S(1)} copy-done((f32[1,16,16,16,128]{4,3,2,1,0:T(8,128)S(1)}, f32[1,16,16,16,128]{4,3,2,1,0:T(8,128)}, u32[]{:S(2)}) %copy-start.1) | copy-done | bytes 2097176
  9.2 2.2 %shard_map.73.u_ref = f32[16,16,16,128]{3,2,1,0:T(8,128)S(1)} custom-call(s32[1,4]{1,0:T(1,128)S(1)} %copy-done.3, f32[4]{0:T(128)S(1)} %copy-done.4, f32[4]{0:T(128)S(1)} %copy-done.5, f32[16,16,16,128]{3,2,1,0:T(8,128)S(1)} %bitcast.7), custom_call_target="tpu_custom_call" | custom-call | flops 10000000 | bytes 4194304 | tf_op jit(solution)/shard_map/pallas_call | solution.py:287
  11.5 1.0 %shard_map.75 = (f32[256,128]{1,0:T(8,128)S(1)}, f32[32,128]{1,0:T(8,128)S(1)}) custom-call(s32[1,4]{1,0:T(1,128)S(1)} %copy-done.3, f32[4]{0:T(128)S(1)} %copy-done.4, f32[4]{0:T(128)S(1)} %copy-done.5, s32[1]{0:T(128)S(6)} %copy.8.wgt, s32[2]{0:T(128)S(1)} %pad_add_fusion.pos, f32[3,16,256]{2,1,0:T(8,128)S(1)} %get-tuple-element.40.lo_ref, ...), custom_call_target="tpu_custom_call" | custom-call | tf_op jit(solution)/shard_map/pallas_call | solution.py:296
  12.6 1.0 %shard_map.76 = (f32[304,128]{1,0:T(8,128)S(1)}, f32[304,128]{1,0:T(8,128)S(1)}, f32[304,128]{1,0:T(8,128)S(1)}, f32[304,128]{1,0:T(8,128)S(1)}) custom-call(s32[1,4]{1,0:T(1,128)S(1)} %copy-done.3, f32[4]{0:T(128)S(1)} %copy-done.4, f32[4]{0:T(128)S(1)} %copy-done.5, s32[1]{0:T(128)S(6)} %copy.8.wgt, s32[2]{0:T(128)S(1)} %pad_add_fusion.pos, ...), custom_call_target="tpu_custom_call" | custom-call | flops 10000000 | bytes 4194304 | tf_op jit(solution)/shard_map/pallas_call | solution.py:306
  13.6 1.7 %collective-permute-start.2 = (f32[304,128]{1,0:T(8,128)S(1)}, f32[304,128]{1,0:T(8,128)S(1)}, u32[]{:S(2)}, u32[]{:S(2)}) collective-permute-start(f32[304,128]{1,0:T(8,128)S(1)} %get-tuple-element.51), channel_id=1, source_target_pairs={{0,32},{32,0},{64,96},{96,64},{1,33},{33,1},{65,97},{97,65},{2,34}... | collective-permute-start | bytes 466952 | tf_op jit(solution)/shard_map/ppermute | solution.py:316
  15.2 2.2 %collective-permute-start.3 = (f32[304,128]{1,0:T(8,128)S(1)}, f32[304,128]{1,0:T(8,128)S(1)}, u32[]{:S(2)}, u32[]{:S(2)}) collective-permute-start(f32[304,128]{1,0:T(8,128)S(1)} %get-tuple-element.52), channel_id=1, source_target_pairs={{0,96},{32,64},{64,32},{96,0},{1,97},{33,65},{65,33},{97,1},{2,98}... | collective-permute-start | bytes 466952 | tf_op jit(solution)/shard_map/ppermute | solution.py:316
  17.4 0.7 collective-permute-start.4
  18.1 2.1 %collective-permute-done.2 = f32[304,128]{1,0:T(8,128)S(1)} collective-permute-done((f32[304,128]{1,0:T(8,128)S(1)}, f32[304,128]{1,0:T(8,128)S(1)}, u32[]{:S(2)}, u32[]{:S(2)}) %collective-permute-start.2) | collective-permute-done | bytes 155680 | tf_op jit(solution)/shard_map/ppermute | solution.py:316
  20.3 1.8 %collective-permute-done.3 = f32[304,128]{1,0:T(8,128)S(1)} collective-permute-done((f32[304,128]{1,0:T(8,128)S(1)}, f32[304,128]{1,0:T(8,128)S(1)}, u32[]{:S(2)}, u32[]{:S(2)}) %collective-permute-start.3) | collective-permute-done | bytes 155680 | tf_op jit(solution)/shard_map/ppermute | solution.py:316
  22.1 2.1 %collective-permute-done.4 = f32[304,128]{1,0:T(8,128)S(1)} collective-permute-done((f32[304,128]{1,0:T(8,128)S(1)}, f32[304,128]{1,0:T(8,128)S(1)}, u32[]{:S(2)}, u32[]{:S(2)}) %collective-permute-start.4) | collective-permute-done | bytes 155680 | tf_op jit(solution)/shard_map/ppermute | solution.py:316
  24.2 7.3 %collective-permute-start.5 = (f32[304,128]{1,0:T(8,128)S(1)}, f32[304,128]{1,0:T(8,128)S(1)}, u32[]{:S(2)}, u32[]{:S(2)}) collective-permute-start(f32[304,128]{1,0:T(8,128)S(1)} %add_add_fusion.1.a_ref), channel_id=1, source_target_pairs={{0,128},{128,0},{1,129},{129,1},{2,130},{130,2},{3,131},{131,3},{4... | collective-permute-start | bytes 466952 | tf_op jit(solution)/shard_map/ppermute | solution.py:339
  31.5 1.0 %shard_map.77 = (f32[272,128]{1,0:T(8,128)S(1)}, f32[272,128]{1,0:T(8,128)S(1)}, f32[272,128]{1,0:T(8,128)S(1)}, f32[272,128]{1,0:T(8,128)S(1)}) custom-call(s32[1,4]{1,0:T(1,128)S(1)} %copy-done.3, f32[4]{0:T(128)S(1)} %copy-done.4, f32[4]{0:T(128)S(1)} %copy-done.5, s32[1]{0:T(128)S(6)} %copy.8.wgt, s32[2]{0:T(128)S(1)} %pad_add_fusion.pos, ...), custom_call_target="tpu_custom_call" | custom-call | flops 10000000 | bytes 4194304 | tf_op jit(solution)/shard_map/pallas_call | solution.py:306
  32.5 1.8 %collective-permute-start.6 = (f32[272,128]{1,0:T(8,128)S(1)}, f32[272,128]{1,0:T(8,128)S(1)}, u32[]{:S(2)}, u32[]{:S(2)}) collective-permute-start(f32[272,128]{1,0:T(8,128)S(1)} %get-tuple-element.59), channel_id=1, source_target_pairs={{0,32},{32,0},{64,96},{96,64},{1,33},{33,1},{65,97},{97,65},{2,34}... | collective-permute-start | bytes 417800 | tf_op jit(solution)/shard_map/ppermute | solution.py:316
  34.3 0.1 constant_dynamic-slice_fusion
  34.3 0.0 collective-permute-start.7
  34.4 2.4 %collective-permute-start.8 = (f32[272,128]{1,0:T(8,128)S(1)}, f32[272,128]{1,0:T(8,128)S(1)}, u32[]{:S(2)}, u32[]{:S(2)}) collective-permute-start(f32[272,128]{1,0:T(8,128)S(1)} %get-tuple-element.61), channel_id=1, source_target_pairs={{0,64},{32,96},{64,0},{96,32},{1,65},{33,97},{65,1},{97,33},{2,66}... | collective-permute-start | bytes 417800 | tf_op jit(solution)/shard_map/ppermute | solution.py:316
  36.7 1.4 %shard_map.78 = (f32[544,128]{1,0:T(8,128)S(1)}, f32[544,128]{1,0:T(8,128)S(1)}, f32[544,128]{1,0:T(8,128)S(1)}, f32[544,128]{1,0:T(8,128)S(1)}) custom-call(s32[1,4]{1,0:T(1,128)S(1)} %copy-done.3, f32[4]{0:T(128)S(1)} %copy-done.4, f32[4]{0:T(128)S(1)} %copy-done.5, s32[1]{0:T(128)S(6)} %copy.8.wgt, s32[2]{0:T(128)S(1)} %pad_add_fusion.pos, ...), custom_call_target="tpu_custom_call" | custom-call | flops 10000000 | bytes 4194304 | tf_op jit(solution)/shard_map/pallas_call | solution.py:306
  38.1 1.8 %collective-permute-start.10 = (f32[544,128]{1,0:T(8,128)S(1)}, f32[544,128]{1,0:T(8,128)S(1)}, u32[]{:S(2)}, u32[]{:S(2)}) collective-permute-start(f32[544,128]{1,0:T(8,128)S(1)} %get-tuple-element.70), channel_id=1, source_target_pairs={{0,32},{32,0},{64,96},{96,64},{1,33},{33,1},{65,97},{97,65},{2,34}... | collective-permute-start | bytes 835592 | tf_op jit(solution)/shard_map/ppermute | solution.py:316
  39.9 0.6 collective-permute-start.11
  40.5 2.5 %collective-permute-start.12 = (f32[544,128]{1,0:T(8,128)S(1)}, f32[544,128]{1,0:T(8,128)S(1)}, u32[]{:S(2)}, u32[]{:S(2)}) collective-permute-start(f32[544,128]{1,0:T(8,128)S(1)} %get-tuple-element.72), channel_id=1, source_target_pairs={{0,64},{32,96},{64,0},{96,32},{1,65},{33,97},{65,1},{97,33},{2,66}... | collective-permute-start | bytes 835592 | tf_op jit(solution)/shard_map/ppermute | solution.py:316
  43.0 1.2 %collective-permute-done.7 = f32[272,128]{1,0:T(8,128)S(1)} collective-permute-done((f32[272,128]{1,0:T(8,128)S(1)}, f32[272,128]{1,0:T(8,128)S(1)}, u32[]{:S(2)}, u32[]{:S(2)}) %collective-permute-start.7) | collective-permute-done | bytes 139296 | tf_op jit(solution)/shard_map/ppermute | solution.py:316
  44.1 1.9 %collective-permute-start.18 = (f32[32,128]{1,0:T(8,128)S(1)}, f32[32,128]{1,0:T(8,128)S(1)}, u32[]{:S(2)}, u32[]{:S(2)}) collective-permute-start(f32[32,128]{1,0:T(8,128)S(1)} %slice_add_fusion), channel_id=1, source_target_pairs={{8,12},{0,16},{16,18},{48,52},{80,88},{32,56},{24,28},{64,92},{96,... | collective-permute-start | bytes 49160 | tf_op jit(solution)/shard_map/ppermute | solution.py:341
  46.1 1.8 %collective-permute-start.17 = (f32[32,128]{1,0:T(8,128)S(1)}, f32[32,128]{1,0:T(8,128)S(1)}, u32[]{:S(2)}, u32[]{:S(2)}) collective-permute-start(f32[32,128]{1,0:T(8,128)S(1)} %slice_add_fusion), channel_id=1, source_target_pairs={{0,1},{32,34},{4,2},{2,3},{64,68},{8,4},{36,37},{68,70},{40,38},{6... | collective-permute-start | bytes 49160 | tf_op jit(solution)/shard_map/ppermute | solution.py:341
  47.9 0.6 collective-permute-start.9
  48.5 3.1 %collective-permute-done.11 = f32[544,128]{1,0:T(8,128)S(1)} collective-permute-done((f32[544,128]{1,0:T(8,128)S(1)}, f32[544,128]{1,0:T(8,128)S(1)}, u32[]{:S(2)}, u32[]{:S(2)}) %collective-permute-start.11) | collective-permute-done | bytes 278560 | tf_op jit(solution)/shard_map/ppermute | solution.py:316
  51.6 0.1 add_add_fusion.a_ref
  51.7 2.6 %collective-permute-start.16 = (f32[544,128]{1,0:T(8,128)S(1)}, f32[544,128]{1,0:T(8,128)S(1)}, u32[]{:S(2)}, u32[]{:S(2)}) collective-permute-start(f32[544,128]{1,0:T(8,128)S(1)} %add_add_fusion.a_ref), channel_id=1, source_target_pairs={{0,128},{128,0},{1,129},{129,1},{2,130},{130,2},{3,131},{131,3},{4... | collective-permute-start | bytes 835592 | tf_op jit(solution)/shard_map/ppermute | solution.py:339
  54.3 5.8 %collective-permute-done.9.d_ref = f32[272,128]{1,0:T(8,128)S(1)} collective-permute-done((f32[272,128]{1,0:T(8,128)S(1)}, f32[272,128]{1,0:T(8,128)S(1)}, u32[]{:S(2)}, u32[]{:S(2)}) %collective-permute-start.9) | collective-permute-done | bytes 139296 | tf_op jit(solution)/shard_map/ppermute | solution.py:339
  60.1 0.7 shard_map.79.refs_0_
  60.8 0.1 collective-permute-start.15
  60.9 0.1 collective-permute-start.14
  61.0 3.4 %collective-permute-start.13 = (f32[512,128]{1,0:T(8,128)S(1)}, f32[512,128]{1,0:T(8,128)S(1)}, u32[]{:S(2)}, u32[]{:S(2)}) collective-permute-start(f32[512,128]{1,0:T(8,128)S(1)} %shard_map.79.refs_0_), channel_id=1, source_target_pairs={{0,32},{32,0},{64,96},{96,64},{1,33},{33,1},{65,97},{97,65},{2,34}... | collective-permute-start | bytes 786440 | tf_op jit(solution)/shard_map/ppermute | solution.py:316
  64.4 0.5 fusion
  65.0 1.8 %add_add_fusion.3.fix_ref = f32[32,128]{1,0:T(8,128)S(1)} fusion(f32[32,128]{1,0:T(8,128)S(1)} %collective-permute-done.18, f32[32,128]{1,0:T(8,128)S(1)} %collective-permute-done.17, f32[32,128]{1,0:T(8,128)S(1)} %slice_add_fusion, f32[]{:T(128)} %bitcast.5, f32[]{:T(128)} %bitcast.4, f32[]{:T(128)} %bitcast.3), kind=kLoop, calls=%fused_computation.4 | loop fusion | flops 20480 | bytes 65548 | tf_op jit(solution)/shard_map/add | solution.py:353
  66.8 4.5 %collective-permute-done.15.refs_3_ = f32[512,128]{1,0:T(8,128)S(1)} collective-permute-done((f32[512,128]{1,0:T(8,128)S(1)}, f32[512,128]{1,0:T(8,128)S(1)}, u32[]{:S(2)}, u32[]{:S(2)}) %collective-permute-start.15) | collective-permute-done | bytes 262176 | tf_op jit(solution)/shard_map/ppermute | solution.py:316
  71.3 5.6 %collective-permute-done.14.refs_2_ = f32[512,128]{1,0:T(8,128)S(1)} collective-permute-done((f32[512,128]{1,0:T(8,128)S(1)}, f32[512,128]{1,0:T(8,128)S(1)}, u32[]{:S(2)}, u32[]{:S(2)}) %collective-permute-start.14) | collective-permute-done | bytes 262176 | tf_op jit(solution)/shard_map/ppermute | solution.py:316
  76.9 0.6 shard_map.80.refs_4_
  77.5 0.6 collective-permute-start.21
  78.1 0.3 collective-permute-start.20
  78.4 2.7 %collective-permute-start.19 = (f32[544,128]{1,0:T(8,128)S(1)}, f32[544,128]{1,0:T(8,128)S(1)}, u32[]{:S(2)}, u32[]{:S(2)}) collective-permute-start(f32[544,128]{1,0:T(8,128)S(1)} %shard_map.80.refs_4_), channel_id=1, source_target_pairs={{0,32},{32,0},{64,96},{96,64},{1,33},{33,1},{65,97},{97,65},{2,34}... | collective-permute-start | bytes 835592 | tf_op jit(solution)/shard_map/ppermute | solution.py:316
  81.1 4.7 %collective-permute-done.21.refs_7_ = f32[544,128]{1,0:T(8,128)S(1)} collective-permute-done((f32[544,128]{1,0:T(8,128)S(1)}, f32[544,128]{1,0:T(8,128)S(1)}, u32[]{:S(2)}, u32[]{:S(2)}) %collective-permute-start.21) | collective-permute-done | bytes 278560 | tf_op jit(solution)/shard_map/ppermute | solution.py:316
  85.8 2.9 %collective-permute-done.20.refs_6_ = f32[544,128]{1,0:T(8,128)S(1)} collective-permute-done((f32[544,128]{1,0:T(8,128)S(1)}, f32[544,128]{1,0:T(8,128)S(1)}, u32[]{:S(2)}, u32[]{:S(2)}) %collective-permute-start.20) | collective-permute-done | bytes 278560 | tf_op jit(solution)/shard_map/ppermute | solution.py:316
  88.7 2.2 %shard_map.81 = f32[16,16,16,128]{3,2,1,0:T(8,128)} custom-call(s32[2]{0:T(128)S(1)} %pad_add_fusion.pos, f32[512,128]{1,0:T(8,128)S(1)} %shard_map.79.refs_0_, f32[512,128]{1,0:T(8,128)S(1)} %collective-permute-done.13.refs_1_, f32[512,128]{1,0:T(8,128)S(1)} %collective-permute-done.14.refs_2_, f32[512,128]{1,0:T(8,128)S(1)} %collective-permute-done.15.refs_3_, ...), custom_call_target="tpu_custom_call" | custom-call | tf_op jit(solution)/shard_map/pallas_call | solution.py:358
  (27 shorter events, 0.1 us)
Async XLA Ops:
  0.0 7.6 %copy-start.5 = (f32[4]{0:T(128)S(1)}, f32[4]{0:T(128)}, u32[]{:S(2)}) copy-start(f32[4]{0:T(128)} %dif.9) | copy-start | bytes 52
  0.0 7.6 %copy-start.4 = (f32[4]{0:T(128)S(1)}, f32[4]{0:T(128)}, u32[]{:S(2)}) copy-start(f32[4]{0:T(128)} %vel.9) | copy-start | bytes 52
  0.0 7.6 %copy-start.3 = (s32[1,4]{1,0:T(1,128)S(1)}, s32[1,4]{1,0:T(1,128)}, u32[]{:S(2)}) copy-start(s32[1,4]{1,0:T(1,128)} %lev.9) | copy-start | bytes 52
  0.0 1.6 %copy-start = (f32[1,16,16,16,128]{4,3,2,1,0:T(8,128)S(1)}, f32[1,16,16,16,128]{4,3,2,1,0:T(8,128)}, u32[]{:S(2)}) copy-start(f32[1,16,16,16,128]{4,3,2,1,0:T(8,128)} %param.7) | copy-start | bytes 6291460
  2.4 9.1 %collective-permute-start = (f32[2,16,256]{2,1,0:T(8,128)S(1)}, f32[2,16,256]{2,1,0:T(8,128)S(1)}, u32[]{:S(2)}, u32[]{:S(2)}) collective-permute-start(f32[2,16,256]{2,1,0:T(8,128)S(1)} %get-tuple-element.41.hi_ref), channel_id=1, source_target_pairs={{0,1},{1,2},{2,3},{3,4},{4,5},{5,6},{6,7},{7,8},{8,9},{9,10},{10,1... | collective-permute-start | bytes 98312 | tf_op jit(solution)/shard_map/ppermute | solution.py:284
  2.5 9.1 %collective-permute-start.1 = (f32[3,16,256]{2,1,0:T(8,128)S(1)}, f32[3,16,256]{2,1,0:T(8,128)S(1)}, u32[]{:S(2)}, u32[]{:S(2)}) collective-permute-start(f32[3,16,256]{2,1,0:T(8,128)S(1)} %get-tuple-element.40.lo_ref), channel_id=1, source_target_pairs={{0,31},{1,0},{2,1},{3,2},{4,3},{5,4},{6,5},{7,6},{8,7},{9,8},{10,9... | collective-permute-start | bytes 147464 | tf_op jit(solution)/shard_map/ppermute | solution.py:285
  7.7 1.6 %copy-start.1 = (f32[1,16,16,16,128]{4,3,2,1,0:T(8,128)S(1)}, f32[1,16,16,16,128]{4,3,2,1,0:T(8,128)}, u32[]{:S(2)}) copy-start(f32[1,16,16,16,128]{4,3,2,1,0:T(8,128)} %param.7) | copy-start | bytes 6291460
  12.6 21.7 %copy-start.6 = (f32[3,128]{1,0:T(4,128)S(1)}, f32[3,128]{1,0:T(4,128)}, u32[]{:S(2)}) copy-start(f32[3,128]{1,0:T(4,128)} %constant.30.clone) | copy-start | bytes 4612
  13.6 6.7 %collective-permute-start.2 = (f32[304,128]{1,0:T(8,128)S(1)}, f32[304,128]{1,0:T(8,128)S(1)}, u32[]{:S(2)}, u32[]{:S(2)}) collective-permute-start(f32[304,128]{1,0:T(8,128)S(1)} %get-tuple-element.51), channel_id=1, source_target_pairs={{0,32},{32,0},{64,96},{96,64},{1,33},{33,1},{65,97},{97,65},{2,34}... | collective-permute-start | bytes 466952 | tf_op jit(solution)/shard_map/ppermute | solution.py:316
  15.2 6.9 %collective-permute-start.3 = (f32[304,128]{1,0:T(8,128)S(1)}, f32[304,128]{1,0:T(8,128)S(1)}, u32[]{:S(2)}, u32[]{:S(2)}) collective-permute-start(f32[304,128]{1,0:T(8,128)S(1)} %get-tuple-element.52), channel_id=1, source_target_pairs={{0,96},{32,64},{64,32},{96,0},{1,97},{33,65},{65,33},{97,1},{2,98}... | collective-permute-start | bytes 466952 | tf_op jit(solution)/shard_map/ppermute | solution.py:316
  17.4 6.7 %collective-permute-start.4 = (f32[304,128]{1,0:T(8,128)S(1)}, f32[304,128]{1,0:T(8,128)S(1)}, u32[]{:S(2)}, u32[]{:S(2)}) collective-permute-start(f32[304,128]{1,0:T(8,128)S(1)} %get-tuple-element.53), channel_id=1, source_target_pairs={{0,64},{32,96},{64,0},{96,32},{1,65},{33,97},{65,1},{97,33},{2,66}... | collective-permute-start | bytes 466952 | tf_op jit(solution)/shard_map/ppermute | solution.py:316
  24.2 16.3 %collective-permute-start.5 = (f32[304,128]{1,0:T(8,128)S(1)}, f32[304,128]{1,0:T(8,128)S(1)}, u32[]{:S(2)}, u32[]{:S(2)}) collective-permute-start(f32[304,128]{1,0:T(8,128)S(1)} %add_add_fusion.1.a_ref), channel_id=1, source_target_pairs={{0,128},{128,0},{1,129},{129,1},{2,130},{130,2},{3,131},{131,3},{4... | collective-permute-start | bytes 466952 | tf_op jit(solution)/shard_map/ppermute | solution.py:339
  32.5 7.5 %collective-permute-start.6 = (f32[272,128]{1,0:T(8,128)S(1)}, f32[272,128]{1,0:T(8,128)S(1)}, u32[]{:S(2)}, u32[]{:S(2)}) collective-permute-start(f32[272,128]{1,0:T(8,128)S(1)} %get-tuple-element.59), channel_id=1, source_target_pairs={{0,32},{32,0},{64,96},{96,64},{1,33},{33,1},{65,97},{97,65},{2,34}... | collective-permute-start | bytes 417800 | tf_op jit(solution)/shard_map/ppermute | solution.py:316
  34.3 25.8 %copy-start.2 = (f32[128,128]{1,0:T(8,128)S(1)}, f32[128,128]{1,0:T(8,128)}, u32[]{:S(2)}) copy-start(f32[128,128]{1,0:T(8,128)} %constant.29.clone.mat_ref) | copy-start | bytes 196612
  34.3 9.8 %collective-permute-start.7 = (f32[272,128]{1,0:T(8,128)S(1)}, f32[272,128]{1,0:T(8,128)S(1)}, u32[]{:S(2)}, u32[]{:S(2)}) collective-permute-start(f32[272,128]{1,0:T(8,128)S(1)} %get-tuple-element.60), channel_id=1, source_target_pairs={{0,96},{32,64},{64,32},{96,0},{1,97},{33,65},{65,33},{97,1},{2,98}... | collective-permute-start | bytes 417800 | tf_op jit(solution)/shard_map/ppermute | solution.py:316
  34.4 11.7 %collective-permute-start.8 = (f32[272,128]{1,0:T(8,128)S(1)}, f32[272,128]{1,0:T(8,128)S(1)}, u32[]{:S(2)}, u32[]{:S(2)}) collective-permute-start(f32[272,128]{1,0:T(8,128)S(1)} %get-tuple-element.61), channel_id=1, source_target_pairs={{0,64},{32,96},{64,0},{96,32},{1,65},{33,97},{65,1},{97,33},{2,66}... | collective-permute-start | bytes 417800 | tf_op jit(solution)/shard_map/ppermute | solution.py:316
  38.1 9.8 %collective-permute-start.10 = (f32[544,128]{1,0:T(8,128)S(1)}, f32[544,128]{1,0:T(8,128)S(1)}, u32[]{:S(2)}, u32[]{:S(2)}) collective-permute-start(f32[544,128]{1,0:T(8,128)S(1)} %get-tuple-element.70), channel_id=1, source_target_pairs={{0,32},{32,0},{64,96},{96,64},{1,33},{33,1},{65,97},{97,65},{2,34}... | collective-permute-start | bytes 835592 | tf_op jit(solution)/shard_map/ppermute | solution.py:316
  39.9 11.7 %collective-permute-start.11 = (f32[544,128]{1,0:T(8,128)S(1)}, f32[544,128]{1,0:T(8,128)S(1)}, u32[]{:S(2)}, u32[]{:S(2)}) collective-permute-start(f32[544,128]{1,0:T(8,128)S(1)} %get-tuple-element.71), channel_id=1, source_target_pairs={{0,96},{32,64},{64,32},{96,0},{1,97},{33,65},{65,33},{97,1},{2,98}... | collective-permute-start | bytes 835592 | tf_op jit(solution)/shard_map/ppermute | solution.py:316
  40.5 11.1 %collective-permute-start.12 = (f32[544,128]{1,0:T(8,128)S(1)}, f32[544,128]{1,0:T(8,128)S(1)}, u32[]{:S(2)}, u32[]{:S(2)}) collective-permute-start(f32[544,128]{1,0:T(8,128)S(1)} %get-tuple-element.72), channel_id=1, source_target_pairs={{0,64},{32,96},{64,0},{96,32},{1,65},{33,97},{65,1},{97,33},{2,66}... | collective-permute-start | bytes 835592 | tf_op jit(solution)/shard_map/ppermute | solution.py:316
  44.1 16.9 %collective-permute-start.18 = (f32[32,128]{1,0:T(8,128)S(1)}, f32[32,128]{1,0:T(8,128)S(1)}, u32[]{:S(2)}, u32[]{:S(2)}) collective-permute-start(f32[32,128]{1,0:T(8,128)S(1)} %slice_add_fusion), channel_id=1, source_target_pairs={{8,12},{0,16},{16,18},{48,52},{80,88},{32,56},{24,28},{64,92},{96,... | collective-permute-start | bytes 49160 | tf_op jit(solution)/shard_map/ppermute | solution.py:341
  46.1 18.9 %collective-permute-start.17 = (f32[32,128]{1,0:T(8,128)S(1)}, f32[32,128]{1,0:T(8,128)S(1)}, u32[]{:S(2)}, u32[]{:S(2)}) collective-permute-start(f32[32,128]{1,0:T(8,128)S(1)} %slice_add_fusion), channel_id=1, source_target_pairs={{0,1},{32,34},{4,2},{2,3},{64,68},{8,4},{36,37},{68,70},{40,38},{6... | collective-permute-start | bytes 49160 | tf_op jit(solution)/shard_map/ppermute | solution.py:341
  47.9 12.2 %collective-permute-start.9 = (f32[272,128]{1,0:T(8,128)S(1)}, f32[272,128]{1,0:T(8,128)S(1)}, u32[]{:S(2)}, u32[]{:S(2)}) collective-permute-start(f32[272,128]{1,0:T(8,128)S(1)} %add_add_fusion.2.c_ref), channel_id=1, source_target_pairs={{0,128},{128,0},{1,129},{129,1},{2,130},{130,2},{3,131},{131,3},{4... | collective-permute-start | bytes 417800 | tf_op jit(solution)/shard_map/ppermute | solution.py:339
  51.7 25.2 %collective-permute-start.16 = (f32[544,128]{1,0:T(8,128)S(1)}, f32[544,128]{1,0:T(8,128)S(1)}, u32[]{:S(2)}, u32[]{:S(2)}) collective-permute-start(f32[544,128]{1,0:T(8,128)S(1)} %add_add_fusion.a_ref), channel_id=1, source_target_pairs={{0,128},{128,0},{1,129},{129,1},{2,130},{130,2},{3,131},{131,3},{4... | collective-permute-start | bytes 835592 | tf_op jit(solution)/shard_map/ppermute | solution.py:339
  60.8 10.5 %collective-permute-start.15 = (f32[512,128]{1,0:T(8,128)S(1)}, f32[512,128]{1,0:T(8,128)S(1)}, u32[]{:S(2)}, u32[]{:S(2)}) collective-permute-start(f32[512,128]{1,0:T(8,128)S(1)} %shard_map.79.refs_0_), channel_id=1, source_target_pairs={{0,64},{32,96},{64,0},{96,32},{1,65},{33,97},{65,1},{97,33},{2,66}... | collective-permute-start | bytes 786440 | tf_op jit(solution)/shard_map/ppermute | solution.py:316
  60.9 16.0 %collective-permute-start.14 = (f32[512,128]{1,0:T(8,128)S(1)}, f32[512,128]{1,0:T(8,128)S(1)}, u32[]{:S(2)}, u32[]{:S(2)}) collective-permute-start(f32[512,128]{1,0:T(8,128)S(1)} %shard_map.79.refs_0_), channel_id=1, source_target_pairs={{0,96},{32,64},{64,32},{96,0},{1,97},{33,65},{65,33},{97,1},{2,98}... | collective-permute-start | bytes 786440 | tf_op jit(solution)/shard_map/ppermute | solution.py:316
  61.0 15.9 %collective-permute-start.13 = (f32[512,128]{1,0:T(8,128)S(1)}, f32[512,128]{1,0:T(8,128)S(1)}, u32[]{:S(2)}, u32[]{:S(2)}) collective-permute-start(f32[512,128]{1,0:T(8,128)S(1)} %shard_map.79.refs_0_), channel_id=1, source_target_pairs={{0,32},{32,0},{64,96},{96,64},{1,33},{33,1},{65,97},{97,65},{2,34}... | collective-permute-start | bytes 786440 | tf_op jit(solution)/shard_map/ppermute | solution.py:316
  77.5 8.2 %collective-permute-start.21 = (f32[544,128]{1,0:T(8,128)S(1)}, f32[544,128]{1,0:T(8,128)S(1)}, u32[]{:S(2)}, u32[]{:S(2)}) collective-permute-start(f32[544,128]{1,0:T(8,128)S(1)} %shard_map.80.refs_4_), channel_id=1, source_target_pairs={{0,64},{32,96},{64,0},{96,32},{1,65},{33,97},{65,1},{97,33},{2,66}... | collective-permute-start | bytes 835592 | tf_op jit(solution)/shard_map/ppermute | solution.py:316
  78.1 10.6 %collective-permute-start.20 = (f32[544,128]{1,0:T(8,128)S(1)}, f32[544,128]{1,0:T(8,128)S(1)}, u32[]{:S(2)}, u32[]{:S(2)}) collective-permute-start(f32[544,128]{1,0:T(8,128)S(1)} %shard_map.80.refs_4_), channel_id=1, source_target_pairs={{0,96},{32,64},{64,32},{96,0},{1,97},{33,65},{65,33},{97,1},{2,98}... | collective-permute-start | bytes 835592 | tf_op jit(solution)/shard_map/ppermute | solution.py:316
  78.4 10.2 %collective-permute-start.19 = (f32[544,128]{1,0:T(8,128)S(1)}, f32[544,128]{1,0:T(8,128)S(1)}, u32[]{:S(2)}, u32[]{:S(2)}) collective-permute-start(f32[544,128]{1,0:T(8,128)S(1)} %shard_map.80.refs_4_), channel_id=1, source_target_pairs={{0,32},{32,0},{64,96},{96,64},{1,33},{33,1},{65,97},{97,65},{2,34}... | collective-permute-start | bytes 835592 | tf_op jit(solution)/shard_map/ppermute | solution.py:316
